TPU v7x, 32 devices: a whole 2x2x4 slice. The times are simulated.
32 devices in a mesh: pts: 8 (over y, x, core), mem: 4 (over z).
Axes of the slice: x: 2, y: 2, z: 4, core: 2. Of those that a mesh axis runs over, the one named last changes fastest.
Arguments:
- ensemble: bfloat16 [64, 128, 4096], P('mem', None, 'pts'), may hold values from -4 to 4
- increment: float32 [128, 4096], P(None, 'pts'), may hold values from -8 to 8
- obs_weight: float32 [128, 4096], P(None, 'pts'), may hold values from 0.3 to 3
- vertical: bfloat16 [128, 128], replicated, may hold values from -0.5 to 0.5
- block_table: bfloat16 [12, 128, 128], replicated, may hold values from -0.15625 to 0.15625
- block_cols: int32 [32, 12], replicated, may hold values from 0 to 31, as said below
Outputs:
- weighted: float32 [128, 4096], P(None, 'pts')
- applied: float32 [128, 4096], P(None, 'pts')
Inputs may be any that keep to these rules, and one draw needn't show every extreme that they name: `block_cols`: row r begins with r itself, and its 12 entries are different block indices.
All inputs are finite; a program needn't handle non-finite values.
Results may differ from a plain program's by a relative error of at most 0.012.
Values may be sent and summed in bfloat16 or wider, within the bound.
No kernel may reach another device: no remote copies, remote signals or barrier semaphores. Data moves between devices by JAX's collectives and lax.ppermute only.
A program may use at most 128 MiB of HBM per device.

v0:
```python
import jax
import jax.numpy as jnp
from jax import lax
from jax.sharding import PartitionSpec as P


def localize(values, block_table, block_cols):
    leading = values.shape[:-1]
    npoints = values.shape[-1]
    blk_width = block_table.shape[-1]
    flattened = values.reshape(-1, npoints // blk_width, blk_width)

    def add_slot(column, running):
        chosen = lax.dynamic_index_in_dim(block_cols, column, 1, keepdims=False)
        picked = jnp.take(flattened, chosen, axis=1)
        kernel = lax.dynamic_index_in_dim(block_table, column, 0, keepdims=False)
        return running + jnp.einsum(
            "rnk,lk->rnl", picked, kernel, preferred_element_type=jnp.float32
        )

    running = lax.fori_loop(
        0, block_table.shape[0], add_slot, jnp.zeros(flattened.shape, jnp.float32)
    )
    return running.reshape(leading + (npoints,)).astype(jnp.bfloat16)


def per_device(ensemble, increment, obs_weight, vertical, block_table, block_cols):
    spread_levels = lax.all_to_all(ensemble, "pts", split_axis=1, concat_axis=2, tiled=True)

    def horiz_items(moved):
        return localize(moved, block_table, block_cols)

    def cov_local(field_now):
        product = (ensemble.astype(jnp.float32) * field_now).astype(jnp.bfloat16)
        vert_mixed = jnp.einsum(
            "lk,mkp->mlp", vertical, product, preferred_element_type=jnp.float32
        ).astype(jnp.bfloat16)
        level_local = horiz_items(
            lax.all_to_all(vert_mixed, "pts", split_axis=1, concat_axis=2, tiled=True)
        )
        level_sums = jnp.sum(
            spread_levels.astype(jnp.float32) * level_local.astype(jnp.float32), axis=0
        )
        return lax.all_to_all(level_sums, "pts", split_axis=1, concat_axis=0, tiled=True)

    def member_total(member_terms, use_weights):
        summed = lax.psum(member_terms, "mem")
        if use_weights:
            summed = summed * obs_weight
        return summed

    weighted = member_total(cov_local(increment), True)
    applied = member_total(cov_local(weighted), False)
    return (weighted, applied)


def solution(mesh):
    return jax.shard_map(
        per_device,
        mesh=mesh,
        in_specs=(P("mem", None, "pts"), P(None, "pts"), P(None, "pts"), P(), P(), P()),
        out_specs=(P(None, "pts"), P(None, "pts")),
        check_vma=False,
    )
```

profile of v0, /device:TPU:0, one launch (start us, length us, event | category | flops | bytes accessed | tf_op | source)
XLA Modules:
  0.0 431.7 jit_solution(762440760316623220)
XLA Ops:
  10.3 3.0 copy.35
  13.3 5.3 %all-to-all-start.1 = ((bf16[16,128,512]{2,0,1:T(8,128)(2,1)}), bf16[16,128,512]{2,0,1:T(8,128)(2,1)}, u32[]{:S(2)}, u32[]{:S(2)}) async-start(bf16[16,128,512]{2,0,1:T(8,128)(2,1)} %copy.35), calls=%async_computation.1 | async-start | bytes 4194304 | tf_op jit(solution)/shard_map/all_to_all | solution.py:39
  21.1 24.2 %all-to-all-done.1 = bf16[16,128,512]{2,0,1:T(8,128)(2,1)} async-done(((bf16[16,128,512]{2,0,1:T(8,128)(2,1)}), bf16[16,128,512]{2,0,1:T(8,128)(2,1)}, u32[]{:S(2)}, u32[]{:S(2)}) %all-to-all-start.1) | async-done | bytes 2097184 | tf_op jit(solution)/shard_map/all_to_all | solution.py:39
  45.3 4.4 %all-to-all-start = ((bf16[16,128,512]{2,0,1:T(8,128)(2,1)}), bf16[16,128,512]{2,0,1:T(8,128)(2,1)}, u32[]{:S(2)}, u32[]{:S(2)}) async-start(bf16[16,128,512]{2,0,1:T(8,128)(2,1)} %copy.32), calls=%async_computation | async-start | bytes 4194304 | tf_op jit(solution)/shard_map/all_to_all | solution.py:28
  49.8 2.8 copy.37
  52.5 2.8 reshape.41
  55.3 3.7 copy.38
  59.0 96.6 %while.28 = (s32[]{:T(128)}, f32[256,32,128]{2,0,1:T(8,128)}, s32[32,12]{0,1:T(8,128)}, bf16[256,32,128]{2,0,1:T(8,128)(2,1)}, bf16[12,128,128]{2,1,0:T(8,128)(2,1)}, /*index=5*/s32[]{:T(128)}, s32[]{:T(128)}) while((s32[]{:T(128)}, f32[256,32,128]{2,0,1:T(8,128)}, s32[32,12]{0,1:T(8,128)}, bf16[256,32,128]{2,0,1:T(8,128)(2,1)}, ...), condition=%wide.region_1.0_spmd.clone, body=%wide.region_0.2_spmd.clone.sunk | while | flops 271582400 | bytes 14718107 | solution.py:21
  59.7 2.5 gather_fusion
  62.3 3.5 select_add_fusion.4
  66.4 2.5 gather_fusion
  69.0 4.9 %select_add_fusion.4 = f32[256,32,128]{2,0,1:T(8,128)} fusion(f32[256,32,128]{2,0,1:T(8,128)} %get-tuple-element.351, bf16[32,256,128]{2,1,0:T(8,128)(2,1)S(1)} %gather_fusion, pred[32]{0:T(512)(128)(4,1)S(1)} %get-tuple-element.335, pred[]{:T(512)S(6)} %compare.6, bf16[12,128,128]{2,1,0:T(8,128)(2,1)} %get-tuple-element.361, s32[]{:T(128)} %get-tuple-element.350), kind=kOutput, calls=%fused_computation.2.clone.1 | convolution fusion | flops 271581184 | bytes 10519073 | tf_op jit(solution)/shard_map/while/body/eval_jaxpr/rnk,lk->rnl/dot_general | solution.py:17
  74.6 2.5 gather_fusion
  77.2 4.9 %select_add_fusion.4 = f32[256,32,128]{2,0,1:T(8,128)} fusion(f32[256,32,128]{2,0,1:T(8,128)} %get-tuple-element.351, bf16[32,256,128]{2,1,0:T(8,128)(2,1)S(1)} %gather_fusion, pred[32]{0:T(512)(128)(4,1)S(1)} %get-tuple-element.335, pred[]{:T(512)S(6)} %compare.6, bf16[12,128,128]{2,1,0:T(8,128)(2,1)} %get-tuple-element.361, s32[]{:T(128)} %get-tuple-element.350), kind=kOutput, calls=%fused_computation.2.clone.1 | convolution fusion | flops 271581184 | bytes 10519073 | tf_op jit(solution)/shard_map/while/body/eval_jaxpr/rnk,lk->rnl/dot_general | solution.py:17
  82.8 2.5 gather_fusion
  85.3 4.9 %select_add_fusion.4 = f32[256,32,128]{2,0,1:T(8,128)} fusion(f32[256,32,128]{2,0,1:T(8,128)} %get-tuple-element.351, bf16[32,256,128]{2,1,0:T(8,128)(2,1)S(1)} %gather_fusion, pred[32]{0:T(512)(128)(4,1)S(1)} %get-tuple-element.335, pred[]{:T(512)S(6)} %compare.6, bf16[12,128,128]{2,1,0:T(8,128)(2,1)} %get-tuple-element.361, s32[]{:T(128)} %get-tuple-element.350), kind=kOutput, calls=%fused_computation.2.clone.1 | convolution fusion | flops 271581184 | bytes 10519073 | tf_op jit(solution)/shard_map/while/body/eval_jaxpr/rnk,lk->rnl/dot_general | solution.py:17
  91.0 2.5 gather_fusion
  93.5 4.9 %select_add_fusion.4 = f32[256,32,128]{2,0,1:T(8,128)} fusion(f32[256,32,128]{2,0,1:T(8,128)} %get-tuple-element.351, bf16[32,256,128]{2,1,0:T(8,128)(2,1)S(1)} %gather_fusion, pred[32]{0:T(512)(128)(4,1)S(1)} %get-tuple-element.335, pred[]{:T(512)S(6)} %compare.6, bf16[12,128,128]{2,1,0:T(8,128)(2,1)} %get-tuple-element.361, s32[]{:T(128)} %get-tuple-element.350), kind=kOutput, calls=%fused_computation.2.clone.1 | convolution fusion | flops 271581184 | bytes 10519073 | tf_op jit(solution)/shard_map/while/body/eval_jaxpr/rnk,lk->rnl/dot_general | solution.py:17
  99.1 2.5 gather_fusion
  101.7 4.9 %select_add_fusion.4 = f32[256,32,128]{2,0,1:T(8,128)} fusion(f32[256,32,128]{2,0,1:T(8,128)} %get-tuple-element.351, bf16[32,256,128]{2,1,0:T(8,128)(2,1)S(1)} %gather_fusion, pred[32]{0:T(512)(128)(4,1)S(1)} %get-tuple-element.335, pred[]{:T(512)S(6)} %compare.6, bf16[12,128,128]{2,1,0:T(8,128)(2,1)} %get-tuple-element.361, s32[]{:T(128)} %get-tuple-element.350), kind=kOutput, calls=%fused_computation.2.clone.1 | convolution fusion | flops 271581184 | bytes 10519073 | tf_op jit(solution)/shard_map/while/body/eval_jaxpr/rnk,lk->rnl/dot_general | solution.py:17
  107.3 2.5 gather_fusion
  109.9 4.9 %select_add_fusion.4 = f32[256,32,128]{2,0,1:T(8,128)} fusion(f32[256,32,128]{2,0,1:T(8,128)} %get-tuple-element.351, bf16[32,256,128]{2,1,0:T(8,128)(2,1)S(1)} %gather_fusion, pred[32]{0:T(512)(128)(4,1)S(1)} %get-tuple-element.335, pred[]{:T(512)S(6)} %compare.6, bf16[12,128,128]{2,1,0:T(8,128)(2,1)} %get-tuple-element.361, s32[]{:T(128)} %get-tuple-element.350), kind=kOutput, calls=%fused_computation.2.clone.1 | convolution fusion | flops 271581184 | bytes 10519073 | tf_op jit(solution)/shard_map/while/body/eval_jaxpr/rnk,lk->rnl/dot_general | solution.py:17
  115.5 2.5 gather_fusion
  118.0 4.9 %select_add_fusion.4 = f32[256,32,128]{2,0,1:T(8,128)} fusion(f32[256,32,128]{2,0,1:T(8,128)} %get-tuple-element.351, bf16[32,256,128]{2,1,0:T(8,128)(2,1)S(1)} %gather_fusion, pred[32]{0:T(512)(128)(4,1)S(1)} %get-tuple-element.335, pred[]{:T(512)S(6)} %compare.6, bf16[12,128,128]{2,1,0:T(8,128)(2,1)} %get-tuple-element.361, s32[]{:T(128)} %get-tuple-element.350), kind=kOutput, calls=%fused_computation.2.clone.1 | convolution fusion | flops 271581184 | bytes 10519073 | tf_op jit(solution)/shard_map/while/body/eval_jaxpr/rnk,lk->rnl/dot_general | solution.py:17
  123.6 2.5 gather_fusion
  126.2 4.9 %select_add_fusion.4 = f32[256,32,128]{2,0,1:T(8,128)} fusion(f32[256,32,128]{2,0,1:T(8,128)} %get-tuple-element.351, bf16[32,256,128]{2,1,0:T(8,128)(2,1)S(1)} %gather_fusion, pred[32]{0:T(512)(128)(4,1)S(1)} %get-tuple-element.335, pred[]{:T(512)S(6)} %compare.6, bf16[12,128,128]{2,1,0:T(8,128)(2,1)} %get-tuple-element.361, s32[]{:T(128)} %get-tuple-element.350), kind=kOutput, calls=%fused_computation.2.clone.1 | convolution fusion | flops 271581184 | bytes 10519073 | tf_op jit(solution)/shard_map/while/body/eval_jaxpr/rnk,lk->rnl/dot_general | solution.py:17
  131.8 2.5 gather_fusion
  134.4 4.9 %select_add_fusion.4 = f32[256,32,128]{2,0,1:T(8,128)} fusion(f32[256,32,128]{2,0,1:T(8,128)} %get-tuple-element.351, bf16[32,256,128]{2,1,0:T(8,128)(2,1)S(1)} %gather_fusion, pred[32]{0:T(512)(128)(4,1)S(1)} %get-tuple-element.335, pred[]{:T(512)S(6)} %compare.6, bf16[12,128,128]{2,1,0:T(8,128)(2,1)} %get-tuple-element.361, s32[]{:T(128)} %get-tuple-element.350), kind=kOutput, calls=%fused_computation.2.clone.1 | convolution fusion | flops 271581184 | bytes 10519073 | tf_op jit(solution)/shard_map/while/body/eval_jaxpr/rnk,lk->rnl/dot_general | solution.py:17
  140.0 2.5 gather_fusion
  142.5 4.9 %select_add_fusion.4 = f32[256,32,128]{2,0,1:T(8,128)} fusion(f32[256,32,128]{2,0,1:T(8,128)} %get-tuple-element.351, bf16[32,256,128]{2,1,0:T(8,128)(2,1)S(1)} %gather_fusion, pred[32]{0:T(512)(128)(4,1)S(1)} %get-tuple-element.335, pred[]{:T(512)S(6)} %compare.6, bf16[12,128,128]{2,1,0:T(8,128)(2,1)} %get-tuple-element.361, s32[]{:T(128)} %get-tuple-element.350), kind=kOutput, calls=%fused_computation.2.clone.1 | convolution fusion | flops 271581184 | bytes 10519073 | tf_op jit(solution)/shard_map/while/body/eval_jaxpr/rnk,lk->rnl/dot_general | solution.py:17
  150.7 4.9 %select_add_fusion.4 = f32[256,32,128]{2,0,1:T(8,128)} fusion(f32[256,32,128]{2,0,1:T(8,128)} %get-tuple-element.351, bf16[32,256,128]{2,1,0:T(8,128)(2,1)S(1)} %gather_fusion, pred[32]{0:T(512)(128)(4,1)S(1)} %get-tuple-element.335, pred[]{:T(512)S(6)} %compare.6, bf16[12,128,128]{2,1,0:T(8,128)(2,1)} %get-tuple-element.361, s32[]{:T(128)} %get-tuple-element.350), kind=kOutput, calls=%fused_computation.2.clone.1 | convolution fusion | flops 271581184 | bytes 10519073 | tf_op jit(solution)/shard_map/while/body/eval_jaxpr/rnk,lk->rnl/dot_general | solution.py:17
  158.1 4.4 %copy.39 = f32[256,32,128]{2,1,0:T(8,128)} copy(f32[256,32,128]{2,0,1:T(8,128)S(1)} %convert_convert_fusion.1) | data formatting | bytes 8388608 | tf_op jit(solution)/shard_map/convert_element_type | solution.py:42
  162.5 4.9 %reshape.43 = f32[16,16,8,512]{3,2,1,0:T(8,128)} reshape(f32[256,32,128]{2,1,0:T(8,128)} %copy.39) | data formatting | bytes 8388608 | tf_op jit(solution)/shard_map/convert_element_type | solution.py:42
  167.4 2.9 copy.33
  170.4 3.9 fusion.20
  174.3 10.9 %all_to_all.71 = f32[16,8,512]{2,0,1:T(8,128)} all-to-all(f32[16,8,512]{2,0,1:T(8,128)S(1)} %fusion.20), channel_id=1, replica_groups=mesh['pts'=8,'mem'=4] {'pts'}, dimensions={1} | all-to-all | bytes 524288 | tf_op jit(solution)/shard_map/all_to_all | solution.py:44
  185.2 35.4 %all-reduce.3.cloned.1.call-done = f32[128,512]{1,0:T(8,128)} async-done(((f32[128,512]{1,0:T(8,128)}), f32[128,512]{1,0:T(8,128)}) %all-reduce.3.cloned.1.call-update) | async-done | bytes 262160 | tf_op jit(solution)/shard_map/psum | solution.py:47
  223.7 4.7 %copy.42 = bf16[16,128,512]{2,0,1:T(8,128)(2,1)} copy(bf16[16,128,512]{1,2,0:T(8,128)(2,1)} %convert_bitcast_fusion.1) | data formatting | bytes 4194304 | tf_op jit(solution)/shard_map/convert_element_type | solution.py:37
  228.4 3.7 all-to-all-start.3
  232.1 26.6 %all-to-all-done.3 = bf16[16,128,512]{2,0,1:T(8,128)(2,1)S(1)} async-done(((bf16[16,128,512]{2,0,1:T(8,128)(2,1)}), bf16[16,128,512]{2,0,1:T(8,128)(2,1)S(1)}, u32[]{:S(2)}, u32[]{:S(2)}) %all-to-all-start.3) | async-done | bytes 2097184 | tf_op jit(solution)/shard_map/all_to_all | solution.py:39
  261.2 3.1 reshape.42
  266.4 96.6 %while.29 = (s32[]{:T(128)}, f32[256,32,128]{2,0,1:T(8,128)}, s32[32,12]{0,1:T(8,128)}, bf16[256,32,128]{2,0,1:T(8,128)(2,1)}, bf16[12,128,128]{2,1,0:T(8,128)(2,1)}, /*index=5*/s32[]{:T(128)}, s32[]{:T(128)}) while((s32[]{:T(128)}, f32[256,32,128]{2,0,1:T(8,128)}, s32[32,12]{0,1:T(8,128)}, bf16[256,32,128]{2,0,1:T(8,128)(2,1)}, ...), condition=%wide.region_5.7_spmd.clone, body=%wide.region_4.6_spmd.clone.sunk | while | flops 271582400 | bytes 14718107 | solution.py:21
  269.7 3.5 select_add_fusion.5
  273.9 2.5 gather_fusion.1
  276.4 4.9 %select_add_fusion.5 = f32[256,32,128]{2,0,1:T(8,128)} fusion(f32[256,32,128]{2,0,1:T(8,128)} %get-tuple-element.372, bf16[32,256,128]{2,1,0:T(8,128)(2,1)S(1)} %gather_fusion.1, pred[32]{0:T(512)(128)(4,1)S(1)} %get-tuple-element.342, pred[]{:T(512)S(6)} %compare.7, bf16[12,128,128]{2,1,0:T(8,128)(2,1)} %get-tuple-element.382, s32[]{:T(128)} %get-tuple-element.371), kind=kOutput, calls=%fused_computation.14.clone.1 | convolution fusion | flops 271581184 | bytes 10519073 | tf_op jit(solution)/shard_map/while/body/eval_jaxpr/rnk,lk->rnl/dot_general | solution.py:17
  282.0 2.5 gather_fusion.1
  284.6 4.9 %select_add_fusion.5 = f32[256,32,128]{2,0,1:T(8,128)} fusion(f32[256,32,128]{2,0,1:T(8,128)} %get-tuple-element.372, bf16[32,256,128]{2,1,0:T(8,128)(2,1)S(1)} %gather_fusion.1, pred[32]{0:T(512)(128)(4,1)S(1)} %get-tuple-element.342, pred[]{:T(512)S(6)} %compare.7, bf16[12,128,128]{2,1,0:T(8,128)(2,1)} %get-tuple-element.382, s32[]{:T(128)} %get-tuple-element.371), kind=kOutput, calls=%fused_computation.14.clone.1 | convolution fusion | flops 271581184 | bytes 10519073 | tf_op jit(solution)/shard_map/while/body/eval_jaxpr/rnk,lk->rnl/dot_general | solution.py:17
  290.2 2.5 gather_fusion.1
  292.7 4.9 %select_add_fusion.5 = f32[256,32,128]{2,0,1:T(8,128)} fusion(f32[256,32,128]{2,0,1:T(8,128)} %get-tuple-element.372, bf16[32,256,128]{2,1,0:T(8,128)(2,1)S(1)} %gather_fusion.1, pred[32]{0:T(512)(128)(4,1)S(1)} %get-tuple-element.342, pred[]{:T(512)S(6)} %compare.7, bf16[12,128,128]{2,1,0:T(8,128)(2,1)} %get-tuple-element.382, s32[]{:T(128)} %get-tuple-element.371), kind=kOutput, calls=%fused_computation.14.clone.1 | convolution fusion | flops 271581184 | bytes 10519073 | tf_op jit(solution)/shard_map/while/body/eval_jaxpr/rnk,lk->rnl/dot_general | solution.py:17
  298.4 2.5 gather_fusion.1
  300.9 4.9 %select_add_fusion.5 = f32[256,32,128]{2,0,1:T(8,128)} fusion(f32[256,32,128]{2,0,1:T(8,128)} %get-tuple-element.372, bf16[32,256,128]{2,1,0:T(8,128)(2,1)S(1)} %gather_fusion.1, pred[32]{0:T(512)(128)(4,1)S(1)} %get-tuple-element.342, pred[]{:T(512)S(6)} %compare.7, bf16[12,128,128]{2,1,0:T(8,128)(2,1)} %get-tuple-element.382, s32[]{:T(128)} %get-tuple-element.371), kind=kOutput, calls=%fused_computation.14.clone.1 | convolution fusion | flops 271581184 | bytes 10519073 | tf_op jit(solution)/shard_map/while/body/eval_jaxpr/rnk,lk->rnl/dot_general | solution.py:17
  306.5 2.5 gather_fusion.1
  309.1 4.9 %select_add_fusion.5 = f32[256,32,128]{2,0,1:T(8,128)} fusion(f32[256,32,128]{2,0,1:T(8,128)} %get-tuple-element.372, bf16[32,256,128]{2,1,0:T(8,128)(2,1)S(1)} %gather_fusion.1, pred[32]{0:T(512)(128)(4,1)S(1)} %get-tuple-element.342, pred[]{:T(512)S(6)} %compare.7, bf16[12,128,128]{2,1,0:T(8,128)(2,1)} %get-tuple-element.382, s32[]{:T(128)} %get-tuple-element.371), kind=kOutput, calls=%fused_computation.14.clone.1 | convolution fusion | flops 271581184 | bytes 10519073 | tf_op jit(solution)/shard_map/while/body/eval_jaxpr/rnk,lk->rnl/dot_general | solution.py:17
  317.3 4.9 %select_add_fusion.5 = f32[256,32,128]{2,0,1:T(8,128)} fusion(f32[256,32,128]{2,0,1:T(8,128)} %get-tuple-element.372, bf16[32,256,128]{2,1,0:T(8,128)(2,1)S(1)} %gather_fusion.1, pred[32]{0:T(512)(128)(4,1)S(1)} %get-tuple-element.342, pred[]{:T(512)S(6)} %compare.7, bf16[12,128,128]{2,1,0:T(8,128)(2,1)} %get-tuple-element.382, s32[]{:T(128)} %get-tuple-element.371), kind=kOutput, calls=%fused_computation.14.clone.1 | convolution fusion | flops 271581184 | bytes 10519073 | tf_op jit(solution)/shard_map/while/body/eval_jaxpr/rnk,lk->rnl/dot_general | solution.py:17
  325.4 4.9 %select_add_fusion.5 = f32[256,32,128]{2,0,1:T(8,128)} fusion(f32[256,32,128]{2,0,1:T(8,128)} %get-tuple-element.372, bf16[32,256,128]{2,1,0:T(8,128)(2,1)S(1)} %gather_fusion.1, pred[32]{0:T(512)(128)(4,1)S(1)} %get-tuple-element.342, pred[]{:T(512)S(6)} %compare.7, bf16[12,128,128]{2,1,0:T(8,128)(2,1)} %get-tuple-element.382, s32[]{:T(128)} %get-tuple-element.371), kind=kOutput, calls=%fused_computation.14.clone.1 | convolution fusion | flops 271581184 | bytes 10519073 | tf_op jit(solution)/shard_map/while/body/eval_jaxpr/rnk,lk->rnl/dot_general | solution.py:17
  333.6 4.9 %select_add_fusion.5 = f32[256,32,128]{2,0,1:T(8,128)} fusion(f32[256,32,128]{2,0,1:T(8,128)} %get-tuple-element.372, bf16[32,256,128]{2,1,0:T(8,128)(2,1)S(1)} %gather_fusion.1, pred[32]{0:T(512)(128)(4,1)S(1)} %get-tuple-element.342, pred[]{:T(512)S(6)} %compare.7, bf16[12,128,128]{2,1,0:T(8,128)(2,1)} %get-tuple-element.382, s32[]{:T(128)} %get-tuple-element.371), kind=kOutput, calls=%fused_computation.14.clone.1 | convolution fusion | flops 271581184 | bytes 10519073 | tf_op jit(solution)/shard_map/while/body/eval_jaxpr/rnk,lk->rnl/dot_general | solution.py:17
  341.8 4.9 %select_add_fusion.5 = f32[256,32,128]{2,0,1:T(8,128)} fusion(f32[256,32,128]{2,0,1:T(8,128)} %get-tuple-element.372, bf16[32,256,128]{2,1,0:T(8,128)(2,1)S(1)} %gather_fusion.1, pred[32]{0:T(512)(128)(4,1)S(1)} %get-tuple-element.342, pred[]{:T(512)S(6)} %compare.7, bf16[12,128,128]{2,1,0:T(8,128)(2,1)} %get-tuple-element.382, s32[]{:T(128)} %get-tuple-element.371), kind=kOutput, calls=%fused_computation.14.clone.1 | convolution fusion | flops 271581184 | bytes 10519073 | tf_op jit(solution)/shard_map/while/body/eval_jaxpr/rnk,lk->rnl/dot_general | solution.py:17
  349.9 4.9 %select_add_fusion.5 = f32[256,32,128]{2,0,1:T(8,128)} fusion(f32[256,32,128]{2,0,1:T(8,128)} %get-tuple-element.372, bf16[32,256,128]{2,1,0:T(8,128)(2,1)S(1)} %gather_fusion.1, pred[32]{0:T(512)(128)(4,1)S(1)} %get-tuple-element.342, pred[]{:T(512)S(6)} %compare.7, bf16[12,128,128]{2,1,0:T(8,128)(2,1)} %get-tuple-element.382, s32[]{:T(128)} %get-tuple-element.371), kind=kOutput, calls=%fused_computation.14.clone.1 | convolution fusion | flops 271581184 | bytes 10519073 | tf_op jit(solution)/shard_map/while/body/eval_jaxpr/rnk,lk->rnl/dot_general | solution.py:17
  358.1 4.9 %select_add_fusion.5 = f32[256,32,128]{2,0,1:T(8,128)} fusion(f32[256,32,128]{2,0,1:T(8,128)} %get-tuple-element.372, bf16[32,256,128]{2,1,0:T(8,128)(2,1)S(1)} %gather_fusion.1, pred[32]{0:T(512)(128)(4,1)S(1)} %get-tuple-element.342, pred[]{:T(512)S(6)} %compare.7, bf16[12,128,128]{2,1,0:T(8,128)(2,1)} %get-tuple-element.382, s32[]{:T(128)} %get-tuple-element.371), kind=kOutput, calls=%fused_computation.14.clone.1 | convolution fusion | flops 271581184 | bytes 10519073 | tf_op jit(solution)/shard_map/while/body/eval_jaxpr/rnk,lk->rnl/dot_general | solution.py:17
  365.5 4.4 %copy.46 = f32[256,32,128]{2,1,0:T(8,128)} copy(f32[256,32,128]{2,0,1:T(8,128)S(1)} %convert_convert_fusion) | data formatting | bytes 8388608 | tf_op jit(solution)/shard_map/convert_element_type | solution.py:42
  369.9 5.1 %reshape.44 = f32[16,16,8,512]{3,2,1,0:T(8,128)} reshape(f32[256,32,128]{2,1,0:T(8,128)} %copy.46) | data formatting | bytes 8388608 | tf_op jit(solution)/shard_map/convert_element_type | solution.py:42
  375.0 4.8 %fusion.21 = f32[16,8,512]{2,0,1:T(8,128)S(1)} fusion(bf16[16,8,16,512]{3,2,1,0:T(8,128)(2,1)S(1)} %bitcast.66, f32[16,16,8,512]{3,2,1,0:T(8,128)} %reshape.44), kind=kLoop, calls=%fused_computation.34 | loop fusion | flops 3080192 | bytes 6553600 | tf_op jit(solution)/shard_map/reduce_sum | solution.py:41
  379.8 10.0 %all_to_all.72 = f32[16,8,512]{2,0,1:T(8,128)} all-to-all(f32[16,8,512]{2,0,1:T(8,128)S(1)} %fusion.21), channel_id=1, replica_groups=mesh['pts'=8,'mem'=4] {'pts'}, dimensions={1} | all-to-all | bytes 524288 | tf_op jit(solution)/shard_map/all_to_all | solution.py:44
  389.8 33.4 %all-reduce.5.cloned.1.call-done = f32[128,512]{1,0:T(8,128)} async-done(((f32[128,512]{1,0:T(8,128)}), f32[128,512]{1,0:T(8,128)}) %all-reduce.5.cloned.1.call-update) | async-done | bytes 262160 | tf_op jit(solution)/shard_map/psum | solution.py:47
  (90 shorter events, 57.3 us)
Async XLA Ops:
  7.2 0.8 copy-start
  13.3 5.3 %copy-start.4 = (bf16[16,128,512]{2,1,0:T(8,128)(2,1)S(1)}, bf16[16,128,512]{2,1,0:T(8,128)(2,1)}, u32[]{:S(2)}) copy-start(bf16[16,128,512]{2,1,0:T(8,128)(2,1)} %param.12) | copy-start | bytes 6291460
  13.3 32.1 %all-to-all-start.1 = ((bf16[16,128,512]{2,0,1:T(8,128)(2,1)}), bf16[16,128,512]{2,0,1:T(8,128)(2,1)}, u32[]{:S(2)}, u32[]{:S(2)}) async-start(bf16[16,128,512]{2,0,1:T(8,128)(2,1)} %copy.35), calls=%async_computation.1 | async-start | bytes 4194304 | tf_op jit(solution)/shard_map/all_to_all | solution.py:39
  45.3 122.1 %all-to-all-start = ((bf16[16,128,512]{2,0,1:T(8,128)(2,1)}), bf16[16,128,512]{2,0,1:T(8,128)(2,1)}, u32[]{:S(2)}, u32[]{:S(2)}) async-start(bf16[16,128,512]{2,0,1:T(8,128)(2,1)} %copy.32), calls=%async_computation | async-start | bytes 4194304 | tf_op jit(solution)/shard_map/all_to_all | solution.py:28
  49.7 170.9 %all-reduce.3.cloned.1.call-start = ((), (), s32[]{:S(2)}) async-start(), calls=%async_computation.5 | async-start | bytes 524288 | tf_op jit(solution)/shard_map/psum | solution.py:47
  167.4 2.9 copy-start.6
  170.3 3.9 copy-start.2
  170.4 50.2 %copy-start.8 = (f32[128,512]{1,0:T(8,128)S(1)}, f32[128,512]{1,0:T(8,128)}, u32[]{:S(2)}) copy-start(f32[128,512]{1,0:T(8,128)} %param.14) | copy-start | bytes 786436
  170.4 51.2 %copy-start.5 = (bf16[16,128,512]{2,1,0:T(8,128)(2,1)S(1)}, bf16[16,128,512]{2,1,0:T(8,128)(2,1)}, u32[]{:S(2)}) copy-start(bf16[16,128,512]{2,1,0:T(8,128)(2,1)} %param.12) | copy-start | bytes 6291460
  221.6 2.1 copy-start.7
  228.4 30.3 %all-to-all-start.3 = ((bf16[16,128,512]{2,0,1:T(8,128)(2,1)}), bf16[16,128,512]{2,0,1:T(8,128)(2,1)S(1)}, u32[]{:S(2)}, u32[]{:S(2)}) async-start(bf16[16,128,512]{2,0,1:T(8,128)(2,1)} %copy.42), calls=%async_computation.3 | async-start | bytes 4194304 | tf_op jit(solution)/shard_map/all_to_all | solution.py:39
  232.0 191.1 %all-reduce.5.cloned.1.call-start = ((), (), s32[]{:S(2)}) async-start(), calls=%async_computation.6 | async-start | bytes 524288 | tf_op jit(solution)/shard_map/psum | solution.py:47
  369.9 5.1 %copy-start.3 = (bf16[16,128,512]{2,1,0:T(8,128)(2,1)S(1)}, bf16[16,128,512]{2,1,0:T(8,128)(2,1)}, u32[]{:S(2)}) copy-start(bf16[16,128,512]{2,1,0:T(8,128)(2,1)} %copy-done.2) | copy-start | bytes 6291460
  375.0 49.9 %copy-start.1 = (bf16[128,128]{1,0:T(8,128)(2,1)S(1)}, bf16[128,128]{1,0:T(8,128)(2,1)}, u32[]{:S(2)}) copy-start(bf16[128,128]{1,0:T(8,128)(2,1)} %param.15) | copy-start | bytes 98308
Sparse Core Ops, SparseCore 0:
  185.3 35.2 all-reduce.2
  389.9 33.2 all-reduce.4
where the time goes:
time: 435 us; the launch traced here: 432 us
  waiting for transfers between devices  120 us (28%)
  matrix products  119 us (27%)
  local copies, waits for them, and re-layouts  112 us (26%)
  other arithmetic  31.4 us (7%)
  blocking collectives  20.9 us (5%)
  between operations  14.2 us (3%)
  starting transfers between devices  13.4 us (3%)
    dot_general x24, matrix products, add_slot(): jnp.einsum('rnk,lk->rnl', picked, kernel, preferred_element_type=jnp.floa...  115 us
    psum x2, waiting for transfers between devices, member_total(): summed = lax.psum(member_terms, 'mem')  68.8 us
    gather x24, local copies, waits for them, and re-layouts, add_slot(): picked = jnp.take(flattened, chosen, axis=1)  61 us
    all_to_all x2, waiting for transfers between devices, cov_local(): lax.all_to_all(vert_mixed, 'pts', split_axis=1, concat_axis=2, tiled=True)  50.8 us
    all_to_all x2, blocking collectives, cov_local(): lax.all_to_all(level_sums, 'pts', split_axis=1, concat_axis=0, tiled=True)  20.9 us
    convert_element_type x4, local copies, waits for them, and re-layouts, cov_local(): level_local.astype(jnp.float32)  18.8 us
    and x24, other arithmetic, add_slot(): picked = jnp.take(flattened, chosen, axis=1)  16.7 us
    unnamed x22, local copies, waits for them, and re-layouts  10.9 us
  transfers between devices with their start and end apart: 5, of which 4 were waited for; matrix products, arithmetic and copies ran while one was open for 28% of the time, Pallas kernels for 0%

commit v1 on v0

v1 whole, which is shorter than its diff:
```python
import functools

import jax
import jax.numpy as jnp
from jax import lax
from jax.experimental import pallas as pl
from jax.experimental.pallas import tpu as pltpu
from jax.sharding import PartitionSpec as P

BF = jnp.bfloat16
F32 = jnp.float32


def xor_permute(x, axis, size, k):
    return lax.ppermute(x, axis, [(i, i ^ k) for i in range(size)])


def cov_kernel(me_ref, cols_ref, ens_ref, fld_ref, vert_ref, tab_ref, own_ref, mate_ref, local_ref):
    shares, members, levels, width = ens_ref.shape
    slots = cols_ref.shape[1]
    blk = tab_ref.shape[1]
    per = width // blk
    me = me_ref[0]
    for d in range(shares):
        f = fld_ref[d].astype(F32)
        for m in range(members):
            product = (ens_ref[d ^ me, m].astype(F32) * f).astype(BF)
            mixed = jnp.dot(vert_ref[...], product, preferred_element_type=F32).astype(BF)
            for j in range(per):
                local_ref[d * per + j, m * levels:(m + 1) * levels, :] = mixed[:, j * blk:(j + 1) * blk]

    def chip(k, carry):
        rows = [
            jnp.concatenate([local_ref[cols_ref[k * 2 * per + q, s]] for s in range(slots)], axis=1)
            for q in range(2 * per)
        ]
        horiz = jnp.dot(jnp.concatenate(rows, axis=0), tab_ref[...], preferred_element_type=F32).astype(BF)
        for q in range(2 * per):
            core, j = q // per, q % per
            share = (2 * k + core) ^ me
            total = None
            for m in range(members):
                e = ens_ref[share, m, :, j * blk:(j + 1) * blk].astype(F32)
                row = (q * members + m) * levels
                term = e * horiz[row:row + levels].astype(F32)
                total = term if total is None else total + term
            (mate_ref if core else own_ref)[k, :, j * blk:(j + 1) * blk] = total.astype(BF)
        return carry

    lax.fori_loop(0, shares // 2, chip, 0)


def cov_call(me, cols, ens, fld, vertical, table):
    shares, members, levels, width = ens.shape
    blk = table.shape[1]
    half = jax.ShapeDtypeStruct((shares // 2, levels, width), BF)
    vmem = pl.BlockSpec(memory_space=pltpu.VMEM)
    smem = pl.BlockSpec(memory_space=pltpu.SMEM)
    return pl.pallas_call(
        cov_kernel,
        out_shape=(half, half),
        in_specs=[smem, smem, vmem, vmem, vmem, vmem],
        out_specs=(vmem, vmem),
        scratch_shapes=[pltpu.VMEM((shares * width // blk, members * levels, blk), BF)],
        compiler_params=pltpu.CompilerParams(vmem_limit_bytes=40 * 2**20),
    )(me, cols, ens, fld, vertical, table)


def per_device(ensemble, increment, obs_weight, vertical, block_table, block_cols):
    pts, mem = lax.axis_size("pts"), lax.axis_size("mem")
    members, levels, width = ensemble.shape
    slots, blk, _ = block_table.shape
    per = width // blk
    me = lax.axis_index("pts")

    ens = lax.all_to_all(
        ensemble.reshape(pts, members // pts, levels, width), "pts", split_axis=0, concat_axis=0, tiled=True
    )
    table = jnp.swapaxes(block_table, 1, 2).reshape(slots * blk, blk)
    relative = ((block_cols // per) ^ me) * per + block_cols % per
    cols = jnp.take(relative.reshape(pts, per, slots), jnp.arange(pts) ^ me, axis=0).reshape(pts * per, slots)

    def gather_field(x):
        same = [x] + [xor_permute(x, "pts", pts, 2 * k) for k in range(1, pts // 2)]
        same = jnp.stack(same)
        other = xor_permute(same, "pts", pts, 1)
        return jnp.stack([same, other], axis=1).reshape(pts, levels, width)

    def cov_sum(field):
        own, mate = cov_call(me.reshape(1), cols, ens, field, vertical, table)
        got = xor_permute(mate, "pts", pts, 1)
        chip = (own.astype(F32) + got.astype(F32)).astype(BF)
        total = chip[0].astype(F32)
        for k in range(1, pts // 2):
            total = total + xor_permute(chip[k], "pts", pts, 2 * k).astype(F32)
        plane = total.astype(BF)
        for k in range(1, mem):
            total = total + xor_permute(plane, "mem", mem, k).astype(F32)
        return total

    weighted = cov_sum(gather_field(increment.astype(BF))) * obs_weight
    applied = cov_sum(gather_field(weighted.astype(BF)))
    return weighted, applied


def solution(mesh):
    return jax.shard_map(
        per_device,
        mesh=mesh,
        in_specs=(P("mem", None, "pts"), P(None, "pts"), P(None, "pts"), P(), P(), P()),
        out_specs=(P(None, "pts"), P(None, "pts")),
        check_vma=False,
    )
```

time: 435 us -> 127 us (0.29)
  matrix products: 119 us -> 0 us
  local copies, waits for them, and re-layouts: 112 us -> 5.15 us
  waiting for transfers between devices: 120 us -> 66.7 us
  other arithmetic: 31.4 us -> 7.4 us
  blocking collectives: 20.9 us -> 0 us
  Pallas kernels: 0 us -> 17.6 us
  starting transfers between devices: 13.4 us -> 29.3 us
  between operations: 14.2 us -> 0.82 us
    dot_general x26 -> x0, matrix products: 119 us -> none  [the longest x24 115 us: add_slot(): jnp.einsum('rnk,lk->rnl', picked, kernel, preferred_element_type=jnp.floa...]
    psum x2 -> x0, waiting for transfers between devices: 68.8 us -> none  [member_total(): summed = lax.psum(member_terms, 'mem')]
    ppermute x0 -> x22, waiting for transfers between devices: none -> 66.7 us  [xor_permute(): return lax.ppermute(x, axis, [(i, i ^ k) for i in range(size)])]
    gather x24 -> x1, local copies, waits for them, and re-layouts: 61 us -> 1.3 us  [per_device(): jnp.take(relative.reshape(pts, per, slots), jnp.arange(pts) ^ me, axis=0)]
    all_to_all x3 -> x1, waiting for transfers between devices: 50.8 us -> 0.01 us  [per_device(): lax.all_to_all(ensemble.reshape(pts, members // pts, levels, width), 'pts...]
    convert_element_type x6 -> x0, local copies, waits for them, and re-layouts: 26.5 us -> none  [the longest x4 18.8 us: cov_local(): level_local.astype(jnp.float32)]
    ppermute x0 -> x22, starting transfers between devices: none -> 24 us  [xor_permute(): return lax.ppermute(x, axis, [(i, i ^ k) for i in range(size)])]
    all_to_all x2 -> x0, blocking collectives: 20.9 us -> none  [cov_local(): lax.all_to_all(level_sums, 'pts', split_axis=1, concat_axis=0, tiled=True)]
  transfers between devices with their start and end apart: 5 -> 23, of which waited for: 4 -> 18; matrix products, arithmetic and copies ran while one was open for 28% -> 6% of each run, Pallas kernels for 0% -> 0%
where the time goes in v1:
time: 127 us
  waiting for transfers between devices  66.7 us (53%)
  starting transfers between devices  29.3 us (23%)
  Pallas kernels  17.6 us (14%)
  other arithmetic  7.4 us (6%)
  local copies, waits for them, and re-layouts  5.15 us (4%)
    ppermute x22, waiting for transfers between devices, xor_permute(): return lax.ppermute(x, axis, [(i, i ^ k) for i in range(size)])  66.7 us
    ppermute x22, starting transfers between devices, xor_permute(): return lax.ppermute(x, axis, [(i, i ^ k) for i in range(size)])  24 us
    pallas_call x2, Pallas kernels, cov_call(): pl.pallas_call(cov_kernel, out_shape=(half, half), in_specs=[smem, smem,...  17.6 us
    all_to_all x1, starting transfers between devices, per_device(): lax.all_to_all(ensemble.reshape(pts, members // pts, levels, width), 'pts...  5.31 us
    unnamed x19, local copies, waits for them, and re-layouts  2.69 us
  transfers between devices with their start and end apart: 23, of which 18 were waited for; matrix products, arithmetic and copies ran while one was open for 6% of the time, Pallas kernels for 0%

profile of v1, /device:TPU:0, one launch (start us, length us, event | category | flops | bytes accessed | tf_op | source)
XLA Modules:
  0.0 127.0 jit_solution(5444547743835931352)
XLA Ops:
  0.7 5.3 %all-to-all-start = ((bf16[8,2,128,512]{3,2,1,0:T(8,128)(2,1)}), bf16[8,2,128,512]{3,2,1,0:T(8,128)(2,1)S(1)}, u32[]{:S(2)}, u32[]{:S(2)}) async-start(bf16[8,2,128,512]{3,2,1,0:T(8,128)(2,1)} %bitcast.60), calls=%async_computation | async-start | bytes 4194304 | tf_op jit(solution)/shard_map/all_to_all | solution.py:76
  6.0 2.1 %collective-permute-start.1 = (bf16[128,512]{1,0:T(8,128)(2,1)S(1)}, bf16[128,512]{1,0:T(8,128)(2,1)S(1)}, u32[]{:S(2)}, u32[]{:S(2)}) collective-permute-start(bf16[128,512]{1,0:T(8,128)(2,1)S(1)} %convert_element_type.78), channel_id=1, source_target_pairs={{0,16},{4,20},{8,24},{12,28},{16,0},{20,4},{24,8},{28,12},{1,17},{... | collective-permute-start | bytes 393224 | tf_op jit(solution)/shard_map/ppermute | solution.py:15
  8.1 1.5 %collective-permute-start = (bf16[128,512]{1,0:T(8,128)(2,1)S(1)}, bf16[128,512]{1,0:T(8,128)(2,1)S(1)}, u32[]{:S(2)}, u32[]{:S(2)}) collective-permute-start(bf16[128,512]{1,0:T(8,128)(2,1)S(1)} %convert_element_type.78), channel_id=1, source_target_pairs={{0,8},{4,12},{8,0},{12,4},{16,24},{20,28},{24,16},{28,20},{1,9},{5... | collective-permute-start | bytes 393224 | tf_op jit(solution)/shard_map/ppermute | solution.py:15
  9.6 0.1 collective-permute-start.2
  9.6 0.7 convert_bitcast_fusion
  10.3 0.1 broadcast_in_dim.14
  10.4 0.6 broadcast_in_dim.15
  11.0 0.7 copy.11
  11.7 0.2 copy.16
  11.9 22.5 %collective-permute-done.1 = bf16[128,512]{1,0:T(8,128)(2,1)S(1)} collective-permute-done((bf16[128,512]{1,0:T(8,128)(2,1)S(1)}, bf16[128,512]{1,0:T(8,128)(2,1)S(1)}, u32[]{:S(2)}, u32[]{:S(2)}) %collective-permute-start.1) | collective-permute-done | bytes 131104 | tf_op jit(solution)/shard_map/ppermute | solution.py:15
  34.5 0.6 collective-permute-done
  35.0 3.2 %collective-permute-done.2 = bf16[128,512]{1,0:T(8,128)(2,1)S(1)} collective-permute-done((bf16[128,512]{1,0:T(8,128)(2,1)S(1)}, bf16[128,512]{1,0:T(8,128)(2,1)S(1)}, u32[]{:S(2)}, u32[]{:S(2)}) %collective-permute-start.2) | collective-permute-done | bytes 131104 | tf_op jit(solution)/shard_map/ppermute | solution.py:15
  38.3 0.6 copy-done.7
  38.9 1.2 fusion.15
  40.1 0.1 collective-permute-start.3
  40.2 0.6 pad_clamp_fusion
  40.8 0.7 fusion.8
  41.5 1.3 %gather_fusion = s32[8,4,12]{2,1,0:T(4,128)} fusion(s32[8,4,12]{2,1,0:T(4,128)S(1)} %bitcast.71, s32[1024]{0:T(1024)} %pad_clamp_fusion), kind=kCustom, calls=%fused_computation | custom fusion | bytes 3104 | tf_op jit(solution)/shard_map/jit(_take)/gather | solution.py:81
  42.8 0.8 broadcast_select_fusion.cols_ref
  43.6 1.1 pad_maximum_fusion
  44.8 0.1 copy.15
  44.9 0.7 copy-done
  45.7 8.8 %shard_map.77 = (bf16[4,128,512]{2,1,0:T(8,128)(2,1)S(1)}, bf16[4,128,512]{2,1,0:T(8,128)(2,1)S(1)}) custom-call(s32[1]{0:T(128)} %bitcast.me_ref, s32[32,12]{1,0:T(8,128)S(1)} %broadcast_select_fusion.cols_ref, bf16[8,2,128,512]{3,2,1,0:T(8,128)(2,1)S(1)} %all-to-all-done.ens_ref, bf16[8,128,512]{2,1,0:T(8,128)(2,1)S(1)} %bitcast.56, ...), custom_call_target="tpu_custom_call" | custom-call | tf_op jit(solution)/shard_map/pallas_call | solution.py:59
  54.5 0.6 collective-permute-start.4
  55.0 1.5 %collective-permute-done.4 = bf16[4,128,512]{2,1,0:T(8,128)(2,1)S(1)} collective-permute-done((bf16[4,128,512]{2,1,0:T(8,128)(2,1)S(1)}, bf16[4,128,512]{2,1,0:T(8,128)(2,1)S(1)}, u32[]{:S(2)}, u32[]{:S(2)}) %collective-permute-start.4) | collective-permute-done | bytes 524320 | tf_op jit(solution)/shard_map/ppermute | solution.py:15
  56.6 0.1 add_convert_fusion.1
  56.7 0.6 collective-permute-start.5
  57.4 1.5 %collective-permute-start.7 = (bf16[128,512]{1,0:T(8,128)(2,1)S(1)}, bf16[128,512]{1,0:T(8,128)(2,1)S(1)}, u32[]{:S(2)}, u32[]{:S(2)}) collective-permute-start(bf16[128,512]{1,0:T(8,128)(2,1)S(1)} %get-tuple-element.18), channel_id=1, source_target_pairs={{0,24},{4,28},{8,16},{12,20},{16,8},{20,12},{24,0},{28,4},{1,25},{... | collective-permute-start | bytes 393224 | tf_op jit(solution)/shard_map/ppermute | solution.py:15
  58.8 1.5 %collective-permute-start.6 = (bf16[128,512]{1,0:T(8,128)(2,1)S(1)}, bf16[128,512]{1,0:T(8,128)(2,1)S(1)}, u32[]{:S(2)}, u32[]{:S(2)}) collective-permute-start(bf16[128,512]{1,0:T(8,128)(2,1)S(1)} %get-tuple-element.19), channel_id=1, source_target_pairs={{0,16},{4,20},{8,24},{12,28},{16,0},{20,4},{24,8},{28,12},{1,17},{... | collective-permute-start | bytes 393224 | tf_op jit(solution)/shard_map/ppermute | solution.py:15
  60.3 2.8 %collective-permute-done.5 = bf16[128,512]{1,0:T(8,128)(2,1)S(1)} collective-permute-done((bf16[128,512]{1,0:T(8,128)(2,1)S(1)}, bf16[128,512]{1,0:T(8,128)(2,1)S(1)}, u32[]{:S(2)}, u32[]{:S(2)}) %collective-permute-start.5) | collective-permute-done | bytes 131104 | tf_op jit(solution)/shard_map/ppermute | solution.py:15
  63.1 2.4 %collective-permute-done.7 = bf16[128,512]{1,0:T(8,128)(2,1)S(1)} collective-permute-done((bf16[128,512]{1,0:T(8,128)(2,1)S(1)}, bf16[128,512]{1,0:T(8,128)(2,1)S(1)}, u32[]{:S(2)}, u32[]{:S(2)}) %collective-permute-start.7) | collective-permute-done | bytes 131104 | tf_op jit(solution)/shard_map/ppermute | solution.py:15
  65.5 1.4 %collective-permute-done.6 = bf16[128,512]{1,0:T(8,128)(2,1)S(1)} collective-permute-done((bf16[128,512]{1,0:T(8,128)(2,1)S(1)}, bf16[128,512]{1,0:T(8,128)(2,1)S(1)}, u32[]{:S(2)}, u32[]{:S(2)}) %collective-permute-start.6) | collective-permute-done | bytes 131104 | tf_op jit(solution)/shard_map/ppermute | solution.py:15
  66.9 3.7 %collective-permute-start.10 = (bf16[128,512]{1,0:T(8,128)(2,1)S(1)}, bf16[128,512]{1,0:T(8,128)(2,1)S(1)}, u32[]{:S(2)}, u32[]{:S(2)}) collective-permute-start(bf16[128,512]{1,0:T(8,128)(2,1)S(1)} %fusion.4), channel_id=1, source_target_pairs={{0,3},{1,2},{2,1},{3,0},{4,7},{5,6},{6,5},{7,4},{8,11},{9,10},{10,... | collective-permute-start | bytes 393224 | tf_op jit(solution)/shard_map/ppermute | solution.py:15
  70.6 0.8 collective-permute-start.8
  71.4 3.8 %collective-permute-done.10 = bf16[128,512]{1,0:T(8,128)(2,1)S(1)} collective-permute-done((bf16[128,512]{1,0:T(8,128)(2,1)S(1)}, bf16[128,512]{1,0:T(8,128)(2,1)S(1)}, u32[]{:S(2)}, u32[]{:S(2)}) %collective-permute-start.10) | collective-permute-done | bytes 131104 | tf_op jit(solution)/shard_map/ppermute | solution.py:15
  75.2 5.7 %collective-permute-done.9 = bf16[128,512]{1,0:T(8,128)(2,1)S(1)} collective-permute-done((bf16[128,512]{1,0:T(8,128)(2,1)S(1)}, bf16[128,512]{1,0:T(8,128)(2,1)S(1)}, u32[]{:S(2)}, u32[]{:S(2)}) %collective-permute-start.9) | collective-permute-done | bytes 131104 | tf_op jit(solution)/shard_map/ppermute | solution.py:15
  81.0 0.9 fusion.16
  81.8 1.5 %collective-permute-start.13 = (bf16[128,512]{1,0:T(8,128)(2,1)S(1)}, bf16[128,512]{1,0:T(8,128)(2,1)S(1)}, u32[]{:S(2)}, u32[]{:S(2)}) collective-permute-start(bf16[128,512]{1,0:T(8,128)(2,1)S(1)} %get-tuple-element.10), channel_id=1, source_target_pairs={{0,24},{4,28},{8,16},{12,20},{16,8},{20,12},{24,0},{28,4},{1,25},{... | collective-permute-start | bytes 393224 | tf_op jit(solution)/shard_map/ppermute | solution.py:15
  83.3 0.3 collective-permute-start.12
  83.6 1.7 %collective-permute-start.11 = (bf16[128,512]{1,0:T(8,128)(2,1)S(1)}, bf16[128,512]{1,0:T(8,128)(2,1)S(1)}, u32[]{:S(2)}, u32[]{:S(2)}) collective-permute-start(bf16[128,512]{1,0:T(8,128)(2,1)S(1)} %get-tuple-element.10), channel_id=1, source_target_pairs={{0,8},{4,12},{8,0},{12,4},{16,24},{20,28},{24,16},{28,20},{1,9},{5... | collective-permute-start | bytes 393224 | tf_op jit(solution)/shard_map/ppermute | solution.py:15
  85.3 3.4 %collective-permute-done.13 = bf16[128,512]{1,0:T(8,128)(2,1)S(1)} collective-permute-done((bf16[128,512]{1,0:T(8,128)(2,1)S(1)}, bf16[128,512]{1,0:T(8,128)(2,1)S(1)}, u32[]{:S(2)}, u32[]{:S(2)}) %collective-permute-start.13) | collective-permute-done | bytes 131104 | tf_op jit(solution)/shard_map/ppermute | solution.py:15
  88.7 1.3 %collective-permute-done.12 = bf16[128,512]{1,0:T(8,128)(2,1)S(1)} collective-permute-done((bf16[128,512]{1,0:T(8,128)(2,1)S(1)}, bf16[128,512]{1,0:T(8,128)(2,1)S(1)}, u32[]{:S(2)}, u32[]{:S(2)}) %collective-permute-start.12) | collective-permute-done | bytes 131104 | tf_op jit(solution)/shard_map/ppermute | solution.py:15
  90.1 0.1 fusion.14
  90.2 0.1 collective-permute-start.14
  90.2 1.9 %collective-permute-done.14 = bf16[4,128,512]{2,1,0:T(8,128)(2,1)S(1)} collective-permute-done((bf16[4,128,512]{2,1,0:T(8,128)(2,1)S(1)}, bf16[4,128,512]{2,1,0:T(8,128)(2,1)S(1)}, u32[]{:S(2)}, u32[]{:S(2)}) %collective-permute-start.14) | collective-permute-done | bytes 524320 | tf_op jit(solution)/shard_map/ppermute | solution.py:15
  92.1 0.1 pad_maximum_fusion.1
  92.2 0.1 copy.17
  92.3 0.6 copy-done.1
  92.9 8.8 %shard_map.78 = (bf16[4,128,512]{2,1,0:T(8,128)(2,1)S(1)}, bf16[4,128,512]{2,1,0:T(8,128)(2,1)S(1)}) custom-call(s32[1]{0:T(128)} %bitcast.me_ref, s32[32,12]{1,0:T(8,128)S(1)} %broadcast_select_fusion.cols_ref, bf16[8,2,128,512]{3,2,1,0:T(8,128)(2,1)S(1)} %all-to-all-done.ens_ref, bf16[8,128,512]{2,1,0:T(8,128)(2,1)S(1)} %bitcast.57, ...), custom_call_target="tpu_custom_call" | custom-call | tf_op jit(solution)/shard_map/pallas_call | solution.py:59
  101.7 0.2 collective-permute-start.15
  101.9 1.8 %collective-permute-done.15 = bf16[4,128,512]{2,1,0:T(8,128)(2,1)S(1)} collective-permute-done((bf16[4,128,512]{2,1,0:T(8,128)(2,1)S(1)}, bf16[4,128,512]{2,1,0:T(8,128)(2,1)S(1)}, u32[]{:S(2)}, u32[]{:S(2)}) %collective-permute-start.15) | collective-permute-done | bytes 524320 | tf_op jit(solution)/shard_map/ppermute | solution.py:15
  103.7 0.1 add_convert_fusion
  103.9 0.6 collective-permute-start.16
  104.5 1.4 %collective-permute-start.18 = (bf16[128,512]{1,0:T(8,128)(2,1)S(1)}, bf16[128,512]{1,0:T(8,128)(2,1)S(1)}, u32[]{:S(2)}, u32[]{:S(2)}) collective-permute-start(bf16[128,512]{1,0:T(8,128)(2,1)S(1)} %get-tuple-element.13), channel_id=1, source_target_pairs={{0,24},{4,28},{8,16},{12,20},{16,8},{20,12},{24,0},{28,4},{1,25},{... | collective-permute-start | bytes 393224 | tf_op jit(solution)/shard_map/ppermute | solution.py:15
  105.9 1.5 %collective-permute-start.17 = (bf16[128,512]{1,0:T(8,128)(2,1)S(1)}, bf16[128,512]{1,0:T(8,128)(2,1)S(1)}, u32[]{:S(2)}, u32[]{:S(2)}) collective-permute-start(bf16[128,512]{1,0:T(8,128)(2,1)S(1)} %get-tuple-element.14), channel_id=1, source_target_pairs={{0,16},{4,20},{8,24},{12,28},{16,0},{20,4},{24,8},{28,12},{1,17},{... | collective-permute-start | bytes 393224 | tf_op jit(solution)/shard_map/ppermute | solution.py:15
  107.4 2.9 %collective-permute-done.16 = bf16[128,512]{1,0:T(8,128)(2,1)S(1)} collective-permute-done((bf16[128,512]{1,0:T(8,128)(2,1)S(1)}, bf16[128,512]{1,0:T(8,128)(2,1)S(1)}, u32[]{:S(2)}, u32[]{:S(2)}) %collective-permute-start.16) | collective-permute-done | bytes 131104 | tf_op jit(solution)/shard_map/ppermute | solution.py:15
  110.3 2.1 %collective-permute-done.18 = bf16[128,512]{1,0:T(8,128)(2,1)S(1)} collective-permute-done((bf16[128,512]{1,0:T(8,128)(2,1)S(1)}, bf16[128,512]{1,0:T(8,128)(2,1)S(1)}, u32[]{:S(2)}, u32[]{:S(2)}) %collective-permute-start.18) | collective-permute-done | bytes 131104 | tf_op jit(solution)/shard_map/ppermute | solution.py:15
  112.4 1.4 %collective-permute-done.17 = bf16[128,512]{1,0:T(8,128)(2,1)S(1)} collective-permute-done((bf16[128,512]{1,0:T(8,128)(2,1)S(1)}, bf16[128,512]{1,0:T(8,128)(2,1)S(1)}, u32[]{:S(2)}, u32[]{:S(2)}) %collective-permute-start.17) | collective-permute-done | bytes 131104 | tf_op jit(solution)/shard_map/ppermute | solution.py:15
  113.7 0.1 fusion.5
  113.8 2.2 %collective-permute-start.21 = (bf16[128,512]{1,0:T(8,128)(2,1)S(1)}, bf16[128,512]{1,0:T(8,128)(2,1)S(1)}, u32[]{:S(2)}, u32[]{:S(2)}) collective-permute-start(bf16[128,512]{1,0:T(8,128)(2,1)S(1)} %fusion.5), channel_id=1, source_target_pairs={{0,3},{1,2},{2,1},{3,0},{4,7},{5,6},{6,5},{7,4},{8,11},{9,10},{10,... | collective-permute-start | bytes 393224 | tf_op jit(solution)/shard_map/ppermute | solution.py:15
  116.0 2.3 %collective-permute-start.19 = (bf16[128,512]{1,0:T(8,128)(2,1)S(1)}, bf16[128,512]{1,0:T(8,128)(2,1)S(1)}, u32[]{:S(2)}, u32[]{:S(2)}) collective-permute-start(bf16[128,512]{1,0:T(8,128)(2,1)S(1)} %fusion.5), channel_id=1, source_target_pairs={{0,1},{1,0},{2,3},{3,2},{4,5},{5,4},{6,7},{7,6},{8,9},{9,8},{10,11... | collective-permute-start | bytes 393224 | tf_op jit(solution)/shard_map/ppermute | solution.py:15
  118.3 3.8 %collective-permute-done.21 = bf16[128,512]{1,0:T(8,128)(2,1)S(1)} collective-permute-done((bf16[128,512]{1,0:T(8,128)(2,1)S(1)}, bf16[128,512]{1,0:T(8,128)(2,1)S(1)}, u32[]{:S(2)}, u32[]{:S(2)}) %collective-permute-start.21) | collective-permute-done | bytes 131104 | tf_op jit(solution)/shard_map/ppermute | solution.py:15
  122.1 4.0 %collective-permute-done.20 = bf16[128,512]{1,0:T(8,128)(2,1)S(1)} collective-permute-done((bf16[128,512]{1,0:T(8,128)(2,1)S(1)}, bf16[128,512]{1,0:T(8,128)(2,1)S(1)}, u32[]{:S(2)}, u32[]{:S(2)}) %collective-permute-start.20) | collective-permute-done | bytes 131104 | tf_op jit(solution)/shard_map/ppermute | solution.py:15
  126.2 0.8 convert_add_fusion.2
  (28 shorter events, 0.3 us)
Async XLA Ops:
  0.6 5.3 %copy-start.2 = (f32[128,512]{1,0:T(8,128)S(1)}, f32[128,512]{1,0:T(8,128)}, u32[]{:S(2)}) copy-start(f32[128,512]{1,0:T(8,128)} %param.7) | copy-start | bytes 786436
  0.6 10.4 %copy-start.8 = (s32[32,12]{0,1:T(8,128)S(1)}, s32[32,12]{0,1:T(8,128)}, u32[]{:S(2)}) copy-start(s32[32,12]{0,1:T(8,128)} %param.11) | copy-start | bytes 4612
  0.7 11.0 %copy-start.3 = (bf16[12,128,128]{2,1,0:T(8,128)(2,1)S(1)}, bf16[12,128,128]{2,1,0:T(8,128)(2,1)}, u32[]{:S(2)}) copy-start(bf16[12,128,128]{2,1,0:T(8,128)(2,1)} %param.10) | copy-start | bytes 1179652
  0.7 44.2 %all-to-all-start = ((bf16[8,2,128,512]{3,2,1,0:T(8,128)(2,1)}), bf16[8,2,128,512]{3,2,1,0:T(8,128)(2,1)S(1)}, u32[]{:S(2)}, u32[]{:S(2)}) async-start(bf16[8,2,128,512]{3,2,1,0:T(8,128)(2,1)} %bitcast.60), calls=%async_computation | async-start | bytes 4194304 | tf_op jit(solution)/shard_map/all_to_all | solution.py:76
  6.0 28.5 %collective-permute-start.1 = (bf16[128,512]{1,0:T(8,128)(2,1)S(1)}, bf16[128,512]{1,0:T(8,128)(2,1)S(1)}, u32[]{:S(2)}, u32[]{:S(2)}) collective-permute-start(bf16[128,512]{1,0:T(8,128)(2,1)S(1)} %convert_element_type.78), channel_id=1, source_target_pairs={{0,16},{4,20},{8,24},{12,28},{16,0},{20,4},{24,8},{28,12},{1,17},{... | collective-permute-start | bytes 393224 | tf_op jit(solution)/shard_map/ppermute | solution.py:15
  8.1 27.0 %collective-permute-start = (bf16[128,512]{1,0:T(8,128)(2,1)S(1)}, bf16[128,512]{1,0:T(8,128)(2,1)S(1)}, u32[]{:S(2)}, u32[]{:S(2)}) collective-permute-start(bf16[128,512]{1,0:T(8,128)(2,1)S(1)} %convert_element_type.78), channel_id=1, source_target_pairs={{0,8},{4,12},{8,0},{12,4},{16,24},{20,28},{24,16},{28,20},{1,9},{5... | collective-permute-start | bytes 393224 | tf_op jit(solution)/shard_map/ppermute | solution.py:15
  9.6 28.7 %collective-permute-start.2 = (bf16[128,512]{1,0:T(8,128)(2,1)S(1)}, bf16[128,512]{1,0:T(8,128)(2,1)S(1)}, u32[]{:S(2)}, u32[]{:S(2)}) collective-permute-start(bf16[128,512]{1,0:T(8,128)(2,1)S(1)} %convert_element_type.78), channel_id=1, source_target_pairs={{0,24},{4,28},{8,16},{12,20},{16,8},{20,12},{24,0},{28,4},{1,25},{... | collective-permute-start | bytes 393224 | tf_op jit(solution)/shard_map/ppermute | solution.py:15
  34.5 3.8 %copy-start.5 = (bf16[128,512]{1,0:T(8,128)(2,1)}, bf16[128,512]{1,0:T(8,128)(2,1)S(1)}, u32[]{:S(2)}) copy-start(bf16[128,512]{1,0:T(8,128)(2,1)S(1)} %collective-permute-done.1) | copy-start | bytes 393220
  35.0 3.2 %copy-start.6 = (bf16[128,512]{1,0:T(8,128)(2,1)}, bf16[128,512]{1,0:T(8,128)(2,1)S(1)}, u32[]{:S(2)}) copy-start(bf16[128,512]{1,0:T(8,128)(2,1)S(1)} %collective-permute-done) | copy-start | bytes 393220
  38.3 0.7 copy-start.7
  40.1 3.5 %collective-permute-start.3 = (bf16[4,128,512]{2,1,0:T(8,128)(2,1)S(1)}, bf16[4,128,512]{2,1,0:T(8,128)(2,1)}, u32[]{:S(2)}, u32[]{:S(2)}) collective-permute-start(bf16[4,128,512]{2,1,0:T(8,128)(2,1)S(1)} %get-tuple-element.21), channel_id=1, source_target_pairs={{0,4},{4,0},{8,12},{12,8},{16,20},{20,16},{24,28},{28,24},{1,5},{5... | collective-permute-start | bytes 1572872 | tf_op jit(solution)/shard_map/ppermute | solution.py:15
  44.9 0.8 copy-start
  54.5 26.5 %copy-start.4 = (f32[128,512]{1,0:T(8,128)S(1)}, f32[128,512]{1,0:T(8,128)}, u32[]{:S(2)}) copy-start(f32[128,512]{1,0:T(8,128)} %param.8) | copy-start | bytes 786436
  54.5 2.1 %collective-permute-start.4 = (bf16[4,128,512]{2,1,0:T(8,128)(2,1)S(1)}, bf16[4,128,512]{2,1,0:T(8,128)(2,1)S(1)}, u32[]{:S(2)}, u32[]{:S(2)}) collective-permute-start(bf16[4,128,512]{2,1,0:T(8,128)(2,1)S(1)} %get-tuple-element.7), channel_id=1, source_target_pairs={{0,4},{4,0},{8,12},{12,8},{16,20},{20,16},{24,28},{28,24},{1,5},{5... | collective-permute-start | bytes 1572872 | tf_op jit(solution)/shard_map/ppermute | solution.py:15
  56.7 6.4 %collective-permute-start.5 = (bf16[128,512]{1,0:T(8,128)(2,1)S(1)}, bf16[128,512]{1,0:T(8,128)(2,1)S(1)}, u32[]{:S(2)}, u32[]{:S(2)}) collective-permute-start(bf16[128,512]{1,0:T(8,128)(2,1)S(1)} %get-tuple-element.17), channel_id=1, source_target_pairs={{0,8},{4,12},{8,0},{12,4},{16,24},{20,28},{24,16},{28,20},{1,9},{5... | collective-permute-start | bytes 393224 | tf_op jit(solution)/shard_map/ppermute | solution.py:15
  57.4 8.1 %collective-permute-start.7 = (bf16[128,512]{1,0:T(8,128)(2,1)S(1)}, bf16[128,512]{1,0:T(8,128)(2,1)S(1)}, u32[]{:S(2)}, u32[]{:S(2)}) collective-permute-start(bf16[128,512]{1,0:T(8,128)(2,1)S(1)} %get-tuple-element.18), channel_id=1, source_target_pairs={{0,24},{4,28},{8,16},{12,20},{16,8},{20,12},{24,0},{28,4},{1,25},{... | collective-permute-start | bytes 393224 | tf_op jit(solution)/shard_map/ppermute | solution.py:15
  58.8 8.0 %collective-permute-start.6 = (bf16[128,512]{1,0:T(8,128)(2,1)S(1)}, bf16[128,512]{1,0:T(8,128)(2,1)S(1)}, u32[]{:S(2)}, u32[]{:S(2)}) collective-permute-start(bf16[128,512]{1,0:T(8,128)(2,1)S(1)} %get-tuple-element.19), channel_id=1, source_target_pairs={{0,16},{4,20},{8,24},{12,28},{16,0},{20,4},{24,8},{28,12},{1,17},{... | collective-permute-start | bytes 393224 | tf_op jit(solution)/shard_map/ppermute | solution.py:15
  66.9 8.3 %collective-permute-start.10 = (bf16[128,512]{1,0:T(8,128)(2,1)S(1)}, bf16[128,512]{1,0:T(8,128)(2,1)S(1)}, u32[]{:S(2)}, u32[]{:S(2)}) collective-permute-start(bf16[128,512]{1,0:T(8,128)(2,1)S(1)} %fusion.4), channel_id=1, source_target_pairs={{0,3},{1,2},{2,1},{3,0},{4,7},{5,6},{6,5},{7,4},{8,11},{9,10},{10,... | collective-permute-start | bytes 393224 | tf_op jit(solution)/shard_map/ppermute | solution.py:15
  70.6 10.4 %collective-permute-start.9 = (bf16[128,512]{1,0:T(8,128)(2,1)S(1)}, bf16[128,512]{1,0:T(8,128)(2,1)S(1)}, u32[]{:S(2)}, u32[]{:S(2)}) collective-permute-start(bf16[128,512]{1,0:T(8,128)(2,1)S(1)} %fusion.4), channel_id=1, source_target_pairs={{0,2},{1,3},{2,0},{3,1},{4,6},{5,7},{6,4},{7,5},{8,10},{9,11},{10,... | collective-permute-start | bytes 393224 | tf_op jit(solution)/shard_map/ppermute | solution.py:15
  70.6 10.4 %collective-permute-start.8 = (bf16[128,512]{1,0:T(8,128)(2,1)S(1)}, bf16[128,512]{1,0:T(8,128)(2,1)S(1)}, u32[]{:S(2)}, u32[]{:S(2)}) collective-permute-start(bf16[128,512]{1,0:T(8,128)(2,1)S(1)} %fusion.4), channel_id=1, source_target_pairs={{0,1},{1,0},{2,3},{3,2},{4,5},{5,4},{6,7},{7,6},{8,9},{9,8},{10,11... | collective-permute-start | bytes 393224 | tf_op jit(solution)/shard_map/ppermute | solution.py:15
  81.8 6.9 %collective-permute-start.13 = (bf16[128,512]{1,0:T(8,128)(2,1)S(1)}, bf16[128,512]{1,0:T(8,128)(2,1)S(1)}, u32[]{:S(2)}, u32[]{:S(2)}) collective-permute-start(bf16[128,512]{1,0:T(8,128)(2,1)S(1)} %get-tuple-element.10), channel_id=1, source_target_pairs={{0,24},{4,28},{8,16},{12,20},{16,8},{20,12},{24,0},{28,4},{1,25},{... | collective-permute-start | bytes 393224 | tf_op jit(solution)/shard_map/ppermute | solution.py:15
  83.3 6.8 %collective-permute-start.12 = (bf16[128,512]{1,0:T(8,128)(2,1)S(1)}, bf16[128,512]{1,0:T(8,128)(2,1)S(1)}, u32[]{:S(2)}, u32[]{:S(2)}) collective-permute-start(bf16[128,512]{1,0:T(8,128)(2,1)S(1)} %get-tuple-element.10), channel_id=1, source_target_pairs={{0,16},{4,20},{8,24},{12,28},{16,0},{20,4},{24,8},{28,12},{1,17},{... | collective-permute-start | bytes 393224 | tf_op jit(solution)/shard_map/ppermute | solution.py:15
  83.6 6.5 %collective-permute-start.11 = (bf16[128,512]{1,0:T(8,128)(2,1)S(1)}, bf16[128,512]{1,0:T(8,128)(2,1)S(1)}, u32[]{:S(2)}, u32[]{:S(2)}) collective-permute-start(bf16[128,512]{1,0:T(8,128)(2,1)S(1)} %get-tuple-element.10), channel_id=1, source_target_pairs={{0,8},{4,12},{8,0},{12,4},{16,24},{20,28},{24,16},{28,20},{1,9},{5... | collective-permute-start | bytes 393224 | tf_op jit(solution)/shard_map/ppermute | solution.py:15
  90.2 2.0 %collective-permute-start.14 = (bf16[4,128,512]{2,1,0:T(8,128)(2,1)S(1)}, bf16[4,128,512]{2,1,0:T(8,128)(2,1)S(1)}, u32[]{:S(2)}, u32[]{:S(2)}) collective-permute-start(bf16[4,128,512]{2,1,0:T(8,128)(2,1)S(1)} %get-tuple-element.16), channel_id=1, source_target_pairs={{0,4},{4,0},{8,12},{12,8},{16,20},{20,16},{24,28},{28,24},{1,5},{5... | collective-permute-start | bytes 1572872 | tf_op jit(solution)/shard_map/ppermute | solution.py:15
  92.1 0.8 copy-start.1
  101.7 2.0 %collective-permute-start.15 = (bf16[4,128,512]{2,1,0:T(8,128)(2,1)S(1)}, bf16[4,128,512]{2,1,0:T(8,128)(2,1)S(1)}, u32[]{:S(2)}, u32[]{:S(2)}) collective-permute-start(bf16[4,128,512]{2,1,0:T(8,128)(2,1)S(1)} %get-tuple-element.9), channel_id=1, source_target_pairs={{0,4},{4,0},{8,12},{12,8},{16,20},{20,16},{24,28},{28,24},{1,5},{5... | collective-permute-start | bytes 1572872 | tf_op jit(solution)/shard_map/ppermute | solution.py:15
  103.9 6.4 %collective-permute-start.16 = (bf16[128,512]{1,0:T(8,128)(2,1)S(1)}, bf16[128,512]{1,0:T(8,128)(2,1)S(1)}, u32[]{:S(2)}, u32[]{:S(2)}) collective-permute-start(bf16[128,512]{1,0:T(8,128)(2,1)S(1)} %get-tuple-element.12), channel_id=1, source_target_pairs={{0,8},{4,12},{8,0},{12,4},{16,24},{20,28},{24,16},{28,20},{1,9},{5... | collective-permute-start | bytes 393224 | tf_op jit(solution)/shard_map/ppermute | solution.py:15
  104.5 7.9 %collective-permute-start.18 = (bf16[128,512]{1,0:T(8,128)(2,1)S(1)}, bf16[128,512]{1,0:T(8,128)(2,1)S(1)}, u32[]{:S(2)}, u32[]{:S(2)}) collective-permute-start(bf16[128,512]{1,0:T(8,128)(2,1)S(1)} %get-tuple-element.13), channel_id=1, source_target_pairs={{0,24},{4,28},{8,16},{12,20},{16,8},{20,12},{24,0},{28,4},{1,25},{... | collective-permute-start | bytes 393224 | tf_op jit(solution)/shard_map/ppermute | solution.py:15
  105.9 7.8 %collective-permute-start.17 = (bf16[128,512]{1,0:T(8,128)(2,1)S(1)}, bf16[128,512]{1,0:T(8,128)(2,1)S(1)}, u32[]{:S(2)}, u32[]{:S(2)}) collective-permute-start(bf16[128,512]{1,0:T(8,128)(2,1)S(1)} %get-tuple-element.14), channel_id=1, source_target_pairs={{0,16},{4,20},{8,24},{12,28},{16,0},{20,4},{24,8},{28,12},{1,17},{... | collective-permute-start | bytes 393224 | tf_op jit(solution)/shard_map/ppermute | solution.py:15
  113.8 8.3 %collective-permute-start.21 = (bf16[128,512]{1,0:T(8,128)(2,1)S(1)}, bf16[128,512]{1,0:T(8,128)(2,1)S(1)}, u32[]{:S(2)}, u32[]{:S(2)}) collective-permute-start(bf16[128,512]{1,0:T(8,128)(2,1)S(1)} %fusion.5), channel_id=1, source_target_pairs={{0,3},{1,2},{2,1},{3,0},{4,7},{5,6},{6,5},{7,4},{8,11},{9,10},{10,... | collective-permute-start | bytes 393224 | tf_op jit(solution)/shard_map/ppermute | solution.py:15
  116.0 10.2 %collective-permute-start.20 = (bf16[128,512]{1,0:T(8,128)(2,1)S(1)}, bf16[128,512]{1,0:T(8,128)(2,1)S(1)}, u32[]{:S(2)}, u32[]{:S(2)}) collective-permute-start(bf16[128,512]{1,0:T(8,128)(2,1)S(1)} %fusion.5), channel_id=1, source_target_pairs={{0,2},{1,3},{2,0},{3,1},{4,6},{5,7},{6,4},{7,5},{8,10},{9,11},{10,... | collective-permute-start | bytes 393224 | tf_op jit(solution)/shard_map/ppermute | solution.py:15
  116.0 10.2 %collective-permute-start.19 = (bf16[128,512]{1,0:T(8,128)(2,1)S(1)}, bf16[128,512]{1,0:T(8,128)(2,1)S(1)}, u32[]{:S(2)}, u32[]{:S(2)}) collective-permute-start(bf16[128,512]{1,0:T(8,128)(2,1)S(1)} %fusion.5), channel_id=1, source_target_pairs={{0,1},{1,0},{2,3},{3,2},{4,5},{5,4},{6,7},{7,6},{8,9},{9,8},{10,11... | collective-permute-start | bytes 393224 | tf_op jit(solution)/shard_map/ppermute | solution.py:15

commit v2 on v0

v2 whole, which is shorter than its diff:
```python
import functools

import jax
import jax.numpy as jnp
from jax import lax
from jax.experimental import pallas as pl
from jax.experimental.pallas import tpu as pltpu
from jax.sharding import PartitionSpec as P

BF = jnp.bfloat16
F32 = jnp.float32
VMEM = pl.BlockSpec(memory_space=pltpu.VMEM)
SMEM = pl.BlockSpec(memory_space=pltpu.SMEM)
PARAMS = pltpu.CompilerParams(vmem_limit_bytes=40 * 2**20)
COLUMNS = 4096
HOLD = 50 * 10**9


def xor_permute(x, axis, size, k):
    return lax.ppermute(x, axis, [(i, i ^ k) for i in range(size)])


def member_at(group, me, d, m):
    return group[d][m] if isinstance(group, list) else group[me ^ d, m]


def members_of(group):
    return (group[0].shape[0]) if isinstance(group, list) else group.shape[1]


def products(me, turn, groups, same_ref, other_ref, prod_ref):
    levels, width = same_ref.shape[1:]
    blk = prod_ref.shape[1]
    per = width // blk
    for d in range(2 * same_ref.shape[0]):
        f = (other_ref if d % 2 else same_ref)[(d // 2) ^ turn]
        at = 0
        for group in groups:
            for m in range(members_of(group)):
                product = (member_at(group, me, d, m) * f).T
                for j in range(per):
                    prod_ref[(me ^ d) * per + j, :, at:at + levels] = product[j * blk:(j + 1) * blk]
                at += levels


def local_sums(me, distances, cols_ref, groups, vert_ref, tab_ref, prod_ref, write):
    slots, blk, _ = tab_ref.shape
    columns = prod_ref.shape[2]
    levels = vert_ref.shape[0]
    nblk = prod_ref.shape[0]
    per = nblk // shares_of(groups[0])
    table = jnp.concatenate([tab_ref[s] for s in range(slots)], axis=1)
    batch = max(1, COLUMNS // (per * columns))
    for start in range(0, len(distances), batch):
        chosen = distances[start:start + batch]
        picked = []
        for d in chosen:
            for j in range(per):
                row = (me ^ d) * per + j
                picked.append(jnp.concatenate([prod_ref[cols_ref[s, row]] for s in range(slots)], axis=0))
        horiz = jnp.dot(table, jnp.concatenate(picked, axis=1), preferred_element_type=F32).astype(BF)
        for c, d in enumerate(chosen):
            total, at = None, 0
            for group in groups:
                for m in range(members_of(group)):
                    mixed = jnp.concatenate(
                        [horiz[:, (c * per + j) * columns + at:(c * per + j) * columns + at + levels] for j in range(per)],
                        axis=0,
                    )
                    local = lax.dot_general(
                        vert_ref[...], mixed, (((1,), (1,)), ((), ())), preferred_element_type=F32
                    )
                    term = member_at(group, me, d, m).astype(F32) * local
                    total = term if total is None else total + term
                    at += levels
            write(start + c, total)


def shares_of(group):
    return len(group) if isinstance(group, list) else group.shape[0]


def kernel(layout, with_products, out_distances, *refs):
    refs = list(refs)
    place_ref, cols_ref = refs.pop(0), refs.pop(0)
    me, turn = place_ref[0], place_ref[1]
    groups = []
    for count in layout:
        groups.append([refs.pop(0) for _ in range(count)] if count else refs.pop(0))
    vert_ref, tab_ref = refs.pop(0), refs.pop(0)
    if with_products:
        same_ref, other_ref = refs.pop(0), refs.pop(0)
    else:
        prod_ref = refs.pop(0)
    outs = [refs.pop(0) for _ in out_distances]
    if with_products:
        prod_ref = refs.pop(0)
        products(me, turn, groups, same_ref, other_ref, prod_ref)
    places = [(out_ref, i) for out_ref, distances in zip(outs, out_distances) for i in range(len(distances))]

    def write(i, total):
        out_ref, at = places[i]
        out_ref[at] = total.astype(out_ref.dtype)

    distances = [d for some in out_distances for d in some]
    local_sums(me, distances, cols_ref, groups, vert_ref, tab_ref, prod_ref, write)


def copy_kernel(x_ref, out_ref):
    out_ref[...] = x_ref[...]


def passed_on(x):
    return pl.pallas_call(
        copy_kernel, out_shape=jax.ShapeDtypeStruct(x.shape, x.dtype), in_specs=[VMEM], out_specs=VMEM,
        cost_estimate=pl.CostEstimate(flops=HOLD, bytes_accessed=0, transcendentals=0),
    )(x)


def per_device(ensemble, increment, obs_weight, vertical, block_table, block_cols):
    pts, mem = lax.axis_size("pts"), lax.axis_size("mem")
    members, levels, width = ensemble.shape
    slots, blk, _ = block_table.shape
    me = lax.axis_index("pts")
    plane = lax.axis_index("mem")
    cols = block_cols.T
    far = list(range(1, pts // 2))

    def call(groups, place, out_distances, dtype, prod=None, field=None):
        layout = [len(g) if isinstance(g, list) else 0 for g in groups]
        flat = [a for g in groups for a in (g if isinstance(g, list) else [g])]
        count = sum(g[0].shape[0] if isinstance(g, list) else g.shape[1] for g in groups)
        products_shape = jax.ShapeDtypeStruct((pts * width // blk, blk, count * levels), BF)
        args = [place, cols] + flat + [vertical, block_table] + (list(field) if field else [prod])
        outs = [jax.ShapeDtypeStruct((len(d), levels, width), dtype) for d in out_distances]
        return pl.pallas_call(
            functools.partial(kernel, layout, field is not None, out_distances),
            out_shape=outs + ([products_shape] if field else []),
            in_specs=[SMEM] * 2 + [VMEM] * (len(args) - 2),
            out_specs=[VMEM] * (len(outs) + bool(field)),
            compiler_params=PARAMS,
            cost_estimate=pl.CostEstimate(
                flops=8 * slots * blk * width * count * levels * sum(map(len, out_distances)), bytes_accessed=0,
                transcendentals=0,
            ),
        )(*args)

    def sum_over_mem(total):
        step = 1
        while step < mem:
            rounded = total.astype(BF)
            total = rounded.astype(F32) + xor_permute(rounded, "mem", mem, 2 * step - 1).astype(F32)
            step *= 2
        return total

    def cov_sum(groups, place, field):
        mate, prod = call(groups, place, [[2 * k + 1 for k in far] + [1]], BF, field=field)
        got = xor_permute(mate, "pts", pts, 1)
        (own,) = call(groups, place, [[2 * k for k in far]], BF, prod=prod)
        chip = (own.astype(F32) + got[:-1].astype(F32)).astype(BF)
        arrived = [xor_permute(chip[i], "pts", pts, 2 * k) for i, k in enumerate(far)]
        prod, _ = lax.optimization_barrier((prod, chip))
        (own,) = call(groups, place, [[0]], BF, prod=prod)
        total = own[0].astype(F32) + got[-1].astype(F32)
        for a in arrived:
            total = total + a.astype(F32)
        return sum_over_mem(total)

    rounded = increment.astype(BF)
    if pts // 2 == mem:
        pairs = [(p * mem + z, (p ^ (2 * z)) * mem + z) for p in range(pts) for z in range(mem)]
        fetched = passed_on(lax.ppermute(rounded, ("pts", "mem"), pairs))
        same = jnp.stack([fetched] + [xor_permute(fetched, "mem", mem, k) for k in range(1, mem)])
        place = jnp.stack([me, plane])
    else:
        same = jnp.stack([rounded] + [xor_permute(rounded, "pts", pts, 2 * k) for k in far])
        place = jnp.stack([me, jnp.zeros_like(me)])
    field = (same, xor_permute(same, "pts", pts, 1))

    split = ensemble.reshape(pts, members // pts, levels, width)
    groups = [lax.all_to_all(split, "pts", split_axis=0, concat_axis=0, tiled=True)]
    weighted = cov_sum(groups, place, field) * obs_weight

    rounded = weighted.astype(BF)
    same = jnp.stack([rounded] + [xor_permute(rounded, "pts", pts, 2 * k) for k in far])
    place = jnp.stack([me, jnp.zeros_like(me)])
    applied = cov_sum(groups, place, (same, xor_permute(same, "pts", pts, 1)))
    return weighted, applied


def solution(mesh):
    return jax.shard_map(
        per_device,
        mesh=mesh,
        in_specs=(P("mem", None, "pts"), P(None, "pts"), P(None, "pts"), P(), P(), P()),
        out_specs=(P(None, "pts"), P(None, "pts")),
        check_vma=False,
    )
```

time: 435 us -> 107 us (0.25)
  matrix products: 119 us -> 0 us
  local copies, waits for them, and re-layouts: 112 us -> 1.48 us
  waiting for transfers between devices: 120 us -> 45.4 us
  other arithmetic: 31.4 us -> 4.11 us
  starting transfers between devices: 13.4 us -> 38.5 us
  blocking collectives: 20.9 us -> 0 us
  Pallas kernels: 0 us -> 16.2 us
  between operations: 14.2 us -> 0.83 us
    dot_general x26 -> x0, matrix products: 119 us -> none  [the longest x24 115 us: add_slot(): jnp.einsum('rnk,lk->rnl', picked, kernel, preferred_element_type=jnp.floa...]
    psum x2 -> x0, waiting for transfers between devices: 68.8 us -> none  [member_total(): summed = lax.psum(member_terms, 'mem')]
    gather x24 -> x0, local copies, waits for them, and re-layouts: 61 us -> none  [add_slot(): picked = jnp.take(flattened, chosen, axis=1)]
    all_to_all x3 -> x1, waiting for transfers between devices: 50.8 us -> 3.38 us  [per_device(): lax.all_to_all(split, 'pts', split_axis=0, concat_axis=0, tiled=True)]
    ppermute x0 -> x21, waiting for transfers between devices: none -> 42 us  [the longest x20 42 us: xor_permute(): return lax.ppermute(x, axis, [(i, i ^ k) for i in range(size)])]
    ppermute x0 -> x21, starting transfers between devices: none -> 33.3 us  [the longest x20 32.6 us: xor_permute(): return lax.ppermute(x, axis, [(i, i ^ k) for i in range(size)])]
    convert_element_type x6 -> x0, local copies, waits for them, and re-layouts: 26.5 us -> none  [the longest x4 18.8 us: cov_local(): level_local.astype(jnp.float32)]
    all_to_all x2 -> x0, blocking collectives: 20.9 us -> none  [cov_local(): lax.all_to_all(level_sums, 'pts', split_axis=1, concat_axis=0, tiled=True)]
  transfers between devices with their start and end apart: 5 -> 22, of which waited for: 4 -> 18; matrix products, arithmetic and copies ran while one was open for 28% -> 1% of each run, Pallas kernels for 0% -> 9%
where the time goes in v2:
time: 107 us
  waiting for transfers between devices  45.4 us (42%)
  starting transfers between devices  38.5 us (36%)
  Pallas kernels  16.2 us (15%)
  other arithmetic  4.11 us (4%)
  local copies, waits for them, and re-layouts  1.48 us (1%)
    ppermute x20, waiting for transfers between devices, xor_permute(): return lax.ppermute(x, axis, [(i, i ^ k) for i in range(size)])  42 us
    ppermute x20, starting transfers between devices, xor_permute(): return lax.ppermute(x, axis, [(i, i ^ k) for i in range(size)])  32.6 us
    pallas_call x6, Pallas kernels, call(): pl.pallas_call(functools.partial(kernel, layout, field is not None, out_d...  14.6 us
    all_to_all x1, starting transfers between devices, per_device(): lax.all_to_all(split, 'pts', split_axis=0, concat_axis=0, tiled=True)  5.18 us
    all_to_all x1, waiting for transfers between devices, per_device(): lax.all_to_all(split, 'pts', split_axis=0, concat_axis=0, tiled=True)  3.38 us
  transfers between devices with their start and end apart: 22, of which 18 were waited for; matrix products, arithmetic and copies ran while one was open for 1% of the time, Pallas kernels for 9%

profile of v2, /device:TPU:0, one launch (start us, length us, event | category | flops | bytes accessed | tf_op | source)
XLA Modules:
  0.0 106.5 jit_solution(201033584608212447)
XLA Ops:
  0.6 1.0 convert_element_type.94
  1.6 0.7 collective-permute-start
  2.3 5.2 %all-to-all-start = ((bf16[8,2,128,512]{3,2,1,0:T(8,128)(2,1)}), bf16[8,2,128,512]{3,2,1,0:T(8,128)(2,1)S(1)}, u32[]{:S(2)}, u32[]{:S(2)}) async-start(bf16[8,2,128,512]{3,2,1,0:T(8,128)(2,1)} %bitcast.46), calls=%async_computation | async-start | bytes 4194304 | tf_op jit(solution)/shard_map/all_to_all | solution.py:181
  7.5 0.0 copy-start.3
  7.5 0.0 collective-permute-done.x_ref
  7.5 0.0 copy-start.5
  7.5 0.6 copy-done.5
  8.1 1.6 %shard_map.77 = bf16[128,512]{1,0:T(8,128)(2,1)} custom-call(bf16[128,512]{1,0:T(8,128)(2,1)} %copy-done.5), custom_call_target="tpu_custom_call" | custom-call | flops 49999998976 | tf_op jit(solution)/shard_map/pallas_call | solution.py:114
  9.7 7.2 %collective-permute-start.3 = (bf16[128,512]{1,0:T(8,128)(2,1)}, bf16[128,512]{1,0:T(8,128)(2,1)S(1)}, u32[]{:S(2)}, u32[]{:S(2)}) collective-permute-start(bf16[128,512]{1,0:T(8,128)(2,1)} %shard_map.77), channel_id=1, source_target_pairs={{0,3},{1,2},{2,1},{3,0},{4,7},{5,6},{6,5},{7,4},{8,11},{9,10},{10,... | collective-permute-start | bytes 393224 | tf_op jit(solution)/shard_map/ppermute | solution.py:20
  16.9 0.6 collective-permute-start.1
  17.5 4.1 %collective-permute-done.3 = bf16[128,512]{1,0:T(8,128)(2,1)S(1)} collective-permute-done((bf16[128,512]{1,0:T(8,128)(2,1)}, bf16[128,512]{1,0:T(8,128)(2,1)S(1)}, u32[]{:S(2)}, u32[]{:S(2)}) %collective-permute-start.3) | collective-permute-done | bytes 131104 | tf_op jit(solution)/shard_map/ppermute | solution.py:20
  21.6 6.2 %collective-permute-done.2 = bf16[128,512]{1,0:T(8,128)(2,1)S(1)} collective-permute-done((bf16[128,512]{1,0:T(8,128)(2,1)}, bf16[128,512]{1,0:T(8,128)(2,1)S(1)}, u32[]{:S(2)}, u32[]{:S(2)}) %collective-permute-start.2) | collective-permute-done | bytes 131104 | tf_op jit(solution)/shard_map/ppermute | solution.py:20
  27.8 0.0 collective-permute-done.1
  27.8 1.0 pad_maximum_fusion.refs_5_
  28.8 0.1 collective-permute-start.4
  28.8 0.1 pad_add_fusion.refs_0_
  28.9 1.8 %collective-permute-done.4.refs_6_ = bf16[4,128,512]{2,1,0:T(8,128)(2,1)S(1)} collective-permute-done((bf16[4,128,512]{2,1,0:T(8,128)(2,1)S(1)}, bf16[4,128,512]{2,1,0:T(8,128)(2,1)S(1)}, u32[]{:S(2)}, u32[]{:S(2)}) %collective-permute-start.4) | collective-permute-done | bytes 524320 | tf_op jit(solution)/shard_map/ppermute | solution.py:20
  30.7 3.4 %all-to-all-done.refs_2_ = bf16[8,2,128,512]{3,2,1,0:T(8,128)(2,1)S(1)} async-done(((bf16[8,2,128,512]{3,2,1,0:T(8,128)(2,1)}), bf16[8,2,128,512]{3,2,1,0:T(8,128)(2,1)S(1)}, u32[]{:S(2)}, u32[]{:S(2)}) %all-to-all-start) | async-done | bytes 2097184 | tf_op jit(solution)/shard_map/all_to_all | solution.py:181
  34.1 0.8 copy-done.1
  34.9 3.5 %shard_map.78 = (bf16[4,128,512]{2,1,0:T(8,128)(2,1)S(1)}, bf16[32,128,256]{2,1,0:T(8,128)(2,1)S(1)}) custom-call(s32[2]{0:T(128)S(1)} %pad_add_fusion.refs_0_, s32[12,32]{1,0:T(8,128)S(1)} %bitcast.40, bf16[8,2,128,512]{3,2,1,0:T(8,128)(2,1)S(1)} %all-to-all-done.refs_2_, bf16[128,128]{1,0:T(8,128)(2,1)S(1)} %copy-done.1, ...), custom_call_target="tpu_custom_call" | custom-call | flops 6442450944 | tf_op jit(solution)/shard_map/pallas_call | solution.py:136
  38.4 0.1 collective-permute-start.5
  38.5 2.3 %shard_map.79 = bf16[3,128,512]{2,1,0:T(8,128)(2,1)S(1)} custom-call(s32[2]{0:T(128)S(1)} %pad_add_fusion.refs_0_, s32[12,32]{1,0:T(8,128)S(1)} %bitcast.41, bf16[8,2,128,512]{3,2,1,0:T(8,128)(2,1)S(1)} %all-to-all-done.refs_2_, bf16[128,128]{1,0:T(8,128)(2,1)S(1)} %copy-done.2, bf16[12,128,128]{2,1,0:T(8,128)(2,1)S(1)} %copy-done, ...), custom_call_target="tpu_custom_call" | custom-call | flops 4831838208 | tf_op jit(solution)/shard_map/pallas_call | solution.py:136
  40.8 0.0 collective-permute-done.5
  40.9 0.1 add_convert_fusion.1
  41.0 0.6 collective-permute-start.6
  41.6 1.5 %collective-permute-start.8 = (bf16[128,512]{1,0:T(8,128)(2,1)S(1)}, bf16[128,512]{1,0:T(8,128)(2,1)S(1)}, u32[]{:S(2)}, u32[]{:S(2)}) collective-permute-start(bf16[128,512]{1,0:T(8,128)(2,1)S(1)} %get-tuple-element.20), channel_id=1, source_target_pairs={{0,24},{4,28},{8,16},{12,20},{16,8},{20,12},{24,0},{28,4},{1,25},{... | collective-permute-start | bytes 393224 | tf_op jit(solution)/shard_map/ppermute | solution.py:20
  43.1 1.5 %collective-permute-start.7 = (bf16[128,512]{1,0:T(8,128)(2,1)S(1)}, bf16[128,512]{1,0:T(8,128)(2,1)S(1)}, u32[]{:S(2)}, u32[]{:S(2)}) collective-permute-start(bf16[128,512]{1,0:T(8,128)(2,1)S(1)} %get-tuple-element.21), channel_id=1, source_target_pairs={{0,16},{4,20},{8,24},{12,28},{16,0},{20,4},{24,8},{28,12},{1,17},{... | collective-permute-start | bytes 393224 | tf_op jit(solution)/shard_map/ppermute | solution.py:20
  44.6 1.5 %shard_map.80 = bf16[1,128,512]{2,1,0:T(8,128)(2,1)S(1)} custom-call(s32[2]{0:T(128)S(1)} %pad_add_fusion.refs_0_, s32[12,32]{1,0:T(8,128)S(1)} %bitcast.42, bf16[8,2,128,512]{3,2,1,0:T(8,128)(2,1)S(1)} %all-to-all-done.refs_2_, bf16[128,128]{1,0:T(8,128)(2,1)S(1)} %copy-done.2, bf16[12,128,128]{2,1,0:T(8,128)(2,1)S(1)} %copy-done, ...), custom_call_target="tpu_custom_call" | custom-call | flops 1610612736 | tf_op jit(solution)/shard_map/pallas_call | solution.py:136
  46.0 1.3 %collective-permute-done.6 = bf16[128,512]{1,0:T(8,128)(2,1)S(1)} collective-permute-done((bf16[128,512]{1,0:T(8,128)(2,1)S(1)}, bf16[128,512]{1,0:T(8,128)(2,1)S(1)}, u32[]{:S(2)}, u32[]{:S(2)}) %collective-permute-start.6) | collective-permute-done | bytes 131104 | tf_op jit(solution)/shard_map/ppermute | solution.py:20
  47.4 2.5 %collective-permute-done.8 = bf16[128,512]{1,0:T(8,128)(2,1)S(1)} collective-permute-done((bf16[128,512]{1,0:T(8,128)(2,1)S(1)}, bf16[128,512]{1,0:T(8,128)(2,1)S(1)}, u32[]{:S(2)}, u32[]{:S(2)}) %collective-permute-start.8) | collective-permute-done | bytes 131104 | tf_op jit(solution)/shard_map/ppermute | solution.py:20
  49.9 1.4 %collective-permute-done.7 = bf16[128,512]{1,0:T(8,128)(2,1)S(1)} collective-permute-done((bf16[128,512]{1,0:T(8,128)(2,1)S(1)}, bf16[128,512]{1,0:T(8,128)(2,1)S(1)}, u32[]{:S(2)}, u32[]{:S(2)}) %collective-permute-start.7) | collective-permute-done | bytes 131104 | tf_op jit(solution)/shard_map/ppermute | solution.py:20
  51.2 0.1 fusion.5
  51.3 4.2 %collective-permute-start.9 = (bf16[128,512]{1,0:T(8,128)(2,1)S(1)}, bf16[128,512]{1,0:T(8,128)(2,1)S(1)}, u32[]{:S(2)}, u32[]{:S(2)}) collective-permute-start(bf16[128,512]{1,0:T(8,128)(2,1)S(1)} %fusion.5), channel_id=1, source_target_pairs={{0,1},{1,0},{2,3},{3,2},{4,5},{5,4},{6,7},{7,6},{8,9},{9,8},{10,11... | collective-permute-start | bytes 393224 | tf_op jit(solution)/shard_map/ppermute | solution.py:20
  55.5 2.9 %collective-permute-done.9 = bf16[128,512]{1,0:T(8,128)(2,1)S(1)} collective-permute-done((bf16[128,512]{1,0:T(8,128)(2,1)S(1)}, bf16[128,512]{1,0:T(8,128)(2,1)S(1)}, u32[]{:S(2)}, u32[]{:S(2)}) %collective-permute-start.9) | collective-permute-done | bytes 131104 | tf_op jit(solution)/shard_map/ppermute | solution.py:20
  58.5 5.1 %collective-permute-start.10 = (bf16[128,512]{1,0:T(8,128)(2,1)S(1)}, bf16[128,512]{1,0:T(8,128)(2,1)S(1)}, u32[]{:S(2)}, u32[]{:S(2)}) collective-permute-start(bf16[128,512]{1,0:T(8,128)(2,1)S(1)} %add_convert_fusion.3), channel_id=1, source_target_pairs={{0,3},{1,2},{2,1},{3,0},{4,7},{5,6},{6,5},{7,4},{8,11},{9,10},{10,... | collective-permute-start | bytes 393224 | tf_op jit(solution)/shard_map/ppermute | solution.py:20
  63.5 3.1 %collective-permute-done.10 = bf16[128,512]{1,0:T(8,128)(2,1)S(1)} collective-permute-done((bf16[128,512]{1,0:T(8,128)(2,1)S(1)}, bf16[128,512]{1,0:T(8,128)(2,1)S(1)}, u32[]{:S(2)}, u32[]{:S(2)}) %collective-permute-start.10) | collective-permute-done | bytes 131104 | tf_op jit(solution)/shard_map/ppermute | solution.py:20
  66.6 0.8 fusion.6
  67.4 1.4 %collective-permute-start.13 = (bf16[128,512]{1,0:T(8,128)(2,1)S(1)}, bf16[128,512]{1,0:T(8,128)(2,1)S(1)}, u32[]{:S(2)}, u32[]{:S(2)}) collective-permute-start(bf16[128,512]{1,0:T(8,128)(2,1)S(1)} %get-tuple-element.14), channel_id=1, source_target_pairs={{0,24},{4,28},{8,16},{12,20},{16,8},{20,12},{24,0},{28,4},{1,25},{... | collective-permute-start | bytes 393224 | tf_op jit(solution)/shard_map/ppermute | solution.py:20
  68.8 0.6 collective-permute-start.12
  69.4 1.4 %collective-permute-start.11 = (bf16[128,512]{1,0:T(8,128)(2,1)S(1)}, bf16[128,512]{1,0:T(8,128)(2,1)S(1)}, u32[]{:S(2)}, u32[]{:S(2)}) collective-permute-start(bf16[128,512]{1,0:T(8,128)(2,1)S(1)} %get-tuple-element.14), channel_id=1, source_target_pairs={{0,8},{4,12},{8,0},{12,4},{16,24},{20,28},{24,16},{28,20},{1,9},{5... | collective-permute-start | bytes 393224 | tf_op jit(solution)/shard_map/ppermute | solution.py:20
  70.8 2.5 %collective-permute-done.13 = bf16[128,512]{1,0:T(8,128)(2,1)S(1)} collective-permute-done((bf16[128,512]{1,0:T(8,128)(2,1)S(1)}, bf16[128,512]{1,0:T(8,128)(2,1)S(1)}, u32[]{:S(2)}, u32[]{:S(2)}) %collective-permute-start.13) | collective-permute-done | bytes 131104 | tf_op jit(solution)/shard_map/ppermute | solution.py:20
  73.3 1.3 %collective-permute-done.12 = bf16[128,512]{1,0:T(8,128)(2,1)S(1)} collective-permute-done((bf16[128,512]{1,0:T(8,128)(2,1)S(1)}, bf16[128,512]{1,0:T(8,128)(2,1)S(1)}, u32[]{:S(2)}, u32[]{:S(2)}) %collective-permute-start.12) | collective-permute-done | bytes 131104 | tf_op jit(solution)/shard_map/ppermute | solution.py:20
  74.6 0.1 collective-permute-done.11
  74.7 0.1 pad_maximum_fusion.1.refs_5_
  74.8 0.1 collective-permute-start.14
  74.8 0.1 pad_add_fusion.1.refs_0_
  74.9 1.8 %collective-permute-done.14.refs_6_ = bf16[4,128,512]{2,1,0:T(8,128)(2,1)S(1)} collective-permute-done((bf16[4,128,512]{2,1,0:T(8,128)(2,1)S(1)}, bf16[4,128,512]{2,1,0:T(8,128)(2,1)S(1)}, u32[]{:S(2)}, u32[]{:S(2)}) %collective-permute-start.14) | collective-permute-done | bytes 524320 | tf_op jit(solution)/shard_map/ppermute | solution.py:20
  76.7 3.6 %shard_map.81 = (bf16[4,128,512]{2,1,0:T(8,128)(2,1)S(1)}, bf16[32,128,256]{2,1,0:T(8,128)(2,1)S(1)}) custom-call(s32[2]{0:T(128)S(1)} %pad_add_fusion.1.refs_0_, s32[12,32]{1,0:T(8,128)S(1)} %bitcast.43, bf16[8,2,128,512]{3,2,1,0:T(8,128)(2,1)S(1)} %all-to-all-done.refs_2_, bf16[128,128]{1,0:T(8,128)(2,1)S(1)} %copy-done.2, ...), custom_call_target="tpu_custom_call" | custom-call | flops 6442450944 | tf_op jit(solution)/shard_map/pallas_call | solution.py:136
  80.3 0.2 collective-permute-start.15
  80.5 2.3 %shard_map.82 = bf16[3,128,512]{2,1,0:T(8,128)(2,1)S(1)} custom-call(s32[2]{0:T(128)S(1)} %pad_add_fusion.1.refs_0_, s32[12,32]{1,0:T(8,128)S(1)} %bitcast.44, bf16[8,2,128,512]{3,2,1,0:T(8,128)(2,1)S(1)} %all-to-all-done.refs_2_, bf16[128,128]{1,0:T(8,128)(2,1)S(1)} %copy-done.2, bf16[12,128,128]{2,1,0:T(8,128)(2,1)S(1)} %copy-done, ...), custom_call_target="tpu_custom_call" | custom-call | flops 4831838208 | tf_op jit(solution)/shard_map/pallas_call | solution.py:136
  82.8 0.1 add_convert_fusion
  83.0 1.2 %collective-permute-start.16 = (bf16[128,512]{1,0:T(8,128)(2,1)S(1)}, bf16[128,512]{1,0:T(8,128)(2,1)S(1)}, u32[]{:S(2)}, u32[]{:S(2)}) collective-permute-start(bf16[128,512]{1,0:T(8,128)(2,1)S(1)} %get-tuple-element.16), channel_id=1, source_target_pairs={{0,8},{4,12},{8,0},{12,4},{16,24},{20,28},{24,16},{28,20},{1,9},{5... | collective-permute-start | bytes 393224 | tf_op jit(solution)/shard_map/ppermute | solution.py:20
  84.2 1.5 %collective-permute-start.18 = (bf16[128,512]{1,0:T(8,128)(2,1)S(1)}, bf16[128,512]{1,0:T(8,128)(2,1)S(1)}, u32[]{:S(2)}, u32[]{:S(2)}) collective-permute-start(bf16[128,512]{1,0:T(8,128)(2,1)S(1)} %get-tuple-element.17), channel_id=1, source_target_pairs={{0,24},{4,28},{8,16},{12,20},{16,8},{20,12},{24,0},{28,4},{1,25},{... | collective-permute-start | bytes 393224 | tf_op jit(solution)/shard_map/ppermute | solution.py:20
  85.6 0.9 collective-permute-start.17
  86.6 1.5 %shard_map.83 = bf16[1,128,512]{2,1,0:T(8,128)(2,1)S(1)} custom-call(s32[2]{0:T(128)S(1)} %pad_add_fusion.1.refs_0_, s32[12,32]{1,0:T(8,128)S(1)} %bitcast.45, bf16[8,2,128,512]{3,2,1,0:T(8,128)(2,1)S(1)} %all-to-all-done.refs_2_, bf16[128,128]{1,0:T(8,128)(2,1)S(1)} %copy-done.2, bf16[12,128,128]{2,1,0:T(8,128)(2,1)S(1)} %copy-done, ...), custom_call_target="tpu_custom_call" | custom-call | flops 1610612736 | tf_op jit(solution)/shard_map/pallas_call | solution.py:136
  88.0 1.4 %collective-permute-done.16 = bf16[128,512]{1,0:T(8,128)(2,1)S(1)} collective-permute-done((bf16[128,512]{1,0:T(8,128)(2,1)S(1)}, bf16[128,512]{1,0:T(8,128)(2,1)S(1)}, u32[]{:S(2)}, u32[]{:S(2)}) %collective-permute-start.16) | collective-permute-done | bytes 131104 | tf_op jit(solution)/shard_map/ppermute | solution.py:20
  89.4 2.9 %collective-permute-done.18 = bf16[128,512]{1,0:T(8,128)(2,1)S(1)} collective-permute-done((bf16[128,512]{1,0:T(8,128)(2,1)S(1)}, bf16[128,512]{1,0:T(8,128)(2,1)S(1)}, u32[]{:S(2)}, u32[]{:S(2)}) %collective-permute-start.18) | collective-permute-done | bytes 131104 | tf_op jit(solution)/shard_map/ppermute | solution.py:20
  92.3 1.4 %collective-permute-done.17 = bf16[128,512]{1,0:T(8,128)(2,1)S(1)} collective-permute-done((bf16[128,512]{1,0:T(8,128)(2,1)S(1)}, bf16[128,512]{1,0:T(8,128)(2,1)S(1)}, u32[]{:S(2)}, u32[]{:S(2)}) %collective-permute-start.17) | collective-permute-done | bytes 131104 | tf_op jit(solution)/shard_map/ppermute | solution.py:20
  93.7 0.1 fusion.2
  93.8 0.8 collective-permute-start.19
  94.6 4.2 %collective-permute-done.19 = bf16[128,512]{1,0:T(8,128)(2,1)S(1)} collective-permute-done((bf16[128,512]{1,0:T(8,128)(2,1)S(1)}, bf16[128,512]{1,0:T(8,128)(2,1)S(1)}, u32[]{:S(2)}, u32[]{:S(2)}) %collective-permute-start.19) | collective-permute-done | bytes 131104 | tf_op jit(solution)/shard_map/ppermute | solution.py:20
  98.8 3.8 %collective-permute-start.20 = (bf16[128,512]{1,0:T(8,128)(2,1)S(1)}, bf16[128,512]{1,0:T(8,128)(2,1)S(1)}, u32[]{:S(2)}, u32[]{:S(2)}) collective-permute-start(bf16[128,512]{1,0:T(8,128)(2,1)S(1)} %add_convert_fusion.2), channel_id=1, source_target_pairs={{0,3},{1,2},{2,1},{3,0},{4,7},{5,6},{6,5},{7,4},{8,11},{9,10},{10,... | collective-permute-start | bytes 393224 | tf_op jit(solution)/shard_map/ppermute | solution.py:20
  102.6 3.2 %collective-permute-done.20 = bf16[128,512]{1,0:T(8,128)(2,1)S(1)} collective-permute-done((bf16[128,512]{1,0:T(8,128)(2,1)S(1)}, bf16[128,512]{1,0:T(8,128)(2,1)S(1)}, u32[]{:S(2)}, u32[]{:S(2)}) %collective-permute-start.20) | collective-permute-done | bytes 131104 | tf_op jit(solution)/shard_map/ppermute | solution.py:20
  105.8 0.7 convert_add_fusion
  (14 shorter events, 0.1 us)
Async XLA Ops:
  1.6 5.9 %collective-permute-start = (bf16[128,512]{1,0:T(8,128)(2,1)S(1)}, bf16[128,512]{1,0:T(8,128)(2,1)S(1)}, u32[]{:S(2)}, u32[]{:S(2)}) collective-permute-start(bf16[128,512]{1,0:T(8,128)(2,1)S(1)} %convert_element_type.94), channel_id=1, source_target_pairs={{0,0},{1,9},{2,18},{3,27},{4,4},{5,13},{6,22},{7,31},{8,8},{9,1},{... | collective-permute-start | bytes 393224 | tf_op jit(solution)/shard_map/ppermute | solution.py:172
  2.3 31.8 %all-to-all-start = ((bf16[8,2,128,512]{3,2,1,0:T(8,128)(2,1)}), bf16[8,2,128,512]{3,2,1,0:T(8,128)(2,1)S(1)}, u32[]{:S(2)}, u32[]{:S(2)}) async-start(bf16[8,2,128,512]{3,2,1,0:T(8,128)(2,1)} %bitcast.46), calls=%async_computation | async-start | bytes 4194304 | tf_op jit(solution)/shard_map/all_to_all | solution.py:181
  7.5 26.6 %copy-start = (bf16[12,128,128]{2,1,0:T(8,128)(2,1)S(1)}, bf16[12,128,128]{2,1,0:T(8,128)(2,1)}, u32[]{:S(2)}) copy-start(bf16[12,128,128]{2,1,0:T(8,128)(2,1)} %refs_4_.11) | copy-start | bytes 1179652
  7.5 26.6 %copy-start.3 = (s32[32,12]{0,1:T(8,128)S(1)}, s32[32,12]{0,1:T(8,128)}, u32[]{:S(2)}) copy-start(s32[32,12]{0,1:T(8,128)} %param.11) | copy-start | bytes 4612
  7.5 0.7 copy-start.5
  9.7 11.8 %collective-permute-start.3 = (bf16[128,512]{1,0:T(8,128)(2,1)}, bf16[128,512]{1,0:T(8,128)(2,1)S(1)}, u32[]{:S(2)}, u32[]{:S(2)}) collective-permute-start(bf16[128,512]{1,0:T(8,128)(2,1)} %shard_map.77), channel_id=1, source_target_pairs={{0,3},{1,2},{2,1},{3,0},{4,7},{5,6},{6,5},{7,4},{8,11},{9,10},{10,... | collective-permute-start | bytes 393224 | tf_op jit(solution)/shard_map/ppermute | solution.py:20
  16.9 10.9 %collective-permute-start.2 = (bf16[128,512]{1,0:T(8,128)(2,1)}, bf16[128,512]{1,0:T(8,128)(2,1)S(1)}, u32[]{:S(2)}, u32[]{:S(2)}) collective-permute-start(bf16[128,512]{1,0:T(8,128)(2,1)} %shard_map.77), channel_id=1, source_target_pairs={{0,2},{1,3},{2,0},{3,1},{4,6},{5,7},{6,4},{7,5},{8,10},{9,11},{10,... | collective-permute-start | bytes 393224 | tf_op jit(solution)/shard_map/ppermute | solution.py:20
  16.9 10.9 %collective-permute-start.1 = (bf16[128,512]{1,0:T(8,128)(2,1)}, bf16[128,512]{1,0:T(8,128)(2,1)S(1)}, u32[]{:S(2)}, u32[]{:S(2)}) collective-permute-start(bf16[128,512]{1,0:T(8,128)(2,1)} %shard_map.77), channel_id=1, source_target_pairs={{0,1},{1,0},{2,3},{3,2},{4,5},{5,4},{6,7},{7,6},{8,9},{9,8},{10,11... | collective-permute-start | bytes 393224 | tf_op jit(solution)/shard_map/ppermute | solution.py:20
  28.8 2.0 %collective-permute-start.4 = (bf16[4,128,512]{2,1,0:T(8,128)(2,1)S(1)}, bf16[4,128,512]{2,1,0:T(8,128)(2,1)S(1)}, u32[]{:S(2)}, u32[]{:S(2)}) collective-permute-start(bf16[4,128,512]{2,1,0:T(8,128)(2,1)S(1)} %pad_maximum_fusion.refs_5_), channel_id=1, source_target_pairs={{0,4},{4,0},{8,12},{12,8},{16,20},{20,16},{24,28},{28,24},{1,5},{5... | collective-permute-start | bytes 1572872 | tf_op jit(solution)/shard_map/ppermute | solution.py:20
  34.1 0.8 copy-start.1
  34.9 3.6 %copy-start.2 = (bf16[128,128]{1,0:T(8,128)(2,1)S(1)}, bf16[128,128]{1,0:T(8,128)(2,1)}, u32[]{:S(2)}) copy-start(bf16[128,128]{1,0:T(8,128)(2,1)} %refs_3_.11) | copy-start | bytes 98308
  38.4 2.4 %collective-permute-start.5 = (bf16[4,128,512]{2,1,0:T(8,128)(2,1)S(1)}, bf16[4,128,512]{2,1,0:T(8,128)(2,1)S(1)}, u32[]{:S(2)}, u32[]{:S(2)}) collective-permute-start(bf16[4,128,512]{2,1,0:T(8,128)(2,1)S(1)} %get-tuple-element.9), channel_id=1, source_target_pairs={{0,4},{4,0},{8,12},{12,8},{16,20},{20,16},{24,28},{28,24},{1,5},{5... | collective-permute-start | bytes 1572872 | tf_op jit(solution)/shard_map/ppermute | solution.py:20
  41.0 6.4 %collective-permute-start.6 = (bf16[128,512]{1,0:T(8,128)(2,1)S(1)}, bf16[128,512]{1,0:T(8,128)(2,1)S(1)}, u32[]{:S(2)}, u32[]{:S(2)}) collective-permute-start(bf16[128,512]{1,0:T(8,128)(2,1)S(1)} %get-tuple-element.19), channel_id=1, source_target_pairs={{0,8},{4,12},{8,0},{12,4},{16,24},{20,28},{24,16},{28,20},{1,9},{5... | collective-permute-start | bytes 393224 | tf_op jit(solution)/shard_map/ppermute | solution.py:20
  41.6 8.2 %collective-permute-start.8 = (bf16[128,512]{1,0:T(8,128)(2,1)S(1)}, bf16[128,512]{1,0:T(8,128)(2,1)S(1)}, u32[]{:S(2)}, u32[]{:S(2)}) collective-permute-start(bf16[128,512]{1,0:T(8,128)(2,1)S(1)} %get-tuple-element.20), channel_id=1, source_target_pairs={{0,24},{4,28},{8,16},{12,20},{16,8},{20,12},{24,0},{28,4},{1,25},{... | collective-permute-start | bytes 393224 | tf_op jit(solution)/shard_map/ppermute | solution.py:20
  43.1 23.5 %copy-start.4 = (f32[128,512]{1,0:T(8,128)S(1)}, f32[128,512]{1,0:T(8,128)}, u32[]{:S(2)}) copy-start(f32[128,512]{1,0:T(8,128)} %param.8) | copy-start | bytes 786436
  43.1 8.1 %collective-permute-start.7 = (bf16[128,512]{1,0:T(8,128)(2,1)S(1)}, bf16[128,512]{1,0:T(8,128)(2,1)S(1)}, u32[]{:S(2)}, u32[]{:S(2)}) collective-permute-start(bf16[128,512]{1,0:T(8,128)(2,1)S(1)} %get-tuple-element.21), channel_id=1, source_target_pairs={{0,16},{4,20},{8,24},{12,28},{16,0},{20,4},{24,8},{28,12},{1,17},{... | collective-permute-start | bytes 393224 | tf_op jit(solution)/shard_map/ppermute | solution.py:20
  51.3 7.1 %collective-permute-start.9 = (bf16[128,512]{1,0:T(8,128)(2,1)S(1)}, bf16[128,512]{1,0:T(8,128)(2,1)S(1)}, u32[]{:S(2)}, u32[]{:S(2)}) collective-permute-start(bf16[128,512]{1,0:T(8,128)(2,1)S(1)} %fusion.5), channel_id=1, source_target_pairs={{0,1},{1,0},{2,3},{3,2},{4,5},{5,4},{6,7},{7,6},{8,9},{9,8},{10,11... | collective-permute-start | bytes 393224 | tf_op jit(solution)/shard_map/ppermute | solution.py:20
  58.5 8.1 %collective-permute-start.10 = (bf16[128,512]{1,0:T(8,128)(2,1)S(1)}, bf16[128,512]{1,0:T(8,128)(2,1)S(1)}, u32[]{:S(2)}, u32[]{:S(2)}) collective-permute-start(bf16[128,512]{1,0:T(8,128)(2,1)S(1)} %add_convert_fusion.3), channel_id=1, source_target_pairs={{0,3},{1,2},{2,1},{3,0},{4,7},{5,6},{6,5},{7,4},{8,11},{9,10},{10,... | collective-permute-start | bytes 393224 | tf_op jit(solution)/shard_map/ppermute | solution.py:20
  67.4 6.0 %collective-permute-start.13 = (bf16[128,512]{1,0:T(8,128)(2,1)S(1)}, bf16[128,512]{1,0:T(8,128)(2,1)S(1)}, u32[]{:S(2)}, u32[]{:S(2)}) collective-permute-start(bf16[128,512]{1,0:T(8,128)(2,1)S(1)} %get-tuple-element.14), channel_id=1, source_target_pairs={{0,24},{4,28},{8,16},{12,20},{16,8},{20,12},{24,0},{28,4},{1,25},{... | collective-permute-start | bytes 393224 | tf_op jit(solution)/shard_map/ppermute | solution.py:20
  68.8 5.8 %collective-permute-start.12 = (bf16[128,512]{1,0:T(8,128)(2,1)S(1)}, bf16[128,512]{1,0:T(8,128)(2,1)S(1)}, u32[]{:S(2)}, u32[]{:S(2)}) collective-permute-start(bf16[128,512]{1,0:T(8,128)(2,1)S(1)} %get-tuple-element.14), channel_id=1, source_target_pairs={{0,16},{4,20},{8,24},{12,28},{16,0},{20,4},{24,8},{28,12},{1,17},{... | collective-permute-start | bytes 393224 | tf_op jit(solution)/shard_map/ppermute | solution.py:20
  69.4 5.3 %collective-permute-start.11 = (bf16[128,512]{1,0:T(8,128)(2,1)S(1)}, bf16[128,512]{1,0:T(8,128)(2,1)S(1)}, u32[]{:S(2)}, u32[]{:S(2)}) collective-permute-start(bf16[128,512]{1,0:T(8,128)(2,1)S(1)} %get-tuple-element.14), channel_id=1, source_target_pairs={{0,8},{4,12},{8,0},{12,4},{16,24},{20,28},{24,16},{28,20},{1,9},{5... | collective-permute-start | bytes 393224 | tf_op jit(solution)/shard_map/ppermute | solution.py:20
  74.8 2.0 %collective-permute-start.14 = (bf16[4,128,512]{2,1,0:T(8,128)(2,1)S(1)}, bf16[4,128,512]{2,1,0:T(8,128)(2,1)S(1)}, u32[]{:S(2)}, u32[]{:S(2)}) collective-permute-start(bf16[4,128,512]{2,1,0:T(8,128)(2,1)S(1)} %pad_maximum_fusion.1.refs_5_), channel_id=1, source_target_pairs={{0,4},{4,0},{8,12},{12,8},{16,20},{20,16},{24,28},{28,24},{1,5},{5... | collective-permute-start | bytes 1572872 | tf_op jit(solution)/shard_map/ppermute | solution.py:20
  80.3 2.5 %collective-permute-start.15 = (bf16[4,128,512]{2,1,0:T(8,128)(2,1)S(1)}, bf16[4,128,512]{2,1,0:T(8,128)(2,1)S(1)}, u32[]{:S(2)}, u32[]{:S(2)}) collective-permute-start(bf16[4,128,512]{2,1,0:T(8,128)(2,1)S(1)} %get-tuple-element.12), channel_id=1, source_target_pairs={{0,4},{4,0},{8,12},{12,8},{16,20},{20,16},{24,28},{28,24},{1,5},{5... | collective-permute-start | bytes 1572872 | tf_op jit(solution)/shard_map/ppermute | solution.py:20
  83.0 6.4 %collective-permute-start.16 = (bf16[128,512]{1,0:T(8,128)(2,1)S(1)}, bf16[128,512]{1,0:T(8,128)(2,1)S(1)}, u32[]{:S(2)}, u32[]{:S(2)}) collective-permute-start(bf16[128,512]{1,0:T(8,128)(2,1)S(1)} %get-tuple-element.16), channel_id=1, source_target_pairs={{0,8},{4,12},{8,0},{12,4},{16,24},{20,28},{24,16},{28,20},{1,9},{5... | collective-permute-start | bytes 393224 | tf_op jit(solution)/shard_map/ppermute | solution.py:20
  84.2 8.1 %collective-permute-start.18 = (bf16[128,512]{1,0:T(8,128)(2,1)S(1)}, bf16[128,512]{1,0:T(8,128)(2,1)S(1)}, u32[]{:S(2)}, u32[]{:S(2)}) collective-permute-start(bf16[128,512]{1,0:T(8,128)(2,1)S(1)} %get-tuple-element.17), channel_id=1, source_target_pairs={{0,24},{4,28},{8,16},{12,20},{16,8},{20,12},{24,0},{28,4},{1,25},{... | collective-permute-start | bytes 393224 | tf_op jit(solution)/shard_map/ppermute | solution.py:20
  85.6 8.0 %collective-permute-start.17 = (bf16[128,512]{1,0:T(8,128)(2,1)S(1)}, bf16[128,512]{1,0:T(8,128)(2,1)S(1)}, u32[]{:S(2)}, u32[]{:S(2)}) collective-permute-start(bf16[128,512]{1,0:T(8,128)(2,1)S(1)} %get-tuple-element.18), channel_id=1, source_target_pairs={{0,16},{4,20},{8,24},{12,28},{16,0},{20,4},{24,8},{28,12},{1,17},{... | collective-permute-start | bytes 393224 | tf_op jit(solution)/shard_map/ppermute | solution.py:20
  93.8 5.0 %collective-permute-start.19 = (bf16[128,512]{1,0:T(8,128)(2,1)S(1)}, bf16[128,512]{1,0:T(8,128)(2,1)S(1)}, u32[]{:S(2)}, u32[]{:S(2)}) collective-permute-start(bf16[128,512]{1,0:T(8,128)(2,1)S(1)} %fusion.2), channel_id=1, source_target_pairs={{0,1},{1,0},{2,3},{3,2},{4,5},{5,4},{6,7},{7,6},{8,9},{9,8},{10,11... | collective-permute-start | bytes 393224 | tf_op jit(solution)/shard_map/ppermute | solution.py:20
  98.8 6.9 %collective-permute-start.20 = (bf16[128,512]{1,0:T(8,128)(2,1)S(1)}, bf16[128,512]{1,0:T(8,128)(2,1)S(1)}, u32[]{:S(2)}, u32[]{:S(2)}) collective-permute-start(bf16[128,512]{1,0:T(8,128)(2,1)S(1)} %add_convert_fusion.2), channel_id=1, source_target_pairs={{0,3},{1,2},{2,1},{3,0},{4,7},{5,6},{6,5},{7,4},{8,11},{9,10},{10,... | collective-permute-start | bytes 393224 | tf_op jit(solution)/shard_map/ppermute | solution.py:20

commit v3 on v0

v3 whole, which is shorter than its diff:
```python
import functools

import jax
import jax.numpy as jnp
from jax import lax
from jax.experimental import pallas as pl
from jax.experimental.pallas import tpu as pltpu
from jax.sharding import PartitionSpec as P

BF = jnp.bfloat16
F32 = jnp.float32
VMEM = pl.BlockSpec(memory_space=pltpu.VMEM)
ANY = pl.BlockSpec(memory_space=pl.ANY)
PARAMS = pltpu.CompilerParams(vmem_limit_bytes=24 * 2**20)
COLUMNS = 4096
HOLD = 50 * 10**9


def products(me, turn, core, ens_ref, field_ref, prod_ref):
    _, members, levels, width = ens_ref.shape
    blk = prod_ref.shape[1]
    per = width // blk
    for k in range(field_ref.shape[0]):
        share = me ^ (2 * k + core)
        f = field_ref[k ^ turn]
        for m in range(members):
            product = (ens_ref[share, m] * f).T
            for j in range(per):
                prod_ref[share * per + j, :, m * levels:(m + 1) * levels] = product[j * blk:(j + 1) * blk]


def local_sums(shares, cols_ref, ens_ref, mat_ref, prod_ref, out_ref):
    _, members, levels, width = ens_ref.shape
    slots, blk = cols_ref.shape[0], prod_ref.shape[1]
    per = width // blk
    table = jnp.concatenate([mat_ref[s * blk:(s + 1) * blk, :blk] for s in range(slots)], axis=1)
    vertical = mat_ref[slots * blk:, :levels]
    batch = max(1, COLUMNS // (per * members * levels))
    for start in range(0, len(shares), batch):
        chosen = shares[start:start + batch]
        picked = []
        for share in chosen:
            for j in range(per):
                row = share * per + j
                picked.append(jnp.concatenate([prod_ref[cols_ref[s, row]] for s in range(slots)], axis=0))
        horiz = jnp.dot(table, jnp.concatenate(picked, axis=1), preferred_element_type=F32).astype(BF)
        for c, share in enumerate(chosen):
            total = None
            for m in range(members):
                parts = []
                for j in range(per):
                    at = ((c * per + j) * members + m) * levels
                    parts.append(horiz[:, at:at + levels])
                local = lax.dot_general(
                    vertical, jnp.concatenate(parts, axis=0), (((1,), (1,)), ((), ())),
                    preferred_element_type=F32,
                )
                term = ens_ref[share, m].astype(F32) * local
                total = term if total is None else total + term
            out_ref[start + c] = total.astype(BF)


def sums_kernel(cores, turned, wanted, *refs):
    refs = list(refs)
    cols_ref, copied = refs[-2:]
    copy = pltpu.make_async_copy(refs.pop(0), cols_ref, copied)
    copy.start()
    me = lax.axis_index("pts")
    ens_ref, mat_ref = refs.pop(0), refs.pop(0)
    field_refs = [refs.pop(0) for _ in cores]
    prod_ref = refs.pop(0) if len(cores) < 2 else None
    outs = [refs.pop(0) for _ in wanted]
    if cores:
        prod_ref = refs.pop(0)
        turn = lax.axis_index("mem") if turned else 0
        for core, field_ref in zip(cores, field_refs):
            products(me, turn, core, ens_ref, field_ref, prod_ref)
    copy.wait()
    for out_ref, (core, chips) in zip(outs, wanted):
        shares = [me ^ (2 * k + core) for k in chips]
        local_sums(shares, cols_ref, ens_ref, mat_ref, prod_ref, out_ref)


def products_kernel(ens_ref, field_ref, prod_ref):
    products(lax.axis_index("pts"), 0, 0, ens_ref, field_ref, prod_ref)


def copy_kernel(x_ref, out_ref):
    out_ref[...] = x_ref[...]


def passed_on(x):
    return pl.pallas_call(
        copy_kernel, out_shape=jax.ShapeDtypeStruct(x.shape, x.dtype), in_specs=[VMEM], out_specs=VMEM,
        compiler_params=PARAMS, cost_estimate=pl.CostEstimate(flops=HOLD, bytes_accessed=0, transcendentals=0),
    )(x)


def per_device(ensemble, increment, obs_weight, vertical, block_table, block_cols):
    pts, mem = lax.axis_size("pts"), lax.axis_size("mem")
    chips = pts // 2
    members, levels, width = ensemble.shape
    slots, blk, _ = block_table.shape
    share = members // pts
    cols = block_cols.T
    far = list(range(1, chips))
    wide = max(blk, levels)
    matrices = jnp.concatenate([
        jnp.pad(block_table.reshape(slots * blk, blk), ((0, 0), (0, wide - blk))),
        jnp.pad(vertical, ((0, 0), (0, wide - levels))),
    ])
    prod_shape = jax.ShapeDtypeStruct((pts * width // blk, blk, share * levels), BF)

    def xor_permute(x, axis, k):
        return lax.ppermute(x, axis, [(i, i ^ k) for i in range(lax.axis_size(axis))])

    def to_mate(x):
        return xor_permute(x, "pts", 1)

    def cost(shares):
        flops = 8 * slots * blk * width * share * levels * shares
        return pl.CostEstimate(flops=flops, bytes_accessed=0, transcendentals=0)

    def local(turned, wanted, prod=None, fields=()):
        args = [cols, ens, matrices] + list(fields) + ([] if prod is None else [prod])
        outs = [jax.ShapeDtypeStruct((len(some), levels, width), BF) for _, some in wanted]
        cores = (1,) if len(fields) == 1 else tuple(range(len(fields)))
        return pl.pallas_call(
            functools.partial(sums_kernel, cores, turned, wanted),
            out_shape=outs + ([prod_shape] if fields else []),
            in_specs=[ANY] + [VMEM] * (len(args) - 1),
            out_specs=[VMEM] * (len(outs) + bool(fields)),
            scratch_shapes=[pltpu.SMEM(cols.shape, jnp.int32), pltpu.SemaphoreType.DMA],
            input_output_aliases={len(args) - 1: len(outs)} if len(fields) == 1 else {},
            compiler_params=PARAMS,
            cost_estimate=cost(sum(len(some) for _, some in wanted)),
        )(*args)

    def early_products(field):
        return pl.pallas_call(
            products_kernel, out_shape=prod_shape, in_specs=[VMEM] * 2, out_specs=VMEM, compiler_params=PARAMS,
            cost_estimate=cost(1),
        )(ens, field)

    def sum_over_mem(total):
        step = 1
        while step < mem:
            rounded = total.astype(BF)
            total = rounded.astype(F32) + xor_permute(rounded, "mem", 2 * step - 1).astype(F32)
            step *= 2
        return total

    def cov_sum(turned, fields, prod=None):
        mate, prod = local(turned, [(1, far + [0])], prod=prod, fields=fields)
        got = to_mate(mate)
        (own,) = local(turned, [(0, far)], prod=prod)
        chip = (own.astype(F32) + got[:-1].astype(F32)).astype(BF)
        arrived = [xor_permute(chip[i], "pts", 2 * k) for i, k in reversed(list(enumerate(far)))]
        prod, _ = lax.optimization_barrier((prod, chip))
        (own,) = local(turned, [(0, [0])], prod=prod)
        total = own[0].astype(F32) + got[-1].astype(F32)
        for a in arrived:
            total = total + a.astype(F32)
        return sum_over_mem(total)

    rounded = increment.astype(BF)
    turned = chips == mem
    if turned:
        pairs = [(p * mem + z, (p ^ (2 * z)) * mem + z) for p in range(pts) for z in range(mem)]
        fetched = passed_on(lax.ppermute(rounded, ("pts", "mem"), pairs))
        same = jnp.stack([fetched] + [xor_permute(fetched, "mem", k) for k in range(1, mem)])
    else:
        same = jnp.stack([rounded] + [xor_permute(rounded, "pts", 2 * k) for k in range(1, chips)])

    same, matrices = lax.optimization_barrier((same, matrices))
    ens = lax.all_to_all(
        ensemble.reshape(pts, share, levels, width), "pts", split_axis=0, concat_axis=0, tiled=True
    )
    first_sum = cov_sum(turned, (same, to_mate(same)))

    rounded = (first_sum * obs_weight).astype(BF)
    same = jnp.stack([rounded] + [xor_permute(rounded, "pts", 2 * k) for k in range(1, chips)])
    prod = early_products(same)
    first_sum, prod = lax.optimization_barrier((first_sum, prod))
    weighted = first_sum * obs_weight
    applied = cov_sum(False, (to_mate(same),), prod)
    return weighted, applied


def solution(mesh):
    return jax.shard_map(
        per_device,
        mesh=mesh,
        in_specs=(P("mem", None, "pts"), P(None, "pts"), P(None, "pts"), P(), P(), P()),
        out_specs=(P(None, "pts"), P(None, "pts")),
        check_vma=False,
    )
```

time: 435 us -> 105 us (0.24)
  matrix products: 119 us -> 0 us
  local copies, waits for them, and re-layouts: 112 us -> 1.91 us
  waiting for transfers between devices: 120 us -> 45.9 us
  other arithmetic: 31.4 us -> 3.1 us
  starting transfers between devices: 13.4 us -> 39.5 us
  blocking collectives: 20.9 us -> 0 us
  Pallas kernels: 0 us -> 13.5 us
  between operations: 14.2 us -> 0.85 us
    dot_general x26 -> x0, matrix products: 119 us -> none  [the longest x24 115 us: add_slot(): jnp.einsum('rnk,lk->rnl', picked, kernel, preferred_element_type=jnp.floa...]
    psum x2 -> x0, waiting for transfers between devices: 68.8 us -> none  [member_total(): summed = lax.psum(member_terms, 'mem')]
    gather x24 -> x0, local copies, waits for them, and re-layouts: 61 us -> none  [add_slot(): picked = jnp.take(flattened, chosen, axis=1)]
    all_to_all x3 -> x1, waiting for transfers between devices: 50.8 us -> 5.83 us  [per_device(): lax.all_to_all(ensemble.reshape(pts, share, levels, width), 'pts', split_...]
    ppermute x0 -> x21, waiting for transfers between devices: none -> 40.1 us  [the longest x20 40.1 us: xor_permute(): lax.ppermute(x, axis, [(i, i ^ k) for i in range(lax.axis_size(axis))])]
    ppermute x0 -> x21, starting transfers between devices: none -> 34.3 us  [the longest x20 33.7 us: xor_permute(): lax.ppermute(x, axis, [(i, i ^ k) for i in range(lax.axis_size(axis))])]
    convert_element_type x6 -> x0, local copies, waits for them, and re-layouts: 26.5 us -> none  [the longest x4 18.8 us: cov_local(): level_local.astype(jnp.float32)]
    all_to_all x2 -> x0, blocking collectives: 20.9 us -> none  [cov_local(): lax.all_to_all(level_sums, 'pts', split_axis=1, concat_axis=0, tiled=True)]
  transfers between devices with their start and end apart: 5 -> 22, of which waited for: 4 -> 17; matrix products, arithmetic and copies ran while one was open for 28% -> 1% of each run, Pallas kernels for 0% -> 7%
where the time goes in v3:
time: 105 us
  waiting for transfers between devices  45.9 us (44%)
  starting transfers between devices  39.5 us (38%)
  Pallas kernels  13.5 us (13%)
  other arithmetic  3.1 us (3%)
  local copies, waits for them, and re-layouts  1.91 us (2%)
    ppermute x20, waiting for transfers between devices, xor_permute(): lax.ppermute(x, axis, [(i, i ^ k) for i in range(lax.axis_size(axis))])  40.1 us
    ppermute x20, starting transfers between devices, xor_permute(): lax.ppermute(x, axis, [(i, i ^ k) for i in range(lax.axis_size(axis))])  33.7 us
    pallas_call x6, Pallas kernels, local(): pl.pallas_call(functools.partial(sums_kernel, cores, turned, wanted), out...  13.1 us
    all_to_all x1, waiting for transfers between devices, per_device(): lax.all_to_all(ensemble.reshape(pts, share, levels, width), 'pts', split_...  5.83 us
    all_to_all x1, starting transfers between devices, per_device(): lax.all_to_all(ensemble.reshape(pts, share, levels, width), 'pts', split_...  5.18 us
  transfers between devices with their start and end apart: 22, of which 17 were waited for; matrix products, arithmetic and copies ran while one was open for 1% of the time, Pallas kernels for 7%

profile of v3, /device:TPU:0, one launch (start us, length us, event | category | flops | bytes accessed | tf_op | source)
XLA Modules:
  0.0 104.7 jit_solution(17075934172384375310)
XLA Ops:
  0.6 1.0 convert_element_type.94
  1.6 0.7 collective-permute-start
  2.3 5.2 %all-to-all-start = ((bf16[8,2,128,512]{3,2,1,0:T(8,128)(2,1)}), bf16[8,2,128,512]{3,2,1,0:T(8,128)(2,1)S(1)}, u32[]{:S(2)}, u32[]{:S(2)}) async-start(bf16[8,2,128,512]{3,2,1,0:T(8,128)(2,1)} %bitcast.46), calls=%async_computation | async-start | bytes 4194304 | tf_op jit(solution)/shard_map/all_to_all | solution.py:176
  7.5 0.0 copy-start.5
  7.5 0.0 copy-start.2
  7.5 0.0 collective-permute-done.x_ref
  7.5 7.3 %collective-permute-start.3 = (bf16[128,512]{1,0:T(8,128)(2,1)S(1)}, bf16[128,512]{1,0:T(8,128)(2,1)S(1)}, u32[]{:S(2)}, u32[]{:S(2)}) collective-permute-start(bf16[128,512]{1,0:T(8,128)(2,1)S(1)} %shard_map.77), channel_id=1, source_target_pairs={{0,3},{1,2},{2,1},{3,0},{4,7},{5,6},{6,5},{7,4},{8,11},{9,10},{10,... | collective-permute-start | bytes 393224 | tf_op jit(solution)/shard_map/ppermute | solution.py:115
  14.8 0.0 collective-permute-start.2
  14.8 0.6 collective-permute-start.1
  15.5 3.7 %collective-permute-done.3 = bf16[128,512]{1,0:T(8,128)(2,1)S(1)} collective-permute-done((bf16[128,512]{1,0:T(8,128)(2,1)S(1)}, bf16[128,512]{1,0:T(8,128)(2,1)S(1)}, u32[]{:S(2)}, u32[]{:S(2)}) %collective-permute-start.3) | collective-permute-done | bytes 131104 | tf_op jit(solution)/shard_map/ppermute | solution.py:115
  19.2 6.2 %collective-permute-done.2 = bf16[128,512]{1,0:T(8,128)(2,1)S(1)} collective-permute-done((bf16[128,512]{1,0:T(8,128)(2,1)S(1)}, bf16[128,512]{1,0:T(8,128)(2,1)S(1)}, u32[]{:S(2)}, u32[]{:S(2)}) %collective-permute-start.2) | collective-permute-done | bytes 131104 | tf_op jit(solution)/shard_map/ppermute | solution.py:115
  25.4 0.0 collective-permute-done.1
  25.4 0.1 pad_maximum_fusion.refs_3_
  25.5 0.1 collective-permute-start.4
  25.6 1.9 %collective-permute-done.4.refs_4_ = bf16[4,128,512]{2,1,0:T(8,128)(2,1)S(1)} collective-permute-done((bf16[4,128,512]{2,1,0:T(8,128)(2,1)S(1)}, bf16[4,128,512]{2,1,0:T(8,128)(2,1)S(1)}, u32[]{:S(2)}, u32[]{:S(2)}) %collective-permute-start.4) | collective-permute-done | bytes 524320 | tf_op jit(solution)/shard_map/ppermute | solution.py:115
  27.5 0.8 copy-done
  28.3 5.8 %all-to-all-done.refs_1_.ens_ref = bf16[8,2,128,512]{3,2,1,0:T(8,128)(2,1)S(1)} async-done(((bf16[8,2,128,512]{3,2,1,0:T(8,128)(2,1)}), bf16[8,2,128,512]{3,2,1,0:T(8,128)(2,1)S(1)}, u32[]{:S(2)}, u32[]{:S(2)}) %all-to-all-start) | async-done | bytes 2097184 | tf_op jit(solution)/shard_map/all_to_all | solution.py:176
  34.1 1.0 copy-done.1
  35.2 3.0 %shard_map.78 = (bf16[4,128,512]{2,1,0:T(8,128)(2,1)S(1)}, bf16[32,128,256]{2,1,0:T(8,128)(2,1)S(1)}) custom-call(s32[12,32]{1,0:T(8,128)S(1)} %bitcast.40, bf16[8,2,128,512]{3,2,1,0:T(8,128)(2,1)S(1)} %all-to-all-done.refs_1_.ens_ref, bf16[1664,128]{1,0:T(8,128)(2,1)S(1)} %pad_maximum_fusion.2.refs_2_, bf16[4,128,512]{2,1,0:T(8,128)(2,1)S(1)} %pad_maximum_fusion.refs_3_, ...), custom_call_target="tpu_custom_call" | custom-call | flops 6442450944 | tf_op jit(solution)/shard_map/pallas_call | solution.py:128
  38.1 0.1 collective-permute-start.5
  38.2 2.3 %shard_map.79 = bf16[3,128,512]{2,1,0:T(8,128)(2,1)S(1)} custom-call(s32[12,32]{1,0:T(8,128)S(1)} %bitcast.41, bf16[8,2,128,512]{3,2,1,0:T(8,128)(2,1)S(1)} %all-to-all-done.refs_1_.ens_ref, bf16[1664,128]{1,0:T(8,128)(2,1)S(1)} %pad_maximum_fusion.2.refs_2_, bf16[32,128,256]{2,1,0:T(8,128)(2,1)S(1)} %get-tuple-element.16.refs_3_), custom_call_target="tpu_custom_call" | custom-call | flops 4831838208 | tf_op jit(solution)/shard_map/pallas_call | solution.py:128
  40.5 0.0 collective-permute-done.5
  40.5 0.1 add_convert_fusion.1
  40.6 0.7 collective-permute-start.6
  41.3 1.4 %collective-permute-start.8 = (bf16[128,512]{1,0:T(8,128)(2,1)S(1)}, bf16[128,512]{1,0:T(8,128)(2,1)S(1)}, u32[]{:S(2)}, u32[]{:S(2)}) collective-permute-start(bf16[128,512]{1,0:T(8,128)(2,1)S(1)} %get-tuple-element.26), channel_id=1, source_target_pairs={{0,8},{4,12},{8,0},{12,4},{16,24},{20,28},{24,16},{28,20},{1,9},{5... | collective-permute-start | bytes 393224 | tf_op jit(solution)/shard_map/ppermute | solution.py:115
  42.7 1.5 %collective-permute-start.7 = (bf16[128,512]{1,0:T(8,128)(2,1)S(1)}, bf16[128,512]{1,0:T(8,128)(2,1)S(1)}, u32[]{:S(2)}, u32[]{:S(2)}) collective-permute-start(bf16[128,512]{1,0:T(8,128)(2,1)S(1)} %get-tuple-element.27), channel_id=1, source_target_pairs={{0,16},{4,20},{8,24},{12,28},{16,0},{20,4},{24,8},{28,12},{1,17},{... | collective-permute-start | bytes 393224 | tf_op jit(solution)/shard_map/ppermute | solution.py:115
  44.2 1.4 %shard_map.80 = bf16[1,128,512]{2,1,0:T(8,128)(2,1)S(1)} custom-call(s32[12,32]{1,0:T(8,128)S(1)} %bitcast.42, bf16[8,2,128,512]{3,2,1,0:T(8,128)(2,1)S(1)} %all-to-all-done.refs_1_.ens_ref, bf16[1664,128]{1,0:T(8,128)(2,1)S(1)} %pad_maximum_fusion.2.refs_2_, bf16[32,128,256]{2,1,0:T(8,128)(2,1)S(1)} %get-tuple-element.16.refs_3_), custom_call_target="tpu_custom_call" | custom-call | flops 1610612736 | tf_op jit(solution)/shard_map/pallas_call | solution.py:128
  45.6 2.3 %collective-permute-done.6 = bf16[128,512]{1,0:T(8,128)(2,1)S(1)} collective-permute-done((bf16[128,512]{1,0:T(8,128)(2,1)S(1)}, bf16[128,512]{1,0:T(8,128)(2,1)S(1)}, u32[]{:S(2)}, u32[]{:S(2)}) %collective-permute-start.6) | collective-permute-done | bytes 131104 | tf_op jit(solution)/shard_map/ppermute | solution.py:115
  47.9 1.5 %collective-permute-done.8 = bf16[128,512]{1,0:T(8,128)(2,1)S(1)} collective-permute-done((bf16[128,512]{1,0:T(8,128)(2,1)S(1)}, bf16[128,512]{1,0:T(8,128)(2,1)S(1)}, u32[]{:S(2)}, u32[]{:S(2)}) %collective-permute-start.8) | collective-permute-done | bytes 131104 | tf_op jit(solution)/shard_map/ppermute | solution.py:115
  49.4 0.9 collective-permute-done.7
  50.3 0.1 fusion.5
  50.4 4.2 %collective-permute-start.9 = (bf16[128,512]{1,0:T(8,128)(2,1)S(1)}, bf16[128,512]{1,0:T(8,128)(2,1)S(1)}, u32[]{:S(2)}, u32[]{:S(2)}) collective-permute-start(bf16[128,512]{1,0:T(8,128)(2,1)S(1)} %fusion.5), channel_id=1, source_target_pairs={{0,1},{1,0},{2,3},{3,2},{4,5},{5,4},{6,7},{7,6},{8,9},{9,8},{10,11... | collective-permute-start | bytes 393224 | tf_op jit(solution)/shard_map/ppermute | solution.py:115
  54.6 3.7 %collective-permute-done.9 = bf16[128,512]{1,0:T(8,128)(2,1)S(1)} collective-permute-done((bf16[128,512]{1,0:T(8,128)(2,1)S(1)}, bf16[128,512]{1,0:T(8,128)(2,1)S(1)}, u32[]{:S(2)}, u32[]{:S(2)}) %collective-permute-start.9) | collective-permute-done | bytes 131104 | tf_op jit(solution)/shard_map/ppermute | solution.py:115
  58.3 4.8 %collective-permute-start.10 = (bf16[128,512]{1,0:T(8,128)(2,1)S(1)}, bf16[128,512]{1,0:T(8,128)(2,1)S(1)}, u32[]{:S(2)}, u32[]{:S(2)}) collective-permute-start(bf16[128,512]{1,0:T(8,128)(2,1)S(1)} %add_convert_fusion.3), channel_id=1, source_target_pairs={{0,3},{1,2},{2,1},{3,0},{4,7},{5,6},{6,5},{7,4},{8,11},{9,10},{10,... | collective-permute-start | bytes 393224 | tf_op jit(solution)/shard_map/ppermute | solution.py:115
  63.1 3.0 %collective-permute-done.10 = bf16[128,512]{1,0:T(8,128)(2,1)S(1)} collective-permute-done((bf16[128,512]{1,0:T(8,128)(2,1)S(1)}, bf16[128,512]{1,0:T(8,128)(2,1)S(1)}, u32[]{:S(2)}, u32[]{:S(2)}) %collective-permute-start.10) | collective-permute-done | bytes 131104 | tf_op jit(solution)/shard_map/ppermute | solution.py:115
  66.1 0.7 collective-permute-start.13
  66.8 1.4 %collective-permute-start.12 = (bf16[128,512]{1,0:T(8,128)(2,1)S(1)}, bf16[128,512]{1,0:T(8,128)(2,1)S(1)}, u32[]{:S(2)}, u32[]{:S(2)}) collective-permute-start(bf16[128,512]{1,0:T(8,128)(2,1)S(1)} %get-tuple-element.28), channel_id=1, source_target_pairs={{0,16},{4,20},{8,24},{12,28},{16,0},{20,4},{24,8},{28,12},{1,17},{... | collective-permute-start | bytes 393224 | tf_op jit(solution)/shard_map/ppermute | solution.py:115
  68.2 1.5 %collective-permute-start.11 = (bf16[128,512]{1,0:T(8,128)(2,1)S(1)}, bf16[128,512]{1,0:T(8,128)(2,1)S(1)}, u32[]{:S(2)}, u32[]{:S(2)}) collective-permute-start(bf16[128,512]{1,0:T(8,128)(2,1)S(1)} %get-tuple-element.28), channel_id=1, source_target_pairs={{0,8},{4,12},{8,0},{12,4},{16,24},{20,28},{24,16},{28,20},{1,9},{5... | collective-permute-start | bytes 393224 | tf_op jit(solution)/shard_map/ppermute | solution.py:115
  69.7 2.7 %collective-permute-done.13 = bf16[128,512]{1,0:T(8,128)(2,1)S(1)} collective-permute-done((bf16[128,512]{1,0:T(8,128)(2,1)S(1)}, bf16[128,512]{1,0:T(8,128)(2,1)S(1)}, u32[]{:S(2)}, u32[]{:S(2)}) %collective-permute-start.13) | collective-permute-done | bytes 131104 | tf_op jit(solution)/shard_map/ppermute | solution.py:115
  72.4 0.8 collective-permute-done.12
  73.2 0.0 collective-permute-done.11
  73.2 0.1 pad_maximum_fusion.1.field_ref
  73.2 0.1 collective-permute-start.14
  73.3 0.4 shard_map.81.refs_4_
  73.7 1.5 %collective-permute-done.14.refs_3_ = bf16[4,128,512]{2,1,0:T(8,128)(2,1)S(1)} collective-permute-done((bf16[4,128,512]{2,1,0:T(8,128)(2,1)S(1)}, bf16[4,128,512]{2,1,0:T(8,128)(2,1)S(1)}, u32[]{:S(2)}, u32[]{:S(2)}) %collective-permute-start.14) | collective-permute-done | bytes 524320 | tf_op jit(solution)/shard_map/ppermute | solution.py:115
  75.2 2.8 %shard_map.82 = (bf16[4,128,512]{2,1,0:T(8,128)(2,1)S(1)}, bf16[32,128,256]{2,1,0:T(8,128)(2,1)S(1)}) custom-call(s32[12,32]{1,0:T(8,128)S(1)} %bitcast.43, bf16[8,2,128,512]{3,2,1,0:T(8,128)(2,1)S(1)} %all-to-all-done.refs_1_.ens_ref, bf16[1664,128]{1,0:T(8,128)(2,1)S(1)} %pad_maximum_fusion.2.refs_2_, ...), custom_call_target="tpu_custom_call", output_to_operand_aliasing={{1}: (4, {})} | custom-call | flops 6442450944 | tf_op jit(solution)/shard_map/pallas_call | solution.py:128
  78.0 0.2 collective-permute-start.15
  78.2 2.2 %shard_map.83 = bf16[3,128,512]{2,1,0:T(8,128)(2,1)S(1)} custom-call(s32[12,32]{1,0:T(8,128)S(1)} %bitcast.44, bf16[8,2,128,512]{3,2,1,0:T(8,128)(2,1)S(1)} %all-to-all-done.refs_1_.ens_ref, bf16[1664,128]{1,0:T(8,128)(2,1)S(1)} %pad_maximum_fusion.2.refs_2_, bf16[32,128,256]{2,1,0:T(8,128)(2,1)S(1)} %get-tuple-element.21.refs_3_), custom_call_target="tpu_custom_call" | custom-call | flops 4831838208 | tf_op jit(solution)/shard_map/pallas_call | solution.py:128
  80.5 0.0 collective-permute-done.15
  80.5 0.1 add_convert_fusion
  80.6 1.7 %collective-permute-start.16 = (bf16[128,512]{1,0:T(8,128)(2,1)S(1)}, bf16[128,512]{1,0:T(8,128)(2,1)S(1)}, u32[]{:S(2)}, u32[]{:S(2)}) collective-permute-start(bf16[128,512]{1,0:T(8,128)(2,1)S(1)} %get-tuple-element.22), channel_id=1, source_target_pairs={{0,24},{4,28},{8,16},{12,20},{16,8},{20,12},{24,0},{28,4},{1,25},{... | collective-permute-start | bytes 393224 | tf_op jit(solution)/shard_map/ppermute | solution.py:115
  82.3 1.0 collective-permute-start.18
  83.3 0.9 collective-permute-start.17
  84.2 1.4 %shard_map.84 = bf16[1,128,512]{2,1,0:T(8,128)(2,1)S(1)} custom-call(s32[12,32]{1,0:T(8,128)S(1)} %bitcast.45, bf16[8,2,128,512]{3,2,1,0:T(8,128)(2,1)S(1)} %all-to-all-done.refs_1_.ens_ref, bf16[1664,128]{1,0:T(8,128)(2,1)S(1)} %pad_maximum_fusion.2.refs_2_, bf16[32,128,256]{2,1,0:T(8,128)(2,1)S(1)} %get-tuple-element.21.refs_3_), custom_call_target="tpu_custom_call" | custom-call | flops 1610612736 | tf_op jit(solution)/shard_map/pallas_call | solution.py:128
  85.6 2.3 %collective-permute-done.16 = bf16[128,512]{1,0:T(8,128)(2,1)S(1)} collective-permute-done((bf16[128,512]{1,0:T(8,128)(2,1)S(1)}, bf16[128,512]{1,0:T(8,128)(2,1)S(1)}, u32[]{:S(2)}, u32[]{:S(2)}) %collective-permute-start.16) | collective-permute-done | bytes 131104 | tf_op jit(solution)/shard_map/ppermute | solution.py:115
  87.9 1.9 %collective-permute-done.18 = bf16[128,512]{1,0:T(8,128)(2,1)S(1)} collective-permute-done((bf16[128,512]{1,0:T(8,128)(2,1)S(1)}, bf16[128,512]{1,0:T(8,128)(2,1)S(1)}, u32[]{:S(2)}, u32[]{:S(2)}) %collective-permute-start.18) | collective-permute-done | bytes 131104 | tf_op jit(solution)/shard_map/ppermute | solution.py:115
  89.9 0.3 collective-permute-done.17
  90.2 0.1 fusion.2
  90.3 3.1 %collective-permute-start.19 = (bf16[128,512]{1,0:T(8,128)(2,1)S(1)}, bf16[128,512]{1,0:T(8,128)(2,1)S(1)}, u32[]{:S(2)}, u32[]{:S(2)}) collective-permute-start(bf16[128,512]{1,0:T(8,128)(2,1)S(1)} %fusion.2), channel_id=1, source_target_pairs={{0,1},{1,0},{2,3},{3,2},{4,5},{5,4},{6,7},{7,6},{8,9},{9,8},{10,11... | collective-permute-start | bytes 393224 | tf_op jit(solution)/shard_map/ppermute | solution.py:115
  93.4 3.7 %collective-permute-done.19 = bf16[128,512]{1,0:T(8,128)(2,1)S(1)} collective-permute-done((bf16[128,512]{1,0:T(8,128)(2,1)S(1)}, bf16[128,512]{1,0:T(8,128)(2,1)S(1)}, u32[]{:S(2)}, u32[]{:S(2)}) %collective-permute-start.19) | collective-permute-done | bytes 131104 | tf_op jit(solution)/shard_map/ppermute | solution.py:115
  97.1 2.6 %collective-permute-start.20 = (bf16[128,512]{1,0:T(8,128)(2,1)S(1)}, bf16[128,512]{1,0:T(8,128)(2,1)S(1)}, u32[]{:S(2)}, u32[]{:S(2)}) collective-permute-start(bf16[128,512]{1,0:T(8,128)(2,1)S(1)} %add_convert_fusion.2), channel_id=1, source_target_pairs={{0,3},{1,2},{2,1},{3,0},{4,7},{5,6},{6,5},{7,4},{8,11},{9,10},{10,... | collective-permute-start | bytes 393224 | tf_op jit(solution)/shard_map/ppermute | solution.py:115
  99.7 0.7 mul.7
  100.4 3.6 %collective-permute-done.20 = bf16[128,512]{1,0:T(8,128)(2,1)S(1)} collective-permute-done((bf16[128,512]{1,0:T(8,128)(2,1)S(1)}, bf16[128,512]{1,0:T(8,128)(2,1)S(1)}, u32[]{:S(2)}, u32[]{:S(2)}) %collective-permute-start.20) | collective-permute-done | bytes 131104 | tf_op jit(solution)/shard_map/ppermute | solution.py:115
  104.0 0.7 convert_add_fusion
  (15 shorter events, 0.2 us)
Async XLA Ops:
  1.6 5.9 %collective-permute-start = (bf16[128,512]{1,0:T(8,128)(2,1)S(1)}, bf16[128,512]{1,0:T(8,128)(2,1)S(1)}, u32[]{:S(2)}, u32[]{:S(2)}) collective-permute-start(bf16[128,512]{1,0:T(8,128)(2,1)S(1)} %convert_element_type.94), channel_id=1, source_target_pairs={{0,0},{1,9},{2,18},{3,27},{4,4},{5,13},{6,22},{7,31},{8,8},{9,1},{... | collective-permute-start | bytes 393224 | tf_op jit(solution)/shard_map/ppermute | solution.py:170
  2.3 31.8 %all-to-all-start = ((bf16[8,2,128,512]{3,2,1,0:T(8,128)(2,1)}), bf16[8,2,128,512]{3,2,1,0:T(8,128)(2,1)S(1)}, u32[]{:S(2)}, u32[]{:S(2)}) async-start(bf16[8,2,128,512]{3,2,1,0:T(8,128)(2,1)} %bitcast.46), calls=%async_computation | async-start | bytes 4194304 | tf_op jit(solution)/shard_map/all_to_all | solution.py:176
  7.5 8.0 %copy-start.4 = (bf16[12,128,128]{2,1,0:T(8,128)(2,1)S(1)}, bf16[12,128,128]{2,1,0:T(8,128)(2,1)}, u32[]{:S(2)}) copy-start(bf16[12,128,128]{2,1,0:T(8,128)(2,1)} %param.10) | copy-start | bytes 1179652
  7.5 8.0 %copy-start.5 = (bf16[128,128]{1,0:T(8,128)(2,1)S(1)}, bf16[128,128]{1,0:T(8,128)(2,1)}, u32[]{:S(2)}) copy-start(bf16[128,128]{1,0:T(8,128)(2,1)} %param.9) | copy-start | bytes 98308
  7.5 26.6 %copy-start.2 = (s32[32,12]{0,1:T(8,128)S(1)}, s32[32,12]{0,1:T(8,128)}, u32[]{:S(2)}) copy-start(s32[32,12]{0,1:T(8,128)} %param.11) | copy-start | bytes 4612
  7.5 11.7 %collective-permute-start.3 = (bf16[128,512]{1,0:T(8,128)(2,1)S(1)}, bf16[128,512]{1,0:T(8,128)(2,1)S(1)}, u32[]{:S(2)}, u32[]{:S(2)}) collective-permute-start(bf16[128,512]{1,0:T(8,128)(2,1)S(1)} %shard_map.77), channel_id=1, source_target_pairs={{0,3},{1,2},{2,1},{3,0},{4,7},{5,6},{6,5},{7,4},{8,11},{9,10},{10,... | collective-permute-start | bytes 393224 | tf_op jit(solution)/shard_map/ppermute | solution.py:115
  14.8 10.6 %collective-permute-start.2 = (bf16[128,512]{1,0:T(8,128)(2,1)S(1)}, bf16[128,512]{1,0:T(8,128)(2,1)S(1)}, u32[]{:S(2)}, u32[]{:S(2)}) collective-permute-start(bf16[128,512]{1,0:T(8,128)(2,1)S(1)} %shard_map.77), channel_id=1, source_target_pairs={{0,2},{1,3},{2,0},{3,1},{4,6},{5,7},{6,4},{7,5},{8,10},{9,11},{10,... | collective-permute-start | bytes 393224 | tf_op jit(solution)/shard_map/ppermute | solution.py:115
  14.8 10.6 %collective-permute-start.1 = (bf16[128,512]{1,0:T(8,128)(2,1)S(1)}, bf16[128,512]{1,0:T(8,128)(2,1)S(1)}, u32[]{:S(2)}, u32[]{:S(2)}) collective-permute-start(bf16[128,512]{1,0:T(8,128)(2,1)S(1)} %shard_map.77), channel_id=1, source_target_pairs={{0,1},{1,0},{2,3},{3,2},{4,5},{5,4},{6,7},{7,6},{8,9},{9,8},{10,11... | collective-permute-start | bytes 393224 | tf_op jit(solution)/shard_map/ppermute | solution.py:115
  25.5 2.0 %collective-permute-start.4 = (bf16[4,128,512]{2,1,0:T(8,128)(2,1)S(1)}, bf16[4,128,512]{2,1,0:T(8,128)(2,1)S(1)}, u32[]{:S(2)}, u32[]{:S(2)}) collective-permute-start(bf16[4,128,512]{2,1,0:T(8,128)(2,1)S(1)} %pad_maximum_fusion.refs_3_), channel_id=1, source_target_pairs={{0,4},{4,0},{8,12},{12,8},{16,20},{20,16},{24,28},{28,24},{1,5},{5... | collective-permute-start | bytes 1572872 | tf_op jit(solution)/shard_map/ppermute | solution.py:115
  27.5 0.8 copy-start
  34.1 1.0 copy-start.1
  38.1 2.4 %collective-permute-start.5 = (bf16[4,128,512]{2,1,0:T(8,128)(2,1)S(1)}, bf16[4,128,512]{2,1,0:T(8,128)(2,1)S(1)}, u32[]{:S(2)}, u32[]{:S(2)}) collective-permute-start(bf16[4,128,512]{2,1,0:T(8,128)(2,1)S(1)} %get-tuple-element.15), channel_id=1, source_target_pairs={{0,4},{4,0},{8,12},{12,8},{16,20},{20,16},{24,28},{28,24},{1,5},{5... | collective-permute-start | bytes 1572872 | tf_op jit(solution)/shard_map/ppermute | solution.py:115
  40.6 7.3 %collective-permute-start.6 = (bf16[128,512]{1,0:T(8,128)(2,1)S(1)}, bf16[128,512]{1,0:T(8,128)(2,1)S(1)}, u32[]{:S(2)}, u32[]{:S(2)}) collective-permute-start(bf16[128,512]{1,0:T(8,128)(2,1)S(1)} %get-tuple-element.25), channel_id=1, source_target_pairs={{0,24},{4,28},{8,16},{12,20},{16,8},{20,12},{24,0},{28,4},{1,25},{... | collective-permute-start | bytes 393224 | tf_op jit(solution)/shard_map/ppermute | solution.py:115
  41.3 8.1 %collective-permute-start.8 = (bf16[128,512]{1,0:T(8,128)(2,1)S(1)}, bf16[128,512]{1,0:T(8,128)(2,1)S(1)}, u32[]{:S(2)}, u32[]{:S(2)}) collective-permute-start(bf16[128,512]{1,0:T(8,128)(2,1)S(1)} %get-tuple-element.26), channel_id=1, source_target_pairs={{0,8},{4,12},{8,0},{12,4},{16,24},{20,28},{24,16},{28,20},{1,9},{5... | collective-permute-start | bytes 393224 | tf_op jit(solution)/shard_map/ppermute | solution.py:115
  42.7 23.4 %copy-start.3 = (f32[128,512]{1,0:T(8,128)S(1)}, f32[128,512]{1,0:T(8,128)}, u32[]{:S(2)}) copy-start(f32[128,512]{1,0:T(8,128)} %param.8) | copy-start | bytes 786436
  42.7 7.6 %collective-permute-start.7 = (bf16[128,512]{1,0:T(8,128)(2,1)S(1)}, bf16[128,512]{1,0:T(8,128)(2,1)S(1)}, u32[]{:S(2)}, u32[]{:S(2)}) collective-permute-start(bf16[128,512]{1,0:T(8,128)(2,1)S(1)} %get-tuple-element.27), channel_id=1, source_target_pairs={{0,16},{4,20},{8,24},{12,28},{16,0},{20,4},{24,8},{28,12},{1,17},{... | collective-permute-start | bytes 393224 | tf_op jit(solution)/shard_map/ppermute | solution.py:115
  50.4 7.9 %collective-permute-start.9 = (bf16[128,512]{1,0:T(8,128)(2,1)S(1)}, bf16[128,512]{1,0:T(8,128)(2,1)S(1)}, u32[]{:S(2)}, u32[]{:S(2)}) collective-permute-start(bf16[128,512]{1,0:T(8,128)(2,1)S(1)} %fusion.5), channel_id=1, source_target_pairs={{0,1},{1,0},{2,3},{3,2},{4,5},{5,4},{6,7},{7,6},{8,9},{9,8},{10,11... | collective-permute-start | bytes 393224 | tf_op jit(solution)/shard_map/ppermute | solution.py:115
  58.3 7.8 %collective-permute-start.10 = (bf16[128,512]{1,0:T(8,128)(2,1)S(1)}, bf16[128,512]{1,0:T(8,128)(2,1)S(1)}, u32[]{:S(2)}, u32[]{:S(2)}) collective-permute-start(bf16[128,512]{1,0:T(8,128)(2,1)S(1)} %add_convert_fusion.3), channel_id=1, source_target_pairs={{0,3},{1,2},{2,1},{3,0},{4,7},{5,6},{6,5},{7,4},{8,11},{9,10},{10,... | collective-permute-start | bytes 393224 | tf_op jit(solution)/shard_map/ppermute | solution.py:115
  66.1 6.3 %collective-permute-start.13 = (bf16[128,512]{1,0:T(8,128)(2,1)S(1)}, bf16[128,512]{1,0:T(8,128)(2,1)S(1)}, u32[]{:S(2)}, u32[]{:S(2)}) collective-permute-start(bf16[128,512]{1,0:T(8,128)(2,1)S(1)} %get-tuple-element.28), channel_id=1, source_target_pairs={{0,24},{4,28},{8,16},{12,20},{16,8},{20,12},{24,0},{28,4},{1,25},{... | collective-permute-start | bytes 393224 | tf_op jit(solution)/shard_map/ppermute | solution.py:115
  66.8 6.4 %collective-permute-start.12 = (bf16[128,512]{1,0:T(8,128)(2,1)S(1)}, bf16[128,512]{1,0:T(8,128)(2,1)S(1)}, u32[]{:S(2)}, u32[]{:S(2)}) collective-permute-start(bf16[128,512]{1,0:T(8,128)(2,1)S(1)} %get-tuple-element.28), channel_id=1, source_target_pairs={{0,16},{4,20},{8,24},{12,28},{16,0},{20,4},{24,8},{28,12},{1,17},{... | collective-permute-start | bytes 393224 | tf_op jit(solution)/shard_map/ppermute | solution.py:115
  68.2 5.0 %collective-permute-start.11 = (bf16[128,512]{1,0:T(8,128)(2,1)S(1)}, bf16[128,512]{1,0:T(8,128)(2,1)S(1)}, u32[]{:S(2)}, u32[]{:S(2)}) collective-permute-start(bf16[128,512]{1,0:T(8,128)(2,1)S(1)} %get-tuple-element.28), channel_id=1, source_target_pairs={{0,8},{4,12},{8,0},{12,4},{16,24},{20,28},{24,16},{28,20},{1,9},{5... | collective-permute-start | bytes 393224 | tf_op jit(solution)/shard_map/ppermute | solution.py:115
  73.2 2.0 %collective-permute-start.14 = (bf16[4,128,512]{2,1,0:T(8,128)(2,1)S(1)}, bf16[4,128,512]{2,1,0:T(8,128)(2,1)S(1)}, u32[]{:S(2)}, u32[]{:S(2)}) collective-permute-start(bf16[4,128,512]{2,1,0:T(8,128)(2,1)S(1)} %pad_maximum_fusion.1.field_ref), channel_id=1, source_target_pairs={{0,4},{4,0},{8,12},{12,8},{16,20},{20,16},{24,28},{28,24},{1,5},{5... | collective-permute-start | bytes 1572872 | tf_op jit(solution)/shard_map/ppermute | solution.py:115
  78.0 2.5 %collective-permute-start.15 = (bf16[4,128,512]{2,1,0:T(8,128)(2,1)S(1)}, bf16[4,128,512]{2,1,0:T(8,128)(2,1)S(1)}, u32[]{:S(2)}, u32[]{:S(2)}) collective-permute-start(bf16[4,128,512]{2,1,0:T(8,128)(2,1)S(1)} %get-tuple-element.20), channel_id=1, source_target_pairs={{0,4},{4,0},{8,12},{12,8},{16,20},{20,16},{24,28},{28,24},{1,5},{5... | collective-permute-start | bytes 1572872 | tf_op jit(solution)/shard_map/ppermute | solution.py:115
  80.6 7.3 %collective-permute-start.16 = (bf16[128,512]{1,0:T(8,128)(2,1)S(1)}, bf16[128,512]{1,0:T(8,128)(2,1)S(1)}, u32[]{:S(2)}, u32[]{:S(2)}) collective-permute-start(bf16[128,512]{1,0:T(8,128)(2,1)S(1)} %get-tuple-element.22), channel_id=1, source_target_pairs={{0,24},{4,28},{8,16},{12,20},{16,8},{20,12},{24,0},{28,4},{1,25},{... | collective-permute-start | bytes 393224 | tf_op jit(solution)/shard_map/ppermute | solution.py:115
  82.3 7.5 %collective-permute-start.18 = (bf16[128,512]{1,0:T(8,128)(2,1)S(1)}, bf16[128,512]{1,0:T(8,128)(2,1)S(1)}, u32[]{:S(2)}, u32[]{:S(2)}) collective-permute-start(bf16[128,512]{1,0:T(8,128)(2,1)S(1)} %get-tuple-element.23), channel_id=1, source_target_pairs={{0,8},{4,12},{8,0},{12,4},{16,24},{20,28},{24,16},{28,20},{1,9},{5... | collective-permute-start | bytes 393224 | tf_op jit(solution)/shard_map/ppermute | solution.py:115
  83.3 6.9 %collective-permute-start.17 = (bf16[128,512]{1,0:T(8,128)(2,1)S(1)}, bf16[128,512]{1,0:T(8,128)(2,1)S(1)}, u32[]{:S(2)}, u32[]{:S(2)}) collective-permute-start(bf16[128,512]{1,0:T(8,128)(2,1)S(1)} %get-tuple-element.24), channel_id=1, source_target_pairs={{0,16},{4,20},{8,24},{12,28},{16,0},{20,4},{24,8},{28,12},{1,17},{... | collective-permute-start | bytes 393224 | tf_op jit(solution)/shard_map/ppermute | solution.py:115
  90.3 6.8 %collective-permute-start.19 = (bf16[128,512]{1,0:T(8,128)(2,1)S(1)}, bf16[128,512]{1,0:T(8,128)(2,1)S(1)}, u32[]{:S(2)}, u32[]{:S(2)}) collective-permute-start(bf16[128,512]{1,0:T(8,128)(2,1)S(1)} %fusion.2), channel_id=1, source_target_pairs={{0,1},{1,0},{2,3},{3,2},{4,5},{5,4},{6,7},{7,6},{8,9},{9,8},{10,11... | collective-permute-start | bytes 393224 | tf_op jit(solution)/shard_map/ppermute | solution.py:115
  97.1 6.9 %collective-permute-start.20 = (bf16[128,512]{1,0:T(8,128)(2,1)S(1)}, bf16[128,512]{1,0:T(8,128)(2,1)S(1)}, u32[]{:S(2)}, u32[]{:S(2)}) collective-permute-start(bf16[128,512]{1,0:T(8,128)(2,1)S(1)} %add_convert_fusion.2), channel_id=1, source_target_pairs={{0,3},{1,2},{2,1},{3,0},{4,7},{5,6},{6,5},{7,4},{8,11},{9,10},{10,... | collective-permute-start | bytes 393224 | tf_op jit(solution)/shard_map/ppermute | solution.py:115

commit v4 on v3

--- a/solution.py
+++ b/solution.py
@@ -103,7 +103,7 @@
     slots, blk, _ = block_table.shape
     share = members // pts
     cols = block_cols.T
-    far = list(range(1, chips))
+    far = [k ^ k >> 1 for k in range(1, chips)]
     wide = max(blk, levels)
     matrices = jnp.concatenate([
         jnp.pad(block_table.reshape(slots * blk, blk), ((0, 0), (0, wide - blk))),
@@ -155,7 +155,7 @@
         got = to_mate(mate)
         (own,) = local(turned, [(0, far)], prod=prod)
         chip = (own.astype(F32) + got[:-1].astype(F32)).astype(BF)
-        arrived = [xor_permute(chip[i], "pts", 2 * k) for i, k in reversed(list(enumerate(far)))]
+        arrived = [xor_permute(chip[i], "pts", 2 * k) for i, k in enumerate(far)]
         prod, _ = lax.optimization_barrier((prod, chip))
         (own,) = local(turned, [(0, [0])], prod=prod)
         total = own[0].astype(F32) + got[-1].astype(F32)

time: 105 us -> 103 us (0.981)
  waiting for transfers between devices: 45.9 us -> 43.6 us
    ppermute x20, waiting for transfers between devices: 40.1 us -> 37.8 us  [xor_permute(): lax.ppermute(x, axis, [(i, i ^ k) for i in range(lax.axis_size(axis))])]
  transfers between devices with their start and end apart: 22 -> 22, of which waited for: 17 -> 16; matrix products, arithmetic and copies ran while one was open for 1% -> 1% of each run, Pallas kernels for 7% -> 8%
where the time goes in v4:
time: 103 us
  waiting for transfers between devices  43.6 us (42%)
  starting transfers between devices  39.7 us (39%)
  Pallas kernels  13.5 us (13%)
  other arithmetic  3.1 us (3%)
  local copies, waits for them, and re-layouts  1.91 us (2%)
    ppermute x20, waiting for transfers between devices, xor_permute(): lax.ppermute(x, axis, [(i, i ^ k) for i in range(lax.axis_size(axis))])  37.8 us
    ppermute x20, starting transfers between devices, xor_permute(): lax.ppermute(x, axis, [(i, i ^ k) for i in range(lax.axis_size(axis))])  33.8 us
    pallas_call x6, Pallas kernels, local(): pl.pallas_call(functools.partial(sums_kernel, cores, turned, wanted), out...  13.1 us
    all_to_all x1, waiting for transfers between devices, per_device(): lax.all_to_all(ensemble.reshape(pts, share, levels, width), 'pts', split_...  5.83 us
    all_to_all x1, starting transfers between devices, per_device(): lax.all_to_all(ensemble.reshape(pts, share, levels, width), 'pts', split_...  5.18 us
  transfers between devices with their start and end apart: 22, of which 16 were waited for; matrix products, arithmetic and copies ran while one was open for 1% of the time, Pallas kernels for 8%

profile of v4, /device:TPU:0, one launch (start us, length us, event | category | flops | bytes accessed | tf_op | source)
XLA Modules:
  0.0 102.6 jit_solution(9710265534547726285)
XLA Ops:
  0.6 1.0 convert_element_type.94
  1.6 0.7 collective-permute-start
  2.3 5.2 %all-to-all-start = ((bf16[8,2,128,512]{3,2,1,0:T(8,128)(2,1)}), bf16[8,2,128,512]{3,2,1,0:T(8,128)(2,1)S(1)}, u32[]{:S(2)}, u32[]{:S(2)}) async-start(bf16[8,2,128,512]{3,2,1,0:T(8,128)(2,1)} %bitcast.46), calls=%async_computation | async-start | bytes 4194304 | tf_op jit(solution)/shard_map/all_to_all | solution.py:176
  7.5 0.0 copy-start.5
  7.5 0.0 copy-start.2
  7.5 0.0 collective-permute-done.x_ref
  7.5 7.3 %collective-permute-start.3 = (bf16[128,512]{1,0:T(8,128)(2,1)S(1)}, bf16[128,512]{1,0:T(8,128)(2,1)S(1)}, u32[]{:S(2)}, u32[]{:S(2)}) collective-permute-start(bf16[128,512]{1,0:T(8,128)(2,1)S(1)} %shard_map.77), channel_id=1, source_target_pairs={{0,3},{1,2},{2,1},{3,0},{4,7},{5,6},{6,5},{7,4},{8,11},{9,10},{10,... | collective-permute-start | bytes 393224 | tf_op jit(solution)/shard_map/ppermute | solution.py:115
  14.8 0.0 collective-permute-start.2
  14.8 0.6 collective-permute-start.1
  15.5 3.7 %collective-permute-done.3 = bf16[128,512]{1,0:T(8,128)(2,1)S(1)} collective-permute-done((bf16[128,512]{1,0:T(8,128)(2,1)S(1)}, bf16[128,512]{1,0:T(8,128)(2,1)S(1)}, u32[]{:S(2)}, u32[]{:S(2)}) %collective-permute-start.3) | collective-permute-done | bytes 131104 | tf_op jit(solution)/shard_map/ppermute | solution.py:115
  19.2 6.2 %collective-permute-done.2 = bf16[128,512]{1,0:T(8,128)(2,1)S(1)} collective-permute-done((bf16[128,512]{1,0:T(8,128)(2,1)S(1)}, bf16[128,512]{1,0:T(8,128)(2,1)S(1)}, u32[]{:S(2)}, u32[]{:S(2)}) %collective-permute-start.2) | collective-permute-done | bytes 131104 | tf_op jit(solution)/shard_map/ppermute | solution.py:115
  25.4 0.0 collective-permute-done.1
  25.4 0.1 pad_maximum_fusion.refs_3_
  25.5 0.1 collective-permute-start.4
  25.6 1.9 %collective-permute-done.4.refs_4_ = bf16[4,128,512]{2,1,0:T(8,128)(2,1)S(1)} collective-permute-done((bf16[4,128,512]{2,1,0:T(8,128)(2,1)S(1)}, bf16[4,128,512]{2,1,0:T(8,128)(2,1)S(1)}, u32[]{:S(2)}, u32[]{:S(2)}) %collective-permute-start.4) | collective-permute-done | bytes 524320 | tf_op jit(solution)/shard_map/ppermute | solution.py:115
  27.5 0.8 copy-done
  28.3 5.8 %all-to-all-done.refs_1_.ens_ref = bf16[8,2,128,512]{3,2,1,0:T(8,128)(2,1)S(1)} async-done(((bf16[8,2,128,512]{3,2,1,0:T(8,128)(2,1)}), bf16[8,2,128,512]{3,2,1,0:T(8,128)(2,1)S(1)}, u32[]{:S(2)}, u32[]{:S(2)}) %all-to-all-start) | async-done | bytes 2097184 | tf_op jit(solution)/shard_map/all_to_all | solution.py:176
  34.1 1.0 %copy-done.1 = bf16[4,128,512]{2,1,0:T(8,128)(2,1)S(1)} copy-done((bf16[4,128,512]{2,1,0:T(8,128)(2,1)S(1)}, bf16[4,128,512]{2,1,0:T(8,128)(2,1)}, u32[]{:S(2)}) %copy-start.1) | copy-done | bytes 524312
  35.2 3.0 %shard_map.78 = (bf16[4,128,512]{2,1,0:T(8,128)(2,1)S(1)}, bf16[32,128,256]{2,1,0:T(8,128)(2,1)S(1)}) custom-call(s32[12,32]{1,0:T(8,128)S(1)} %bitcast.40, bf16[8,2,128,512]{3,2,1,0:T(8,128)(2,1)S(1)} %all-to-all-done.refs_1_.ens_ref, bf16[1664,128]{1,0:T(8,128)(2,1)S(1)} %pad_maximum_fusion.2.refs_2_, bf16[4,128,512]{2,1,0:T(8,128)(2,1)S(1)} %pad_maximum_fusion.refs_3_, ...), custom_call_target="tpu_custom_call" | custom-call | flops 6442450944 | tf_op jit(solution)/shard_map/pallas_call | solution.py:128
  38.1 0.1 collective-permute-start.5
  38.2 2.3 %shard_map.79 = bf16[3,128,512]{2,1,0:T(8,128)(2,1)S(1)} custom-call(s32[12,32]{1,0:T(8,128)S(1)} %bitcast.41, bf16[8,2,128,512]{3,2,1,0:T(8,128)(2,1)S(1)} %all-to-all-done.refs_1_.ens_ref, bf16[1664,128]{1,0:T(8,128)(2,1)S(1)} %pad_maximum_fusion.2.refs_2_, bf16[32,128,256]{2,1,0:T(8,128)(2,1)S(1)} %get-tuple-element.16.refs_3_), custom_call_target="tpu_custom_call" | custom-call | flops 4831838208 | tf_op jit(solution)/shard_map/pallas_call | solution.py:128
  40.5 0.0 collective-permute-done.5
  40.5 0.1 add_convert_fusion.1
  40.6 0.6 collective-permute-start.6
  41.3 0.6 collective-permute-start.8
  41.9 2.3 %collective-permute-start.7 = (bf16[128,512]{1,0:T(8,128)(2,1)S(1)}, bf16[128,512]{1,0:T(8,128)(2,1)S(1)}, u32[]{:S(2)}, u32[]{:S(2)}) collective-permute-start(bf16[128,512]{1,0:T(8,128)(2,1)S(1)} %get-tuple-element.27), channel_id=1, source_target_pairs={{0,24},{4,28},{8,16},{12,20},{16,8},{20,12},{24,0},{28,4},{1,25},{... | collective-permute-start | bytes 393224 | tf_op jit(solution)/shard_map/ppermute | solution.py:115
  44.2 1.4 %shard_map.80 = bf16[1,128,512]{2,1,0:T(8,128)(2,1)S(1)} custom-call(s32[12,32]{1,0:T(8,128)S(1)} %bitcast.42, bf16[8,2,128,512]{3,2,1,0:T(8,128)(2,1)S(1)} %all-to-all-done.refs_1_.ens_ref, bf16[1664,128]{1,0:T(8,128)(2,1)S(1)} %pad_maximum_fusion.2.refs_2_, bf16[32,128,256]{2,1,0:T(8,128)(2,1)S(1)} %get-tuple-element.16.refs_3_), custom_call_target="tpu_custom_call" | custom-call | flops 1610612736 | tf_op jit(solution)/shard_map/pallas_call | solution.py:128
  45.6 1.4 %collective-permute-done.6 = bf16[128,512]{1,0:T(8,128)(2,1)S(1)} collective-permute-done((bf16[128,512]{1,0:T(8,128)(2,1)S(1)}, bf16[128,512]{1,0:T(8,128)(2,1)S(1)}, u32[]{:S(2)}, u32[]{:S(2)}) %collective-permute-start.6) | collective-permute-done | bytes 131104 | tf_op jit(solution)/shard_map/ppermute | solution.py:115
  47.0 2.6 %collective-permute-done.8 = bf16[128,512]{1,0:T(8,128)(2,1)S(1)} collective-permute-done((bf16[128,512]{1,0:T(8,128)(2,1)S(1)}, bf16[128,512]{1,0:T(8,128)(2,1)S(1)}, u32[]{:S(2)}, u32[]{:S(2)}) %collective-permute-start.8) | collective-permute-done | bytes 131104 | tf_op jit(solution)/shard_map/ppermute | solution.py:115
  49.6 0.0 collective-permute-done.7
  49.6 0.1 fusion.5
  49.7 4.2 %collective-permute-start.9 = (bf16[128,512]{1,0:T(8,128)(2,1)S(1)}, bf16[128,512]{1,0:T(8,128)(2,1)S(1)}, u32[]{:S(2)}, u32[]{:S(2)}) collective-permute-start(bf16[128,512]{1,0:T(8,128)(2,1)S(1)} %fusion.5), channel_id=1, source_target_pairs={{0,1},{1,0},{2,3},{3,2},{4,5},{5,4},{6,7},{7,6},{8,9},{9,8},{10,11... | collective-permute-start | bytes 393224 | tf_op jit(solution)/shard_map/ppermute | solution.py:115
  53.9 3.2 %collective-permute-done.9 = bf16[128,512]{1,0:T(8,128)(2,1)S(1)} collective-permute-done((bf16[128,512]{1,0:T(8,128)(2,1)S(1)}, bf16[128,512]{1,0:T(8,128)(2,1)S(1)}, u32[]{:S(2)}, u32[]{:S(2)}) %collective-permute-start.9) | collective-permute-done | bytes 131104 | tf_op jit(solution)/shard_map/ppermute | solution.py:115
  57.1 4.8 %collective-permute-start.10 = (bf16[128,512]{1,0:T(8,128)(2,1)S(1)}, bf16[128,512]{1,0:T(8,128)(2,1)S(1)}, u32[]{:S(2)}, u32[]{:S(2)}) collective-permute-start(bf16[128,512]{1,0:T(8,128)(2,1)S(1)} %add_convert_fusion.3), channel_id=1, source_target_pairs={{0,3},{1,2},{2,1},{3,0},{4,7},{5,6},{6,5},{7,4},{8,11},{9,10},{10,... | collective-permute-start | bytes 393224 | tf_op jit(solution)/shard_map/ppermute | solution.py:115
  61.9 3.1 %collective-permute-done.10 = bf16[128,512]{1,0:T(8,128)(2,1)S(1)} collective-permute-done((bf16[128,512]{1,0:T(8,128)(2,1)S(1)}, bf16[128,512]{1,0:T(8,128)(2,1)S(1)}, u32[]{:S(2)}, u32[]{:S(2)}) %collective-permute-start.10) | collective-permute-done | bytes 131104 | tf_op jit(solution)/shard_map/ppermute | solution.py:115
  65.0 1.6 %collective-permute-start.13 = (bf16[128,512]{1,0:T(8,128)(2,1)S(1)}, bf16[128,512]{1,0:T(8,128)(2,1)S(1)}, u32[]{:S(2)}, u32[]{:S(2)}) collective-permute-start(bf16[128,512]{1,0:T(8,128)(2,1)S(1)} %get-tuple-element.28), channel_id=1, source_target_pairs={{0,24},{4,28},{8,16},{12,20},{16,8},{20,12},{24,0},{28,4},{1,25},{... | collective-permute-start | bytes 393224 | tf_op jit(solution)/shard_map/ppermute | solution.py:115
  66.6 1.5 %collective-permute-start.12 = (bf16[128,512]{1,0:T(8,128)(2,1)S(1)}, bf16[128,512]{1,0:T(8,128)(2,1)S(1)}, u32[]{:S(2)}, u32[]{:S(2)}) collective-permute-start(bf16[128,512]{1,0:T(8,128)(2,1)S(1)} %get-tuple-element.28), channel_id=1, source_target_pairs={{0,16},{4,20},{8,24},{12,28},{16,0},{20,4},{24,8},{28,12},{1,17},{... | collective-permute-start | bytes 393224 | tf_op jit(solution)/shard_map/ppermute | solution.py:115
  68.1 0.5 collective-permute-start.11
  68.6 2.5 %collective-permute-done.13 = bf16[128,512]{1,0:T(8,128)(2,1)S(1)} collective-permute-done((bf16[128,512]{1,0:T(8,128)(2,1)S(1)}, bf16[128,512]{1,0:T(8,128)(2,1)S(1)}, u32[]{:S(2)}, u32[]{:S(2)}) %collective-permute-start.13) | collective-permute-done | bytes 131104 | tf_op jit(solution)/shard_map/ppermute | solution.py:115
  71.1 1.3 %collective-permute-done.12 = bf16[128,512]{1,0:T(8,128)(2,1)S(1)} collective-permute-done((bf16[128,512]{1,0:T(8,128)(2,1)S(1)}, bf16[128,512]{1,0:T(8,128)(2,1)S(1)}, u32[]{:S(2)}, u32[]{:S(2)}) %collective-permute-start.12) | collective-permute-done | bytes 131104 | tf_op jit(solution)/shard_map/ppermute | solution.py:115
  72.4 0.7 collective-permute-done.11
  73.1 0.1 pad_maximum_fusion.1.field_ref
  73.1 0.1 collective-permute-start.14
  73.2 0.4 shard_map.81.refs_4_
  73.6 1.5 %collective-permute-done.14.refs_3_ = bf16[4,128,512]{2,1,0:T(8,128)(2,1)S(1)} collective-permute-done((bf16[4,128,512]{2,1,0:T(8,128)(2,1)S(1)}, bf16[4,128,512]{2,1,0:T(8,128)(2,1)S(1)}, u32[]{:S(2)}, u32[]{:S(2)}) %collective-permute-start.14) | collective-permute-done | bytes 524320 | tf_op jit(solution)/shard_map/ppermute | solution.py:115
  75.1 2.8 %shard_map.82 = (bf16[4,128,512]{2,1,0:T(8,128)(2,1)S(1)}, bf16[32,128,256]{2,1,0:T(8,128)(2,1)S(1)}) custom-call(s32[12,32]{1,0:T(8,128)S(1)} %bitcast.43, bf16[8,2,128,512]{3,2,1,0:T(8,128)(2,1)S(1)} %all-to-all-done.refs_1_.ens_ref, bf16[1664,128]{1,0:T(8,128)(2,1)S(1)} %pad_maximum_fusion.2.refs_2_, ...), custom_call_target="tpu_custom_call", output_to_operand_aliasing={{1}: (4, {})} | custom-call | flops 6442450944 | tf_op jit(solution)/shard_map/pallas_call | solution.py:128
  77.9 0.2 collective-permute-start.15
  78.1 2.3 %shard_map.83 = bf16[3,128,512]{2,1,0:T(8,128)(2,1)S(1)} custom-call(s32[12,32]{1,0:T(8,128)S(1)} %bitcast.44, bf16[8,2,128,512]{3,2,1,0:T(8,128)(2,1)S(1)} %all-to-all-done.refs_1_.ens_ref, bf16[1664,128]{1,0:T(8,128)(2,1)S(1)} %pad_maximum_fusion.2.refs_2_, bf16[32,128,256]{2,1,0:T(8,128)(2,1)S(1)} %get-tuple-element.21.refs_3_), custom_call_target="tpu_custom_call" | custom-call | flops 4831838208 | tf_op jit(solution)/shard_map/pallas_call | solution.py:128
  80.4 0.0 collective-permute-done.15
  80.4 0.1 add_convert_fusion
  80.6 0.9 collective-permute-start.16
  81.5 1.0 collective-permute-start.18
  82.5 1.7 %collective-permute-start.17 = (bf16[128,512]{1,0:T(8,128)(2,1)S(1)}, bf16[128,512]{1,0:T(8,128)(2,1)S(1)}, u32[]{:S(2)}, u32[]{:S(2)}) collective-permute-start(bf16[128,512]{1,0:T(8,128)(2,1)S(1)} %get-tuple-element.24), channel_id=1, source_target_pairs={{0,24},{4,28},{8,16},{12,20},{16,8},{20,12},{24,0},{28,4},{1,25},{... | collective-permute-start | bytes 393224 | tf_op jit(solution)/shard_map/ppermute | solution.py:115
  84.1 1.4 %shard_map.84 = bf16[1,128,512]{2,1,0:T(8,128)(2,1)S(1)} custom-call(s32[12,32]{1,0:T(8,128)S(1)} %bitcast.45, bf16[8,2,128,512]{3,2,1,0:T(8,128)(2,1)S(1)} %all-to-all-done.refs_1_.ens_ref, bf16[1664,128]{1,0:T(8,128)(2,1)S(1)} %pad_maximum_fusion.2.refs_2_, bf16[32,128,256]{2,1,0:T(8,128)(2,1)S(1)} %get-tuple-element.21.refs_3_), custom_call_target="tpu_custom_call" | custom-call | flops 1610612736 | tf_op jit(solution)/shard_map/pallas_call | solution.py:128
  85.5 1.4 %collective-permute-done.16 = bf16[128,512]{1,0:T(8,128)(2,1)S(1)} collective-permute-done((bf16[128,512]{1,0:T(8,128)(2,1)S(1)}, bf16[128,512]{1,0:T(8,128)(2,1)S(1)}, u32[]{:S(2)}, u32[]{:S(2)}) %collective-permute-start.16) | collective-permute-done | bytes 131104 | tf_op jit(solution)/shard_map/ppermute | solution.py:115
  87.0 2.8 %collective-permute-done.18 = bf16[128,512]{1,0:T(8,128)(2,1)S(1)} collective-permute-done((bf16[128,512]{1,0:T(8,128)(2,1)S(1)}, bf16[128,512]{1,0:T(8,128)(2,1)S(1)}, u32[]{:S(2)}, u32[]{:S(2)}) %collective-permute-start.18) | collective-permute-done | bytes 131104 | tf_op jit(solution)/shard_map/ppermute | solution.py:115
  89.8 0.0 collective-permute-done.17
  89.8 0.1 fusion.2
  89.9 1.9 %collective-permute-start.19 = (bf16[128,512]{1,0:T(8,128)(2,1)S(1)}, bf16[128,512]{1,0:T(8,128)(2,1)S(1)}, u32[]{:S(2)}, u32[]{:S(2)}) collective-permute-start(bf16[128,512]{1,0:T(8,128)(2,1)S(1)} %fusion.2), channel_id=1, source_target_pairs={{0,1},{1,0},{2,3},{3,2},{4,5},{5,4},{6,7},{7,6},{8,9},{9,8},{10,11... | collective-permute-start | bytes 393224 | tf_op jit(solution)/shard_map/ppermute | solution.py:115
  91.8 3.1 %collective-permute-done.19 = bf16[128,512]{1,0:T(8,128)(2,1)S(1)} collective-permute-done((bf16[128,512]{1,0:T(8,128)(2,1)S(1)}, bf16[128,512]{1,0:T(8,128)(2,1)S(1)}, u32[]{:S(2)}, u32[]{:S(2)}) %collective-permute-start.19) | collective-permute-done | bytes 131104 | tf_op jit(solution)/shard_map/ppermute | solution.py:115
  94.9 3.9 %collective-permute-start.20 = (bf16[128,512]{1,0:T(8,128)(2,1)S(1)}, bf16[128,512]{1,0:T(8,128)(2,1)S(1)}, u32[]{:S(2)}, u32[]{:S(2)}) collective-permute-start(bf16[128,512]{1,0:T(8,128)(2,1)S(1)} %add_convert_fusion.2), channel_id=1, source_target_pairs={{0,3},{1,2},{2,1},{3,0},{4,7},{5,6},{6,5},{7,4},{8,11},{9,10},{10,... | collective-permute-start | bytes 393224 | tf_op jit(solution)/shard_map/ppermute | solution.py:115
  98.8 0.7 mul.7
  99.5 2.3 %collective-permute-done.20 = bf16[128,512]{1,0:T(8,128)(2,1)S(1)} collective-permute-done((bf16[128,512]{1,0:T(8,128)(2,1)S(1)}, bf16[128,512]{1,0:T(8,128)(2,1)S(1)}, u32[]{:S(2)}, u32[]{:S(2)}) %collective-permute-start.20) | collective-permute-done | bytes 131104 | tf_op jit(solution)/shard_map/ppermute | solution.py:115
  101.9 0.7 convert_add_fusion
  (15 shorter events, 0.2 us)
Async XLA Ops:
  1.6 5.9 %collective-permute-start = (bf16[128,512]{1,0:T(8,128)(2,1)S(1)}, bf16[128,512]{1,0:T(8,128)(2,1)S(1)}, u32[]{:S(2)}, u32[]{:S(2)}) collective-permute-start(bf16[128,512]{1,0:T(8,128)(2,1)S(1)} %convert_element_type.94), channel_id=1, source_target_pairs={{0,0},{1,9},{2,18},{3,27},{4,4},{5,13},{6,22},{7,31},{8,8},{9,1},{... | collective-permute-start | bytes 393224 | tf_op jit(solution)/shard_map/ppermute | solution.py:170
  2.3 31.8 %all-to-all-start = ((bf16[8,2,128,512]{3,2,1,0:T(8,128)(2,1)}), bf16[8,2,128,512]{3,2,1,0:T(8,128)(2,1)S(1)}, u32[]{:S(2)}, u32[]{:S(2)}) async-start(bf16[8,2,128,512]{3,2,1,0:T(8,128)(2,1)} %bitcast.46), calls=%async_computation | async-start | bytes 4194304 | tf_op jit(solution)/shard_map/all_to_all | solution.py:176
  7.5 8.0 %copy-start.4 = (bf16[12,128,128]{2,1,0:T(8,128)(2,1)S(1)}, bf16[12,128,128]{2,1,0:T(8,128)(2,1)}, u32[]{:S(2)}) copy-start(bf16[12,128,128]{2,1,0:T(8,128)(2,1)} %param.10) | copy-start | bytes 1179652
  7.5 8.0 %copy-start.5 = (bf16[128,128]{1,0:T(8,128)(2,1)S(1)}, bf16[128,128]{1,0:T(8,128)(2,1)}, u32[]{:S(2)}) copy-start(bf16[128,128]{1,0:T(8,128)(2,1)} %param.9) | copy-start | bytes 98308
  7.5 26.6 %copy-start.2 = (s32[32,12]{0,1:T(8,128)S(1)}, s32[32,12]{0,1:T(8,128)}, u32[]{:S(2)}) copy-start(s32[32,12]{0,1:T(8,128)} %param.11) | copy-start | bytes 4612
  7.5 11.7 %collective-permute-start.3 = (bf16[128,512]{1,0:T(8,128)(2,1)S(1)}, bf16[128,512]{1,0:T(8,128)(2,1)S(1)}, u32[]{:S(2)}, u32[]{:S(2)}) collective-permute-start(bf16[128,512]{1,0:T(8,128)(2,1)S(1)} %shard_map.77), channel_id=1, source_target_pairs={{0,3},{1,2},{2,1},{3,0},{4,7},{5,6},{6,5},{7,4},{8,11},{9,10},{10,... | collective-permute-start | bytes 393224 | tf_op jit(solution)/shard_map/ppermute | solution.py:115
  14.8 10.6 %collective-permute-start.2 = (bf16[128,512]{1,0:T(8,128)(2,1)S(1)}, bf16[128,512]{1,0:T(8,128)(2,1)S(1)}, u32[]{:S(2)}, u32[]{:S(2)}) collective-permute-start(bf16[128,512]{1,0:T(8,128)(2,1)S(1)} %shard_map.77), channel_id=1, source_target_pairs={{0,2},{1,3},{2,0},{3,1},{4,6},{5,7},{6,4},{7,5},{8,10},{9,11},{10,... | collective-permute-start | bytes 393224 | tf_op jit(solution)/shard_map/ppermute | solution.py:115
  14.8 10.6 %collective-permute-start.1 = (bf16[128,512]{1,0:T(8,128)(2,1)S(1)}, bf16[128,512]{1,0:T(8,128)(2,1)S(1)}, u32[]{:S(2)}, u32[]{:S(2)}) collective-permute-start(bf16[128,512]{1,0:T(8,128)(2,1)S(1)} %shard_map.77), channel_id=1, source_target_pairs={{0,1},{1,0},{2,3},{3,2},{4,5},{5,4},{6,7},{7,6},{8,9},{9,8},{10,11... | collective-permute-start | bytes 393224 | tf_op jit(solution)/shard_map/ppermute | solution.py:115
  25.5 2.0 %collective-permute-start.4 = (bf16[4,128,512]{2,1,0:T(8,128)(2,1)S(1)}, bf16[4,128,512]{2,1,0:T(8,128)(2,1)S(1)}, u32[]{:S(2)}, u32[]{:S(2)}) collective-permute-start(bf16[4,128,512]{2,1,0:T(8,128)(2,1)S(1)} %pad_maximum_fusion.refs_3_), channel_id=1, source_target_pairs={{0,4},{4,0},{8,12},{12,8},{16,20},{20,16},{24,28},{28,24},{1,5},{5... | collective-permute-start | bytes 1572872 | tf_op jit(solution)/shard_map/ppermute | solution.py:115
  27.5 0.8 copy-start
  34.1 1.0 %copy-start.1 = (bf16[4,128,512]{2,1,0:T(8,128)(2,1)S(1)}, bf16[4,128,512]{2,1,0:T(8,128)(2,1)}, u32[]{:S(2)}) copy-start(bf16[4,128,512]{2,1,0:T(8,128)(2,1)} %copy-done) | copy-start | bytes 1572868
  38.1 2.4 %collective-permute-start.5 = (bf16[4,128,512]{2,1,0:T(8,128)(2,1)S(1)}, bf16[4,128,512]{2,1,0:T(8,128)(2,1)S(1)}, u32[]{:S(2)}, u32[]{:S(2)}) collective-permute-start(bf16[4,128,512]{2,1,0:T(8,128)(2,1)S(1)} %get-tuple-element.15), channel_id=1, source_target_pairs={{0,4},{4,0},{8,12},{12,8},{16,20},{20,16},{24,28},{28,24},{1,5},{5... | collective-permute-start | bytes 1572872 | tf_op jit(solution)/shard_map/ppermute | solution.py:115
  40.6 6.4 %collective-permute-start.6 = (bf16[128,512]{1,0:T(8,128)(2,1)S(1)}, bf16[128,512]{1,0:T(8,128)(2,1)S(1)}, u32[]{:S(2)}, u32[]{:S(2)}) collective-permute-start(bf16[128,512]{1,0:T(8,128)(2,1)S(1)} %get-tuple-element.25), channel_id=1, source_target_pairs={{0,8},{4,12},{8,0},{12,4},{16,24},{20,28},{24,16},{28,20},{1,9},{5... | collective-permute-start | bytes 393224 | tf_op jit(solution)/shard_map/ppermute | solution.py:115
  41.3 8.4 %collective-permute-start.8 = (bf16[128,512]{1,0:T(8,128)(2,1)S(1)}, bf16[128,512]{1,0:T(8,128)(2,1)S(1)}, u32[]{:S(2)}, u32[]{:S(2)}) collective-permute-start(bf16[128,512]{1,0:T(8,128)(2,1)S(1)} %get-tuple-element.26), channel_id=1, source_target_pairs={{0,16},{4,20},{8,24},{12,28},{16,0},{20,4},{24,8},{28,12},{1,17},{... | collective-permute-start | bytes 393224 | tf_op jit(solution)/shard_map/ppermute | solution.py:115
  41.9 23.1 %copy-start.3 = (f32[128,512]{1,0:T(8,128)S(1)}, f32[128,512]{1,0:T(8,128)}, u32[]{:S(2)}) copy-start(f32[128,512]{1,0:T(8,128)} %param.8) | copy-start | bytes 786436
  41.9 7.8 %collective-permute-start.7 = (bf16[128,512]{1,0:T(8,128)(2,1)S(1)}, bf16[128,512]{1,0:T(8,128)(2,1)S(1)}, u32[]{:S(2)}, u32[]{:S(2)}) collective-permute-start(bf16[128,512]{1,0:T(8,128)(2,1)S(1)} %get-tuple-element.27), channel_id=1, source_target_pairs={{0,24},{4,28},{8,16},{12,20},{16,8},{20,12},{24,0},{28,4},{1,25},{... | collective-permute-start | bytes 393224 | tf_op jit(solution)/shard_map/ppermute | solution.py:115
  49.7 7.4 %collective-permute-start.9 = (bf16[128,512]{1,0:T(8,128)(2,1)S(1)}, bf16[128,512]{1,0:T(8,128)(2,1)S(1)}, u32[]{:S(2)}, u32[]{:S(2)}) collective-permute-start(bf16[128,512]{1,0:T(8,128)(2,1)S(1)} %fusion.5), channel_id=1, source_target_pairs={{0,1},{1,0},{2,3},{3,2},{4,5},{5,4},{6,7},{7,6},{8,9},{9,8},{10,11... | collective-permute-start | bytes 393224 | tf_op jit(solution)/shard_map/ppermute | solution.py:115
  57.1 7.9 %collective-permute-start.10 = (bf16[128,512]{1,0:T(8,128)(2,1)S(1)}, bf16[128,512]{1,0:T(8,128)(2,1)S(1)}, u32[]{:S(2)}, u32[]{:S(2)}) collective-permute-start(bf16[128,512]{1,0:T(8,128)(2,1)S(1)} %add_convert_fusion.3), channel_id=1, source_target_pairs={{0,3},{1,2},{2,1},{3,0},{4,7},{5,6},{6,5},{7,4},{8,11},{9,10},{10,... | collective-permute-start | bytes 393224 | tf_op jit(solution)/shard_map/ppermute | solution.py:115
  65.0 6.0 %collective-permute-start.13 = (bf16[128,512]{1,0:T(8,128)(2,1)S(1)}, bf16[128,512]{1,0:T(8,128)(2,1)S(1)}, u32[]{:S(2)}, u32[]{:S(2)}) collective-permute-start(bf16[128,512]{1,0:T(8,128)(2,1)S(1)} %get-tuple-element.28), channel_id=1, source_target_pairs={{0,24},{4,28},{8,16},{12,20},{16,8},{20,12},{24,0},{28,4},{1,25},{... | collective-permute-start | bytes 393224 | tf_op jit(solution)/shard_map/ppermute | solution.py:115
  66.6 5.8 %collective-permute-start.12 = (bf16[128,512]{1,0:T(8,128)(2,1)S(1)}, bf16[128,512]{1,0:T(8,128)(2,1)S(1)}, u32[]{:S(2)}, u32[]{:S(2)}) collective-permute-start(bf16[128,512]{1,0:T(8,128)(2,1)S(1)} %get-tuple-element.28), channel_id=1, source_target_pairs={{0,16},{4,20},{8,24},{12,28},{16,0},{20,4},{24,8},{28,12},{1,17},{... | collective-permute-start | bytes 393224 | tf_op jit(solution)/shard_map/ppermute | solution.py:115
  68.1 5.0 %collective-permute-start.11 = (bf16[128,512]{1,0:T(8,128)(2,1)S(1)}, bf16[128,512]{1,0:T(8,128)(2,1)S(1)}, u32[]{:S(2)}, u32[]{:S(2)}) collective-permute-start(bf16[128,512]{1,0:T(8,128)(2,1)S(1)} %get-tuple-element.28), channel_id=1, source_target_pairs={{0,8},{4,12},{8,0},{12,4},{16,24},{20,28},{24,16},{28,20},{1,9},{5... | collective-permute-start | bytes 393224 | tf_op jit(solution)/shard_map/ppermute | solution.py:115
  73.1 2.0 %collective-permute-start.14 = (bf16[4,128,512]{2,1,0:T(8,128)(2,1)S(1)}, bf16[4,128,512]{2,1,0:T(8,128)(2,1)S(1)}, u32[]{:S(2)}, u32[]{:S(2)}) collective-permute-start(bf16[4,128,512]{2,1,0:T(8,128)(2,1)S(1)} %pad_maximum_fusion.1.field_ref), channel_id=1, source_target_pairs={{0,4},{4,0},{8,12},{12,8},{16,20},{20,16},{24,28},{28,24},{1,5},{5... | collective-permute-start | bytes 1572872 | tf_op jit(solution)/shard_map/ppermute | solution.py:115
  77.9 2.5 %collective-permute-start.15 = (bf16[4,128,512]{2,1,0:T(8,128)(2,1)S(1)}, bf16[4,128,512]{2,1,0:T(8,128)(2,1)S(1)}, u32[]{:S(2)}, u32[]{:S(2)}) collective-permute-start(bf16[4,128,512]{2,1,0:T(8,128)(2,1)S(1)} %get-tuple-element.20), channel_id=1, source_target_pairs={{0,4},{4,0},{8,12},{12,8},{16,20},{20,16},{24,28},{28,24},{1,5},{5... | collective-permute-start | bytes 1572872 | tf_op jit(solution)/shard_map/ppermute | solution.py:115
  80.6 6.4 %collective-permute-start.16 = (bf16[128,512]{1,0:T(8,128)(2,1)S(1)}, bf16[128,512]{1,0:T(8,128)(2,1)S(1)}, u32[]{:S(2)}, u32[]{:S(2)}) collective-permute-start(bf16[128,512]{1,0:T(8,128)(2,1)S(1)} %get-tuple-element.22), channel_id=1, source_target_pairs={{0,8},{4,12},{8,0},{12,4},{16,24},{20,28},{24,16},{28,20},{1,9},{5... | collective-permute-start | bytes 393224 | tf_op jit(solution)/shard_map/ppermute | solution.py:115
  81.5 8.3 %collective-permute-start.18 = (bf16[128,512]{1,0:T(8,128)(2,1)S(1)}, bf16[128,512]{1,0:T(8,128)(2,1)S(1)}, u32[]{:S(2)}, u32[]{:S(2)}) collective-permute-start(bf16[128,512]{1,0:T(8,128)(2,1)S(1)} %get-tuple-element.23), channel_id=1, source_target_pairs={{0,16},{4,20},{8,24},{12,28},{16,0},{20,4},{24,8},{28,12},{1,17},{... | collective-permute-start | bytes 393224 | tf_op jit(solution)/shard_map/ppermute | solution.py:115
  82.5 7.3 %collective-permute-start.17 = (bf16[128,512]{1,0:T(8,128)(2,1)S(1)}, bf16[128,512]{1,0:T(8,128)(2,1)S(1)}, u32[]{:S(2)}, u32[]{:S(2)}) collective-permute-start(bf16[128,512]{1,0:T(8,128)(2,1)S(1)} %get-tuple-element.24), channel_id=1, source_target_pairs={{0,24},{4,28},{8,16},{12,20},{16,8},{20,12},{24,0},{28,4},{1,25},{... | collective-permute-start | bytes 393224 | tf_op jit(solution)/shard_map/ppermute | solution.py:115
  89.9 5.0 %collective-permute-start.19 = (bf16[128,512]{1,0:T(8,128)(2,1)S(1)}, bf16[128,512]{1,0:T(8,128)(2,1)S(1)}, u32[]{:S(2)}, u32[]{:S(2)}) collective-permute-start(bf16[128,512]{1,0:T(8,128)(2,1)S(1)} %fusion.2), channel_id=1, source_target_pairs={{0,1},{1,0},{2,3},{3,2},{4,5},{5,4},{6,7},{7,6},{8,9},{9,8},{10,11... | collective-permute-start | bytes 393224 | tf_op jit(solution)/shard_map/ppermute | solution.py:115
  94.9 6.9 %collective-permute-start.20 = (bf16[128,512]{1,0:T(8,128)(2,1)S(1)}, bf16[128,512]{1,0:T(8,128)(2,1)S(1)}, u32[]{:S(2)}, u32[]{:S(2)}) collective-permute-start(bf16[128,512]{1,0:T(8,128)(2,1)S(1)} %add_convert_fusion.2), channel_id=1, source_target_pairs={{0,3},{1,2},{2,1},{3,0},{4,7},{5,6},{6,5},{7,4},{8,11},{9,10},{10,... | collective-permute-start | bytes 393224 | tf_op jit(solution)/shard_map/ppermute | solution.py:115

commit v5 on v4

--- a/solution.py
+++ b/solution.py
@@ -16,15 +16,14 @@
 HOLD = 50 * 10**9
 
 
-def products(me, turn, core, ens_ref, field_ref, prod_ref):
+def products(me, turn, core, ens_ref, field_refs, prod_ref):
     _, members, levels, width = ens_ref.shape
     blk = prod_ref.shape[1]
     per = width // blk
-    for k in range(field_ref.shape[0]):
-        share = me ^ (2 * k + core)
-        f = field_ref[k ^ turn]
+    for i, field_ref in enumerate(field_refs):
+        share = me ^ (2 * (i ^ turn) + core)
         for m in range(members):
-            product = (ens_ref[share, m] * f).T
+            product = (ens_ref[share, m] * field_ref[...]).T
             for j in range(per):
                 prod_ref[share * per + j, :, m * levels:(m + 1) * levels] = product[j * blk:(j + 1) * blk]
 
@@ -67,31 +66,31 @@
     copy.start()
     me = lax.axis_index("pts")
     ens_ref, mat_ref = refs.pop(0), refs.pop(0)
-    field_refs = [refs.pop(0) for _ in cores]
+    field_refs = [[refs.pop(0) for _ in range(ens_ref.shape[0] // 2)] for _ in cores]
     prod_ref = refs.pop(0) if len(cores) < 2 else None
     outs = [refs.pop(0) for _ in wanted]
     if cores:
         prod_ref = refs.pop(0)
         turn = lax.axis_index("mem") if turned else 0
-        for core, field_ref in zip(cores, field_refs):
-            products(me, turn, core, ens_ref, field_ref, prod_ref)
+        for core, some in zip(cores, field_refs):
+            products(me, turn, core, ens_ref, some, prod_ref)
     copy.wait()
     for out_ref, (core, chips) in zip(outs, wanted):
         shares = [me ^ (2 * k + core) for k in chips]
         local_sums(shares, cols_ref, ens_ref, mat_ref, prod_ref, out_ref)
 
 
-def products_kernel(ens_ref, field_ref, prod_ref):
-    products(lax.axis_index("pts"), 0, 0, ens_ref, field_ref, prod_ref)
+def products_kernel(ens_ref, *refs):
+    products(lax.axis_index("pts"), 0, 0, ens_ref, list(refs[:-1]), refs[-1])
 
 
 def copy_kernel(x_ref, out_ref):
-    out_ref[...] = x_ref[...]
+    out_ref[...] = x_ref[...].astype(out_ref.dtype)
 
 
 def passed_on(x):
     return pl.pallas_call(
-        copy_kernel, out_shape=jax.ShapeDtypeStruct(x.shape, x.dtype), in_specs=[VMEM], out_specs=VMEM,
+        copy_kernel, out_shape=jax.ShapeDtypeStruct(x.shape, BF), in_specs=[VMEM], out_specs=VMEM,
         compiler_params=PARAMS, cost_estimate=pl.CostEstimate(flops=HOLD, bytes_accessed=0, transcendentals=0),
     )(x)
 
@@ -124,23 +123,23 @@
     def local(turned, wanted, prod=None, fields=()):
         args = [cols, ens, matrices] + list(fields) + ([] if prod is None else [prod])
         outs = [jax.ShapeDtypeStruct((len(some), levels, width), BF) for _, some in wanted]
-        cores = (1,) if len(fields) == 1 else tuple(range(len(fields)))
+        cores = () if not fields else (0, 1) if prod is None else (1,)
         return pl.pallas_call(
             functools.partial(sums_kernel, cores, turned, wanted),
             out_shape=outs + ([prod_shape] if fields else []),
             in_specs=[ANY] + [VMEM] * (len(args) - 1),
             out_specs=[VMEM] * (len(outs) + bool(fields)),
             scratch_shapes=[pltpu.SMEM(cols.shape, jnp.int32), pltpu.SemaphoreType.DMA],
-            input_output_aliases={len(args) - 1: len(outs)} if len(fields) == 1 else {},
+            input_output_aliases={len(args) - 1: len(outs)} if len(cores) == 1 else {},
             compiler_params=PARAMS,
             cost_estimate=cost(sum(len(some) for _, some in wanted)),
         )(*args)
 
-    def early_products(field):
+    def early_products(fields):
         return pl.pallas_call(
-            products_kernel, out_shape=prod_shape, in_specs=[VMEM] * 2, out_specs=VMEM, compiler_params=PARAMS,
-            cost_estimate=cost(1),
-        )(ens, field)
+            products_kernel, out_shape=prod_shape, in_specs=[VMEM] * (1 + len(fields)), out_specs=VMEM,
+            compiler_params=PARAMS, cost_estimate=cost(1),
+        )(ens, *fields)
 
     def sum_over_mem(total):
         step = 1
@@ -167,23 +166,23 @@
     turned = chips == mem
     if turned:
         pairs = [(p * mem + z, (p ^ (2 * z)) * mem + z) for p in range(pts) for z in range(mem)]
-        fetched = passed_on(lax.ppermute(rounded, ("pts", "mem"), pairs))
-        same = jnp.stack([fetched] + [xor_permute(fetched, "mem", k) for k in range(1, mem)])
+        fetched = passed_on(lax.ppermute(increment, ("pts", "mem"), pairs))
+        same = [fetched] + [xor_permute(fetched, "mem", k) for k in range(1, mem)]
     else:
-        same = jnp.stack([rounded] + [xor_permute(rounded, "pts", 2 * k) for k in range(1, chips)])
+        same = [rounded] + [xor_permute(rounded, "pts", 2 * k) for k in range(1, chips)]
 
-    same, matrices = lax.optimization_barrier((same, matrices))
+    same[0], matrices = lax.optimization_barrier((same[0], matrices))
     ens = lax.all_to_all(
         ensemble.reshape(pts, share, levels, width), "pts", split_axis=0, concat_axis=0, tiled=True
     )
-    first_sum = cov_sum(turned, (same, to_mate(same)))
+    first_sum = cov_sum(turned, same + [to_mate(x) for x in same])
 
     rounded = (first_sum * obs_weight).astype(BF)
-    same = jnp.stack([rounded] + [xor_permute(rounded, "pts", 2 * k) for k in range(1, chips)])
+    same = [rounded] + [xor_permute(rounded, "pts", 2 * k) for k in range(1, chips)]
     prod = early_products(same)
     first_sum, prod = lax.optimization_barrier((first_sum, prod))
     weighted = first_sum * obs_weight
-    applied = cov_sum(False, (to_mate(same),), prod)
+    applied = cov_sum(False, [to_mate(x) for x in same], prod)
     return weighted, applied
 
 

time: 103 us -> 102 us (level)
  waiting for transfers between devices: 43.6 us -> 40.4 us
  starting transfers between devices: 39.7 us -> 42.6 us
  other arithmetic: 3.1 us -> 1.99 us
    ppermute x20 -> x26, waiting for transfers between devices: 37.8 us -> 35 us  [xor_permute(): lax.ppermute(x, axis, [(i, i ^ k) for i in range(lax.axis_size(axis))])]
    ppermute x20 -> x26, starting transfers between devices: 33.8 us -> 35.8 us  [xor_permute(): lax.ppermute(x, axis, [(i, i ^ k) for i in range(lax.axis_size(axis))])]
  transfers between devices with their start and end apart: 22 -> 28, of which waited for: 16 -> 18; matrix products, arithmetic and copies ran while one was open for 1% -> 1% of each run, Pallas kernels for 8% -> 8%
where the time goes in v5:
time: 102 us; the launch traced here: 101 us
  starting transfers between devices  42.6 us (42%)
  waiting for transfers between devices  40.4 us (40%)
  Pallas kernels  13.9 us (14%)
  other arithmetic  1.99 us (2%)
  local copies, waits for them, and re-layouts  1.64 us (2%)
    ppermute x26, starting transfers between devices, xor_permute(): lax.ppermute(x, axis, [(i, i ^ k) for i in range(lax.axis_size(axis))])  35.8 us
    ppermute x26, waiting for transfers between devices, xor_permute(): lax.ppermute(x, axis, [(i, i ^ k) for i in range(lax.axis_size(axis))])  35 us
    pallas_call x6, Pallas kernels, local(): pl.pallas_call(functools.partial(sums_kernel, cores, turned, wanted), out...  13.5 us
    all_to_all x1, waiting for transfers between devices, per_device(): lax.all_to_all(ensemble.reshape(pts, share, levels, width), 'pts', split_...  5.4 us
    all_to_all x1, starting transfers between devices, per_device(): lax.all_to_all(ensemble.reshape(pts, share, levels, width), 'pts', split_...  5.17 us
  transfers between devices with their start and end apart: 28, of which 18 were waited for; matrix products, arithmetic and copies ran while one was open for 1% of the time, Pallas kernels for 8%

profile of v5, /device:TPU:0, one launch (start us, length us, event | category | flops | bytes accessed | tf_op | source)
XLA Modules:
  0.0 101.4 jit_solution(9716646379939170087)
XLA Ops:
  0.6 1.6 %collective-permute-start = (f32[128,512]{1,0:T(8,128)}, f32[128,512]{1,0:T(8,128)S(1)}, u32[]{:S(2)}, u32[]{:S(2)}) collective-permute-start(f32[128,512]{1,0:T(8,128)} %param.7), channel_id=1, source_target_pairs={{0,0},{1,9},{2,18},{3,27},{4,4},{5,13},{6,22},{7,31},{8,8},{9,1},{... | collective-permute-start | bytes 786440 | tf_op jit(solution)/shard_map/ppermute | solution.py:169
  2.2 5.2 %all-to-all-start = ((bf16[8,2,128,512]{3,2,1,0:T(8,128)(2,1)}), bf16[8,2,128,512]{3,2,1,0:T(8,128)(2,1)S(1)}, u32[]{:S(2)}, u32[]{:S(2)}) async-start(bf16[8,2,128,512]{3,2,1,0:T(8,128)(2,1)} %bitcast.37), calls=%async_computation | async-start | bytes 4194304 | tf_op jit(solution)/shard_map/all_to_all | solution.py:175
  7.4 0.0 copy-start.5
  7.4 0.0 copy-start.2
  7.5 9.6 %collective-permute-start.3 = (bf16[128,512]{1,0:T(8,128)(2,1)S(1)}, bf16[128,512]{1,0:T(8,128)(2,1)S(1)}, u32[]{:S(2)}, u32[]{:S(2)}) collective-permute-start(bf16[128,512]{1,0:T(8,128)(2,1)S(1)} %shard_map.77.refs_3_), channel_id=1, source_target_pairs={{0,3},{1,2},{2,1},{3,0},{4,7},{5,6},{6,5},{7,4},{8,11},{9,10},{10,... | collective-permute-start | bytes 393224 | tf_op jit(solution)/shard_map/ppermute | solution.py:114
  17.1 0.0 collective-permute-start.2
  17.1 0.6 collective-permute-start.1
  17.8 0.1 collective-permute-start.4
  17.8 3.7 %collective-permute-done.3.refs_6_ = bf16[128,512]{1,0:T(8,128)(2,1)S(1)} collective-permute-done((bf16[128,512]{1,0:T(8,128)(2,1)S(1)}, bf16[128,512]{1,0:T(8,128)(2,1)S(1)}, u32[]{:S(2)}, u32[]{:S(2)}) %collective-permute-start.3) | collective-permute-done | bytes 131104 | tf_op jit(solution)/shard_map/ppermute | solution.py:114
  21.5 0.0 collective-permute-start.7
  21.5 4.9 %collective-permute-done.2.refs_5_ = bf16[128,512]{1,0:T(8,128)(2,1)S(1)} collective-permute-done((bf16[128,512]{1,0:T(8,128)(2,1)S(1)}, bf16[128,512]{1,0:T(8,128)(2,1)S(1)}, u32[]{:S(2)}, u32[]{:S(2)}) %collective-permute-start.2) | collective-permute-done | bytes 131104 | tf_op jit(solution)/shard_map/ppermute | solution.py:114
  26.5 0.0 collective-permute-start.6
  26.5 0.0 collective-permute-done.1.refs_4_
  26.5 0.5 collective-permute-start.5
  27.0 0.0 collective-permute-done.4.refs_7_
  27.0 0.0 collective-permute-done.7.refs_10_
  27.0 0.8 collective-permute-done.6.refs_9_
  27.8 0.2 collective-permute-done.5.refs_8_
  28.0 0.7 copy-done
  28.7 5.4 %all-to-all-done.refs_1_.ens_ref = bf16[8,2,128,512]{3,2,1,0:T(8,128)(2,1)S(1)} async-done(((bf16[8,2,128,512]{3,2,1,0:T(8,128)(2,1)}), bf16[8,2,128,512]{3,2,1,0:T(8,128)(2,1)S(1)}, u32[]{:S(2)}, u32[]{:S(2)}) %all-to-all-start) | async-done | bytes 2097184 | tf_op jit(solution)/shard_map/all_to_all | solution.py:175
  34.1 0.9 copy-done.1
  35.0 3.2 %shard_map.78 = (bf16[4,128,512]{2,1,0:T(8,128)(2,1)S(1)}, bf16[32,128,256]{2,1,0:T(8,128)(2,1)S(1)}) custom-call(s32[12,32]{1,0:T(8,128)S(1)} %bitcast.31, bf16[8,2,128,512]{3,2,1,0:T(8,128)(2,1)S(1)} %all-to-all-done.refs_1_.ens_ref, bf16[1664,128]{1,0:T(8,128)(2,1)S(1)} %pad_maximum_fusion.refs_2_, bf16[128,512]{1,0:T(8,128)(2,1)S(1)} %shard_map.77.refs_3_, ...), custom_call_target="tpu_custom_call" | custom-call | flops 6442450944 | tf_op jit(solution)/shard_map/pallas_call | solution.py:127
  38.2 0.1 collective-permute-start.8
  38.3 2.3 %shard_map.79 = bf16[3,128,512]{2,1,0:T(8,128)(2,1)S(1)} custom-call(s32[12,32]{1,0:T(8,128)S(1)} %bitcast.32, bf16[8,2,128,512]{3,2,1,0:T(8,128)(2,1)S(1)} %all-to-all-done.refs_1_.ens_ref, bf16[1664,128]{1,0:T(8,128)(2,1)S(1)} %pad_maximum_fusion.refs_2_, bf16[32,128,256]{2,1,0:T(8,128)(2,1)S(1)} %get-tuple-element.16.refs_3_), custom_call_target="tpu_custom_call" | custom-call | flops 4831838208 | tf_op jit(solution)/shard_map/pallas_call | solution.py:127
  40.5 0.0 collective-permute-done.8
  40.6 0.1 add_convert_fusion.1
  40.7 0.6 collective-permute-start.9
  41.3 0.6 collective-permute-start.11
  41.9 2.3 %collective-permute-start.10 = (bf16[128,512]{1,0:T(8,128)(2,1)S(1)}, bf16[128,512]{1,0:T(8,128)(2,1)S(1)}, u32[]{:S(2)}, u32[]{:S(2)}) collective-permute-start(bf16[128,512]{1,0:T(8,128)(2,1)S(1)} %get-tuple-element.27), channel_id=1, source_target_pairs={{0,24},{4,28},{8,16},{12,20},{16,8},{20,12},{24,0},{28,4},{1,25},{... | collective-permute-start | bytes 393224 | tf_op jit(solution)/shard_map/ppermute | solution.py:114
  44.2 1.4 %shard_map.80 = bf16[1,128,512]{2,1,0:T(8,128)(2,1)S(1)} custom-call(s32[12,32]{1,0:T(8,128)S(1)} %bitcast.33, bf16[8,2,128,512]{3,2,1,0:T(8,128)(2,1)S(1)} %all-to-all-done.refs_1_.ens_ref, bf16[1664,128]{1,0:T(8,128)(2,1)S(1)} %pad_maximum_fusion.refs_2_, bf16[32,128,256]{2,1,0:T(8,128)(2,1)S(1)} %get-tuple-element.16.refs_3_), custom_call_target="tpu_custom_call" | custom-call | flops 1610612736 | tf_op jit(solution)/shard_map/pallas_call | solution.py:127
  45.7 1.4 %collective-permute-done.9 = bf16[128,512]{1,0:T(8,128)(2,1)S(1)} collective-permute-done((bf16[128,512]{1,0:T(8,128)(2,1)S(1)}, bf16[128,512]{1,0:T(8,128)(2,1)S(1)}, u32[]{:S(2)}, u32[]{:S(2)}) %collective-permute-start.9) | collective-permute-done | bytes 131104 | tf_op jit(solution)/shard_map/ppermute | solution.py:114
  47.1 2.6 %collective-permute-done.11 = bf16[128,512]{1,0:T(8,128)(2,1)S(1)} collective-permute-done((bf16[128,512]{1,0:T(8,128)(2,1)S(1)}, bf16[128,512]{1,0:T(8,128)(2,1)S(1)}, u32[]{:S(2)}, u32[]{:S(2)}) %collective-permute-start.11) | collective-permute-done | bytes 131104 | tf_op jit(solution)/shard_map/ppermute | solution.py:114
  49.7 0.1 fusion.5
  49.8 3.4 %collective-permute-start.12 = (bf16[128,512]{1,0:T(8,128)(2,1)S(1)}, bf16[128,512]{1,0:T(8,128)(2,1)S(1)}, u32[]{:S(2)}, u32[]{:S(2)}) collective-permute-start(bf16[128,512]{1,0:T(8,128)(2,1)S(1)} %fusion.5), channel_id=1, source_target_pairs={{0,1},{1,0},{2,3},{3,2},{4,5},{5,4},{6,7},{7,6},{8,9},{9,8},{10,11... | collective-permute-start | bytes 393224 | tf_op jit(solution)/shard_map/ppermute | solution.py:114
  53.1 2.9 %collective-permute-done.12 = bf16[128,512]{1,0:T(8,128)(2,1)S(1)} collective-permute-done((bf16[128,512]{1,0:T(8,128)(2,1)S(1)}, bf16[128,512]{1,0:T(8,128)(2,1)S(1)}, u32[]{:S(2)}, u32[]{:S(2)}) %collective-permute-start.12) | collective-permute-done | bytes 131104 | tf_op jit(solution)/shard_map/ppermute | solution.py:114
  56.1 5.1 %collective-permute-start.13 = (bf16[128,512]{1,0:T(8,128)(2,1)S(1)}, bf16[128,512]{1,0:T(8,128)(2,1)S(1)}, u32[]{:S(2)}, u32[]{:S(2)}) collective-permute-start(bf16[128,512]{1,0:T(8,128)(2,1)S(1)} %add_convert_fusion.3), channel_id=1, source_target_pairs={{0,3},{1,2},{2,1},{3,0},{4,7},{5,6},{6,5},{7,4},{8,11},{9,10},{10,... | collective-permute-start | bytes 393224 | tf_op jit(solution)/shard_map/ppermute | solution.py:114
  61.2 3.1 %collective-permute-done.13 = bf16[128,512]{1,0:T(8,128)(2,1)S(1)} collective-permute-done((bf16[128,512]{1,0:T(8,128)(2,1)S(1)}, bf16[128,512]{1,0:T(8,128)(2,1)S(1)}, u32[]{:S(2)}, u32[]{:S(2)}) %collective-permute-start.13) | collective-permute-done | bytes 131104 | tf_op jit(solution)/shard_map/ppermute | solution.py:114
  64.3 1.5 %collective-permute-start.16 = (bf16[128,512]{1,0:T(8,128)(2,1)S(1)}, bf16[128,512]{1,0:T(8,128)(2,1)S(1)}, u32[]{:S(2)}, u32[]{:S(2)}) collective-permute-start(bf16[128,512]{1,0:T(8,128)(2,1)S(1)} %get-tuple-element.28.refs_0_), channel_id=1, source_target_pairs={{0,24},{4,28},{8,16},{12,20},{16,8},{20,12},{24,0},{28,4},{1,25},{... | collective-permute-start | bytes 393224 | tf_op jit(solution)/shard_map/ppermute | solution.py:114
  65.8 1.5 %collective-permute-start.15 = (bf16[128,512]{1,0:T(8,128)(2,1)S(1)}, bf16[128,512]{1,0:T(8,128)(2,1)S(1)}, u32[]{:S(2)}, u32[]{:S(2)}) collective-permute-start(bf16[128,512]{1,0:T(8,128)(2,1)S(1)} %get-tuple-element.28.refs_0_), channel_id=1, source_target_pairs={{0,16},{4,20},{8,24},{12,28},{16,0},{20,4},{24,8},{28,12},{1,17},{... | collective-permute-start | bytes 393224 | tf_op jit(solution)/shard_map/ppermute | solution.py:114
  67.3 0.6 collective-permute-start.14
  67.9 0.0 collective-permute-start.17
  67.9 2.5 %collective-permute-done.16.refs_3_ = bf16[128,512]{1,0:T(8,128)(2,1)S(1)} collective-permute-done((bf16[128,512]{1,0:T(8,128)(2,1)S(1)}, bf16[128,512]{1,0:T(8,128)(2,1)S(1)}, u32[]{:S(2)}, u32[]{:S(2)}) %collective-permute-start.16) | collective-permute-done | bytes 131104 | tf_op jit(solution)/shard_map/ppermute | solution.py:114
  70.3 1.3 %collective-permute-done.15.refs_2_ = bf16[128,512]{1,0:T(8,128)(2,1)S(1)} collective-permute-done((bf16[128,512]{1,0:T(8,128)(2,1)S(1)}, bf16[128,512]{1,0:T(8,128)(2,1)S(1)}, u32[]{:S(2)}, u32[]{:S(2)}) %collective-permute-start.15) | collective-permute-done | bytes 131104 | tf_op jit(solution)/shard_map/ppermute | solution.py:114
  71.6 0.6 collective-permute-done.14.refs_1_
  72.2 0.3 shard_map.81.refs_7_
  72.6 0.4 collective-permute-done.19.refs_5_
  73.0 0.6 collective-permute-done.18.refs_4_
  73.6 2.9 %shard_map.82 = (bf16[4,128,512]{2,1,0:T(8,128)(2,1)S(1)}, bf16[32,128,256]{2,1,0:T(8,128)(2,1)S(1)}) custom-call(s32[12,32]{1,0:T(8,128)S(1)} %bitcast.34, bf16[8,2,128,512]{3,2,1,0:T(8,128)(2,1)S(1)} %all-to-all-done.refs_1_.ens_ref, bf16[1664,128]{1,0:T(8,128)(2,1)S(1)} %pad_maximum_fusion.refs_2_, ...), custom_call_target="tpu_custom_call", output_to_operand_aliasing={{1}: (7, {})} | custom-call | flops 6442450944 | tf_op jit(solution)/shard_map/pallas_call | solution.py:127
  76.5 0.2 collective-permute-start.21
  76.7 2.3 %shard_map.83 = bf16[3,128,512]{2,1,0:T(8,128)(2,1)S(1)} custom-call(s32[12,32]{1,0:T(8,128)S(1)} %bitcast.35, bf16[8,2,128,512]{3,2,1,0:T(8,128)(2,1)S(1)} %all-to-all-done.refs_1_.ens_ref, bf16[1664,128]{1,0:T(8,128)(2,1)S(1)} %pad_maximum_fusion.refs_2_, bf16[32,128,256]{2,1,0:T(8,128)(2,1)S(1)} %get-tuple-element.21.refs_3_), custom_call_target="tpu_custom_call" | custom-call | flops 4831838208 | tf_op jit(solution)/shard_map/pallas_call | solution.py:127
  79.0 0.1 add_convert_fusion
  79.1 1.3 %collective-permute-start.22 = (bf16[128,512]{1,0:T(8,128)(2,1)S(1)}, bf16[128,512]{1,0:T(8,128)(2,1)S(1)}, u32[]{:S(2)}, u32[]{:S(2)}) collective-permute-start(bf16[128,512]{1,0:T(8,128)(2,1)S(1)} %get-tuple-element.22), channel_id=1, source_target_pairs={{0,8},{4,12},{8,0},{12,4},{16,24},{20,28},{24,16},{28,20},{1,9},{5... | collective-permute-start | bytes 393224 | tf_op jit(solution)/shard_map/ppermute | solution.py:114
  80.4 0.8 collective-permute-start.24
  81.2 1.5 %collective-permute-start.23 = (bf16[128,512]{1,0:T(8,128)(2,1)S(1)}, bf16[128,512]{1,0:T(8,128)(2,1)S(1)}, u32[]{:S(2)}, u32[]{:S(2)}) collective-permute-start(bf16[128,512]{1,0:T(8,128)(2,1)S(1)} %get-tuple-element.24), channel_id=1, source_target_pairs={{0,24},{4,28},{8,16},{12,20},{16,8},{20,12},{24,0},{28,4},{1,25},{... | collective-permute-start | bytes 393224 | tf_op jit(solution)/shard_map/ppermute | solution.py:114
  82.7 1.4 %shard_map.84 = bf16[1,128,512]{2,1,0:T(8,128)(2,1)S(1)} custom-call(s32[12,32]{1,0:T(8,128)S(1)} %bitcast.36, bf16[8,2,128,512]{3,2,1,0:T(8,128)(2,1)S(1)} %all-to-all-done.refs_1_.ens_ref, bf16[1664,128]{1,0:T(8,128)(2,1)S(1)} %pad_maximum_fusion.refs_2_, bf16[32,128,256]{2,1,0:T(8,128)(2,1)S(1)} %get-tuple-element.21.refs_3_), custom_call_target="tpu_custom_call" | custom-call | flops 1610612736 | tf_op jit(solution)/shard_map/pallas_call | solution.py:127
  84.1 1.4 %collective-permute-done.22 = bf16[128,512]{1,0:T(8,128)(2,1)S(1)} collective-permute-done((bf16[128,512]{1,0:T(8,128)(2,1)S(1)}, bf16[128,512]{1,0:T(8,128)(2,1)S(1)}, u32[]{:S(2)}, u32[]{:S(2)}) %collective-permute-start.22) | collective-permute-done | bytes 131104 | tf_op jit(solution)/shard_map/ppermute | solution.py:114
  85.5 3.0 %collective-permute-done.24 = bf16[128,512]{1,0:T(8,128)(2,1)S(1)} collective-permute-done((bf16[128,512]{1,0:T(8,128)(2,1)S(1)}, bf16[128,512]{1,0:T(8,128)(2,1)S(1)}, u32[]{:S(2)}, u32[]{:S(2)}) %collective-permute-start.24) | collective-permute-done | bytes 131104 | tf_op jit(solution)/shard_map/ppermute | solution.py:114
  88.5 0.1 fusion.2
  88.6 1.8 %collective-permute-start.25 = (bf16[128,512]{1,0:T(8,128)(2,1)S(1)}, bf16[128,512]{1,0:T(8,128)(2,1)S(1)}, u32[]{:S(2)}, u32[]{:S(2)}) collective-permute-start(bf16[128,512]{1,0:T(8,128)(2,1)S(1)} %fusion.2), channel_id=1, source_target_pairs={{0,1},{1,0},{2,3},{3,2},{4,5},{5,4},{6,7},{7,6},{8,9},{9,8},{10,11... | collective-permute-start | bytes 393224 | tf_op jit(solution)/shard_map/ppermute | solution.py:114
  90.4 3.3 %collective-permute-done.25 = bf16[128,512]{1,0:T(8,128)(2,1)S(1)} collective-permute-done((bf16[128,512]{1,0:T(8,128)(2,1)S(1)}, bf16[128,512]{1,0:T(8,128)(2,1)S(1)}, u32[]{:S(2)}, u32[]{:S(2)}) %collective-permute-start.25) | collective-permute-done | bytes 131104 | tf_op jit(solution)/shard_map/ppermute | solution.py:114
  93.7 3.8 %collective-permute-start.26 = (bf16[128,512]{1,0:T(8,128)(2,1)S(1)}, bf16[128,512]{1,0:T(8,128)(2,1)S(1)}, u32[]{:S(2)}, u32[]{:S(2)}) collective-permute-start(bf16[128,512]{1,0:T(8,128)(2,1)S(1)} %add_convert_fusion.2), channel_id=1, source_target_pairs={{0,3},{1,2},{2,1},{3,0},{4,7},{5,6},{6,5},{7,4},{8,11},{9,10},{10,... | collective-permute-start | bytes 393224 | tf_op jit(solution)/shard_map/ppermute | solution.py:114
  97.5 0.7 mul.7
  98.3 2.4 %collective-permute-done.26 = bf16[128,512]{1,0:T(8,128)(2,1)S(1)} collective-permute-done((bf16[128,512]{1,0:T(8,128)(2,1)S(1)}, bf16[128,512]{1,0:T(8,128)(2,1)S(1)}, u32[]{:S(2)}, u32[]{:S(2)}) %collective-permute-start.26) | collective-permute-done | bytes 131104 | tf_op jit(solution)/shard_map/ppermute | solution.py:114
  100.6 0.7 convert_add_fusion
  (24 shorter events, 0.2 us)
Async XLA Ops:
  0.6 6.8 %collective-permute-start = (f32[128,512]{1,0:T(8,128)}, f32[128,512]{1,0:T(8,128)S(1)}, u32[]{:S(2)}, u32[]{:S(2)}) collective-permute-start(f32[128,512]{1,0:T(8,128)} %param.7), channel_id=1, source_target_pairs={{0,0},{1,9},{2,18},{3,27},{4,4},{5,13},{6,22},{7,31},{8,8},{9,1},{... | collective-permute-start | bytes 786440 | tf_op jit(solution)/shard_map/ppermute | solution.py:169
  2.2 31.8 %all-to-all-start = ((bf16[8,2,128,512]{3,2,1,0:T(8,128)(2,1)}), bf16[8,2,128,512]{3,2,1,0:T(8,128)(2,1)S(1)}, u32[]{:S(2)}, u32[]{:S(2)}) async-start(bf16[8,2,128,512]{3,2,1,0:T(8,128)(2,1)} %bitcast.37), calls=%async_computation | async-start | bytes 4194304 | tf_op jit(solution)/shard_map/all_to_all | solution.py:175
  7.4 10.3 %copy-start.4 = (bf16[12,128,128]{2,1,0:T(8,128)(2,1)S(1)}, bf16[12,128,128]{2,1,0:T(8,128)(2,1)}, u32[]{:S(2)}) copy-start(bf16[12,128,128]{2,1,0:T(8,128)(2,1)} %param.10) | copy-start | bytes 1179652
  7.4 10.3 %copy-start.5 = (bf16[128,128]{1,0:T(8,128)(2,1)S(1)}, bf16[128,128]{1,0:T(8,128)(2,1)}, u32[]{:S(2)}) copy-start(bf16[128,128]{1,0:T(8,128)(2,1)} %param.9) | copy-start | bytes 98308
  7.4 26.6 %copy-start.2 = (s32[32,12]{0,1:T(8,128)S(1)}, s32[32,12]{0,1:T(8,128)}, u32[]{:S(2)}) copy-start(s32[32,12]{0,1:T(8,128)} %param.11) | copy-start | bytes 4612
  7.5 14.1 %collective-permute-start.3 = (bf16[128,512]{1,0:T(8,128)(2,1)S(1)}, bf16[128,512]{1,0:T(8,128)(2,1)S(1)}, u32[]{:S(2)}, u32[]{:S(2)}) collective-permute-start(bf16[128,512]{1,0:T(8,128)(2,1)S(1)} %shard_map.77.refs_3_), channel_id=1, source_target_pairs={{0,3},{1,2},{2,1},{3,0},{4,7},{5,6},{6,5},{7,4},{8,11},{9,10},{10,... | collective-permute-start | bytes 393224 | tf_op jit(solution)/shard_map/ppermute | solution.py:114
  17.1 9.4 %collective-permute-start.2 = (bf16[128,512]{1,0:T(8,128)(2,1)S(1)}, bf16[128,512]{1,0:T(8,128)(2,1)S(1)}, u32[]{:S(2)}, u32[]{:S(2)}) collective-permute-start(bf16[128,512]{1,0:T(8,128)(2,1)S(1)} %shard_map.77.refs_3_), channel_id=1, source_target_pairs={{0,2},{1,3},{2,0},{3,1},{4,6},{5,7},{6,4},{7,5},{8,10},{9,11},{10,... | collective-permute-start | bytes 393224 | tf_op jit(solution)/shard_map/ppermute | solution.py:114
  17.1 9.4 %collective-permute-start.1 = (bf16[128,512]{1,0:T(8,128)(2,1)S(1)}, bf16[128,512]{1,0:T(8,128)(2,1)S(1)}, u32[]{:S(2)}, u32[]{:S(2)}) collective-permute-start(bf16[128,512]{1,0:T(8,128)(2,1)S(1)} %shard_map.77.refs_3_), channel_id=1, source_target_pairs={{0,1},{1,0},{2,3},{3,2},{4,5},{5,4},{6,7},{7,6},{8,9},{9,8},{10,11... | collective-permute-start | bytes 393224 | tf_op jit(solution)/shard_map/ppermute | solution.py:114
  17.8 9.2 %collective-permute-start.4 = (bf16[128,512]{1,0:T(8,128)(2,1)S(1)}, bf16[128,512]{1,0:T(8,128)(2,1)S(1)}, u32[]{:S(2)}, u32[]{:S(2)}) collective-permute-start(bf16[128,512]{1,0:T(8,128)(2,1)S(1)} %shard_map.77.refs_3_), channel_id=1, source_target_pairs={{0,4},{4,0},{8,12},{12,8},{16,20},{20,16},{24,28},{28,24},{1,5},{5... | collective-permute-start | bytes 393224 | tf_op jit(solution)/shard_map/ppermute | solution.py:114
  21.5 5.4 %collective-permute-start.7 = (bf16[128,512]{1,0:T(8,128)(2,1)S(1)}, bf16[128,512]{1,0:T(8,128)(2,1)S(1)}, u32[]{:S(2)}, u32[]{:S(2)}) collective-permute-start(bf16[128,512]{1,0:T(8,128)(2,1)S(1)} %collective-permute-done.3.refs_6_), channel_id=1, source_target_pairs={{0,4},{4,0},{8,12},{12,8},{16,20},{20,16},{24,28},{28,24},{1,5},{5... | collective-permute-start | bytes 393224 | tf_op jit(solution)/shard_map/ppermute | solution.py:114
  26.5 1.3 %collective-permute-start.6 = (bf16[128,512]{1,0:T(8,128)(2,1)S(1)}, bf16[128,512]{1,0:T(8,128)(2,1)S(1)}, u32[]{:S(2)}, u32[]{:S(2)}) collective-permute-start(bf16[128,512]{1,0:T(8,128)(2,1)S(1)} %collective-permute-done.2.refs_5_), channel_id=1, source_target_pairs={{0,4},{4,0},{8,12},{12,8},{16,20},{20,16},{24,28},{28,24},{1,5},{5... | collective-permute-start | bytes 393224 | tf_op jit(solution)/shard_map/ppermute | solution.py:114
  26.5 1.5 %collective-permute-start.5 = (bf16[128,512]{1,0:T(8,128)(2,1)S(1)}, bf16[128,512]{1,0:T(8,128)(2,1)S(1)}, u32[]{:S(2)}, u32[]{:S(2)}) collective-permute-start(bf16[128,512]{1,0:T(8,128)(2,1)S(1)} %collective-permute-done.1.refs_4_), channel_id=1, source_target_pairs={{0,4},{4,0},{8,12},{12,8},{16,20},{20,16},{24,28},{28,24},{1,5},{5... | collective-permute-start | bytes 393224 | tf_op jit(solution)/shard_map/ppermute | solution.py:114
  28.0 0.7 copy-start
  34.1 0.9 copy-start.1
  38.2 2.3 %collective-permute-start.8 = (bf16[4,128,512]{2,1,0:T(8,128)(2,1)S(1)}, bf16[4,128,512]{2,1,0:T(8,128)(2,1)S(1)}, u32[]{:S(2)}, u32[]{:S(2)}) collective-permute-start(bf16[4,128,512]{2,1,0:T(8,128)(2,1)S(1)} %get-tuple-element.15), channel_id=1, source_target_pairs={{0,4},{4,0},{8,12},{12,8},{16,20},{20,16},{24,28},{28,24},{1,5},{5... | collective-permute-start | bytes 1572872 | tf_op jit(solution)/shard_map/ppermute | solution.py:114
  40.7 6.4 %collective-permute-start.9 = (bf16[128,512]{1,0:T(8,128)(2,1)S(1)}, bf16[128,512]{1,0:T(8,128)(2,1)S(1)}, u32[]{:S(2)}, u32[]{:S(2)}) collective-permute-start(bf16[128,512]{1,0:T(8,128)(2,1)S(1)} %get-tuple-element.25), channel_id=1, source_target_pairs={{0,8},{4,12},{8,0},{12,4},{16,24},{20,28},{24,16},{28,20},{1,9},{5... | collective-permute-start | bytes 393224 | tf_op jit(solution)/shard_map/ppermute | solution.py:114
  41.3 8.4 %collective-permute-start.11 = (bf16[128,512]{1,0:T(8,128)(2,1)S(1)}, bf16[128,512]{1,0:T(8,128)(2,1)S(1)}, u32[]{:S(2)}, u32[]{:S(2)}) collective-permute-start(bf16[128,512]{1,0:T(8,128)(2,1)S(1)} %get-tuple-element.26), channel_id=1, source_target_pairs={{0,16},{4,20},{8,24},{12,28},{16,0},{20,4},{24,8},{28,12},{1,17},{... | collective-permute-start | bytes 393224 | tf_op jit(solution)/shard_map/ppermute | solution.py:114
  41.9 22.3 %copy-start.3 = (f32[128,512]{1,0:T(8,128)S(1)}, f32[128,512]{1,0:T(8,128)}, u32[]{:S(2)}) copy-start(f32[128,512]{1,0:T(8,128)} %param.8) | copy-start | bytes 786436
  41.9 7.8 %collective-permute-start.10 = (bf16[128,512]{1,0:T(8,128)(2,1)S(1)}, bf16[128,512]{1,0:T(8,128)(2,1)S(1)}, u32[]{:S(2)}, u32[]{:S(2)}) collective-permute-start(bf16[128,512]{1,0:T(8,128)(2,1)S(1)} %get-tuple-element.27), channel_id=1, source_target_pairs={{0,24},{4,28},{8,16},{12,20},{16,8},{20,12},{24,0},{28,4},{1,25},{... | collective-permute-start | bytes 393224 | tf_op jit(solution)/shard_map/ppermute | solution.py:114
  49.8 6.3 %collective-permute-start.12 = (bf16[128,512]{1,0:T(8,128)(2,1)S(1)}, bf16[128,512]{1,0:T(8,128)(2,1)S(1)}, u32[]{:S(2)}, u32[]{:S(2)}) collective-permute-start(bf16[128,512]{1,0:T(8,128)(2,1)S(1)} %fusion.5), channel_id=1, source_target_pairs={{0,1},{1,0},{2,3},{3,2},{4,5},{5,4},{6,7},{7,6},{8,9},{9,8},{10,11... | collective-permute-start | bytes 393224 | tf_op jit(solution)/shard_map/ppermute | solution.py:114
  56.1 8.1 %collective-permute-start.13 = (bf16[128,512]{1,0:T(8,128)(2,1)S(1)}, bf16[128,512]{1,0:T(8,128)(2,1)S(1)}, u32[]{:S(2)}, u32[]{:S(2)}) collective-permute-start(bf16[128,512]{1,0:T(8,128)(2,1)S(1)} %add_convert_fusion.3), channel_id=1, source_target_pairs={{0,3},{1,2},{2,1},{3,0},{4,7},{5,6},{6,5},{7,4},{8,11},{9,10},{10,... | collective-permute-start | bytes 393224 | tf_op jit(solution)/shard_map/ppermute | solution.py:114
  64.3 6.0 %collective-permute-start.16 = (bf16[128,512]{1,0:T(8,128)(2,1)S(1)}, bf16[128,512]{1,0:T(8,128)(2,1)S(1)}, u32[]{:S(2)}, u32[]{:S(2)}) collective-permute-start(bf16[128,512]{1,0:T(8,128)(2,1)S(1)} %get-tuple-element.28.refs_0_), channel_id=1, source_target_pairs={{0,24},{4,28},{8,16},{12,20},{16,8},{20,12},{24,0},{28,4},{1,25},{... | collective-permute-start | bytes 393224 | tf_op jit(solution)/shard_map/ppermute | solution.py:114
  65.8 5.9 %collective-permute-start.15 = (bf16[128,512]{1,0:T(8,128)(2,1)S(1)}, bf16[128,512]{1,0:T(8,128)(2,1)S(1)}, u32[]{:S(2)}, u32[]{:S(2)}) collective-permute-start(bf16[128,512]{1,0:T(8,128)(2,1)S(1)} %get-tuple-element.28.refs_0_), channel_id=1, source_target_pairs={{0,16},{4,20},{8,24},{12,28},{16,0},{20,4},{24,8},{28,12},{1,17},{... | collective-permute-start | bytes 393224 | tf_op jit(solution)/shard_map/ppermute | solution.py:114
  67.3 5.0 %collective-permute-start.14 = (bf16[128,512]{1,0:T(8,128)(2,1)S(1)}, bf16[128,512]{1,0:T(8,128)(2,1)S(1)}, u32[]{:S(2)}, u32[]{:S(2)}) collective-permute-start(bf16[128,512]{1,0:T(8,128)(2,1)S(1)} %get-tuple-element.28.refs_0_), channel_id=1, source_target_pairs={{0,8},{4,12},{8,0},{12,4},{16,24},{20,28},{24,16},{28,20},{1,9},{5... | collective-permute-start | bytes 393224 | tf_op jit(solution)/shard_map/ppermute | solution.py:114
  67.9 4.7 %collective-permute-start.17 = (bf16[128,512]{1,0:T(8,128)(2,1)S(1)}, bf16[128,512]{1,0:T(8,128)(2,1)S(1)}, u32[]{:S(2)}, u32[]{:S(2)}) collective-permute-start(bf16[128,512]{1,0:T(8,128)(2,1)S(1)} %get-tuple-element.28.refs_0_), channel_id=1, source_target_pairs={{0,4},{4,0},{8,12},{12,8},{16,20},{20,16},{24,28},{28,24},{1,5},{5... | collective-permute-start | bytes 393224 | tf_op jit(solution)/shard_map/ppermute | solution.py:114
  70.3 2.2 %collective-permute-start.20 = (bf16[128,512]{1,0:T(8,128)(2,1)S(1)}, bf16[128,512]{1,0:T(8,128)(2,1)S(1)}, u32[]{:S(2)}, u32[]{:S(2)}) collective-permute-start(bf16[128,512]{1,0:T(8,128)(2,1)S(1)} %collective-permute-done.16.refs_3_), channel_id=1, source_target_pairs={{0,4},{4,0},{8,12},{12,8},{16,20},{20,16},{24,28},{28,24},{1,5},{5... | collective-permute-start | bytes 393224 | tf_op jit(solution)/shard_map/ppermute | solution.py:114
  71.6 1.3 %collective-permute-start.19 = (bf16[128,512]{1,0:T(8,128)(2,1)S(1)}, bf16[128,512]{1,0:T(8,128)(2,1)S(1)}, u32[]{:S(2)}, u32[]{:S(2)}) collective-permute-start(bf16[128,512]{1,0:T(8,128)(2,1)S(1)} %collective-permute-done.15.refs_2_), channel_id=1, source_target_pairs={{0,4},{4,0},{8,12},{12,8},{16,20},{20,16},{24,28},{28,24},{1,5},{5... | collective-permute-start | bytes 393224 | tf_op jit(solution)/shard_map/ppermute | solution.py:114
  72.2 1.3 %collective-permute-start.18 = (bf16[128,512]{1,0:T(8,128)(2,1)S(1)}, bf16[128,512]{1,0:T(8,128)(2,1)S(1)}, u32[]{:S(2)}, u32[]{:S(2)}) collective-permute-start(bf16[128,512]{1,0:T(8,128)(2,1)S(1)} %collective-permute-done.14.refs_1_), channel_id=1, source_target_pairs={{0,4},{4,0},{8,12},{12,8},{16,20},{20,16},{24,28},{28,24},{1,5},{5... | collective-permute-start | bytes 393224 | tf_op jit(solution)/shard_map/ppermute | solution.py:114
  76.5 2.5 %collective-permute-start.21 = (bf16[4,128,512]{2,1,0:T(8,128)(2,1)S(1)}, bf16[4,128,512]{2,1,0:T(8,128)(2,1)S(1)}, u32[]{:S(2)}, u32[]{:S(2)}) collective-permute-start(bf16[4,128,512]{2,1,0:T(8,128)(2,1)S(1)} %get-tuple-element.20), channel_id=1, source_target_pairs={{0,4},{4,0},{8,12},{12,8},{16,20},{20,16},{24,28},{28,24},{1,5},{5... | collective-permute-start | bytes 1572872 | tf_op jit(solution)/shard_map/ppermute | solution.py:114
  79.1 6.4 %collective-permute-start.22 = (bf16[128,512]{1,0:T(8,128)(2,1)S(1)}, bf16[128,512]{1,0:T(8,128)(2,1)S(1)}, u32[]{:S(2)}, u32[]{:S(2)}) collective-permute-start(bf16[128,512]{1,0:T(8,128)(2,1)S(1)} %get-tuple-element.22), channel_id=1, source_target_pairs={{0,8},{4,12},{8,0},{12,4},{16,24},{20,28},{24,16},{28,20},{1,9},{5... | collective-permute-start | bytes 393224 | tf_op jit(solution)/shard_map/ppermute | solution.py:114
  80.4 8.1 %collective-permute-start.24 = (bf16[128,512]{1,0:T(8,128)(2,1)S(1)}, bf16[128,512]{1,0:T(8,128)(2,1)S(1)}, u32[]{:S(2)}, u32[]{:S(2)}) collective-permute-start(bf16[128,512]{1,0:T(8,128)(2,1)S(1)} %get-tuple-element.23), channel_id=1, source_target_pairs={{0,16},{4,20},{8,24},{12,28},{16,0},{20,4},{24,8},{28,12},{1,17},{... | collective-permute-start | bytes 393224 | tf_op jit(solution)/shard_map/ppermute | solution.py:114
  81.2 7.3 %collective-permute-start.23 = (bf16[128,512]{1,0:T(8,128)(2,1)S(1)}, bf16[128,512]{1,0:T(8,128)(2,1)S(1)}, u32[]{:S(2)}, u32[]{:S(2)}) collective-permute-start(bf16[128,512]{1,0:T(8,128)(2,1)S(1)} %get-tuple-element.24), channel_id=1, source_target_pairs={{0,24},{4,28},{8,16},{12,20},{16,8},{20,12},{24,0},{28,4},{1,25},{... | collective-permute-start | bytes 393224 | tf_op jit(solution)/shard_map/ppermute | solution.py:114
  88.6 5.0 %collective-permute-start.25 = (bf16[128,512]{1,0:T(8,128)(2,1)S(1)}, bf16[128,512]{1,0:T(8,128)(2,1)S(1)}, u32[]{:S(2)}, u32[]{:S(2)}) collective-permute-start(bf16[128,512]{1,0:T(8,128)(2,1)S(1)} %fusion.2), channel_id=1, source_target_pairs={{0,1},{1,0},{2,3},{3,2},{4,5},{5,4},{6,7},{7,6},{8,9},{9,8},{10,11... | collective-permute-start | bytes 393224 | tf_op jit(solution)/shard_map/ppermute | solution.py:114
  93.7 6.9 %collective-permute-start.26 = (bf16[128,512]{1,0:T(8,128)(2,1)S(1)}, bf16[128,512]{1,0:T(8,128)(2,1)S(1)}, u32[]{:S(2)}, u32[]{:S(2)}) collective-permute-start(bf16[128,512]{1,0:T(8,128)(2,1)S(1)} %add_convert_fusion.2), channel_id=1, source_target_pairs={{0,3},{1,2},{2,1},{3,0},{4,7},{5,6},{6,5},{7,4},{8,11},{9,10},{10,... | collective-permute-start | bytes 393224 | tf_op jit(solution)/shard_map/ppermute | solution.py:114

commit v6 on v5

--- a/solution.py
+++ b/solution.py
@@ -28,7 +28,7 @@
                 prod_ref[share * per + j, :, m * levels:(m + 1) * levels] = product[j * blk:(j + 1) * blk]
 
 
-def local_sums(shares, cols_ref, ens_ref, mat_ref, prod_ref, out_ref):
+def local_sums(shares, cols_ref, ens_ref, mat_ref, prod_ref, outs):
     _, members, levels, width = ens_ref.shape
     slots, blk = cols_ref.shape[0], prod_ref.shape[1]
     per = width // blk
@@ -56,7 +56,7 @@
                 )
                 term = ens_ref[share, m].astype(F32) * local
                 total = term if total is None else total + term
-            out_ref[start + c] = total.astype(BF)
+            outs[start + c][...] = total.astype(BF)
 
 
 def sums_kernel(cores, turned, wanted, *refs):
@@ -75,9 +75,8 @@
         for core, some in zip(cores, field_refs):
             products(me, turn, core, ens_ref, some, prod_ref)
     copy.wait()
-    for out_ref, (core, chips) in zip(outs, wanted):
-        shares = [me ^ (2 * k + core) for k in chips]
-        local_sums(shares, cols_ref, ens_ref, mat_ref, prod_ref, out_ref)
+    places = [(me ^ (2 * k + core), out_ref.at[i]) for out_ref, (core, some) in zip(outs, wanted) for i, k in enumerate(some)]
+    local_sums([share for share, _ in places], cols_ref, ens_ref, mat_ref, prod_ref, [out for _, out in places])
 
 
 def products_kernel(ens_ref, *refs):
@@ -86,6 +85,21 @@
 
 def copy_kernel(x_ref, out_ref):
     out_ref[...] = x_ref[...].astype(out_ref.dtype)
+
+
+def sum_kernel(*refs):
+    total = refs[0][...].astype(F32)
+    for x_ref in refs[1:-1]:
+        total = total + x_ref[...].astype(F32)
+    refs[-1][...] = total
+
+
+def added(arrays):
+    return pl.pallas_call(
+        sum_kernel, out_shape=jax.ShapeDtypeStruct(arrays[0].shape, F32), in_specs=[VMEM] * len(arrays),
+        out_specs=VMEM, compiler_params=PARAMS,
+        cost_estimate=pl.CostEstimate(flops=HOLD // 10, bytes_accessed=0, transcendentals=0),
+    )(*arrays)
 
 
 def passed_on(x):
@@ -150,16 +164,14 @@
         return total
 
     def cov_sum(turned, fields, prod=None):
-        mate, prod = local(turned, [(1, far + [0])], prod=prod, fields=fields)
+        mate, prod = local(turned, [(1, far)], prod=prod, fields=fields)
         got = to_mate(mate)
         (own,) = local(turned, [(0, far)], prod=prod)
-        chip = (own.astype(F32) + got[:-1].astype(F32)).astype(BF)
-        arrived = [xor_permute(chip[i], "pts", 2 * k) for i, k in enumerate(far)]
+        chip = (own.astype(F32) + got.astype(F32)).astype(BF)
+        arrived = [xor_permute(chip[far.index(k)], "pts", 2 * k) for k in sorted(far, reverse=True)]
         prod, _ = lax.optimization_barrier((prod, chip))
-        (own,) = local(turned, [(0, [0])], prod=prod)
-        total = own[0].astype(F32) + got[-1].astype(F32)
-        for a in arrived:
-            total = total + a.astype(F32)
+        mate, own = local(turned, [(1, [0]), (0, [0])], prod=prod)
+        total = added(arrived) + (own[0].astype(F32) + to_mate(mate)[0].astype(F32))
         return sum_over_mem(total)
 
     rounded = increment.astype(BF)

time: 102 us -> 101 us (level)
    ppermute x26 -> x28, waiting for transfers between devices: 35 us -> 34.1 us  [xor_permute(): lax.ppermute(x, axis, [(i, i ^ k) for i in range(lax.axis_size(axis))])]
    ppermute x26 -> x28, starting transfers between devices: 35.8 us -> 36 us  [xor_permute(): lax.ppermute(x, axis, [(i, i ^ k) for i in range(lax.axis_size(axis))])]
  transfers between devices with their start and end apart: 28 -> 30, of which waited for: 18 -> 18; matrix products, arithmetic and copies ran while one was open for 1% -> 1% of each run, Pallas kernels for 8% -> 9%
where the time goes in v6:
time: 101 us; the launch traced here: 100 us
  starting transfers between devices  42.7 us (42%)
  waiting for transfers between devices  39.5 us (39%)
  Pallas kernels  13.7 us (14%)
  other arithmetic  1.91 us (2%)
  local copies, waits for them, and re-layouts  1.64 us (2%)
    ppermute x28, starting transfers between devices, xor_permute(): lax.ppermute(x, axis, [(i, i ^ k) for i in range(lax.axis_size(axis))])  36 us
    ppermute x28, waiting for transfers between devices, xor_permute(): lax.ppermute(x, axis, [(i, i ^ k) for i in range(lax.axis_size(axis))])  34.1 us
    pallas_call x6, Pallas kernels, local(): pl.pallas_call(functools.partial(sums_kernel, cores, turned, wanted), out...  13.2 us
    all_to_all x1, waiting for transfers between devices, per_device(): lax.all_to_all(ensemble.reshape(pts, share, levels, width), 'pts', split_...  5.4 us
    all_to_all x1, starting transfers between devices, per_device(): lax.all_to_all(ensemble.reshape(pts, share, levels, width), 'pts', split_...  5.17 us
  transfers between devices with their start and end apart: 30, of which 18 were waited for; matrix products, arithmetic and copies ran while one was open for 1% of the time, Pallas kernels for 9%

profile of v6, /device:TPU:0, one launch (start us, length us, event | category | flops | bytes accessed | tf_op | source)
XLA Modules:
  0.0 100.3 jit_solution(32522576983016778)
XLA Ops:
  0.6 1.6 %collective-permute-start = (f32[128,512]{1,0:T(8,128)}, f32[128,512]{1,0:T(8,128)S(1)}, u32[]{:S(2)}, u32[]{:S(2)}) collective-permute-start(f32[128,512]{1,0:T(8,128)} %param.7), channel_id=1, source_target_pairs={{0,0},{1,9},{2,18},{3,27},{4,4},{5,13},{6,22},{7,31},{8,8},{9,1},{... | collective-permute-start | bytes 786440 | tf_op jit(solution)/shard_map/ppermute | solution.py:181
  2.2 5.2 %all-to-all-start = ((bf16[8,2,128,512]{3,2,1,0:T(8,128)(2,1)}), bf16[8,2,128,512]{3,2,1,0:T(8,128)(2,1)S(1)}, u32[]{:S(2)}, u32[]{:S(2)}) async-start(bf16[8,2,128,512]{3,2,1,0:T(8,128)(2,1)} %bitcast.29), calls=%async_computation | async-start | bytes 4194304 | tf_op jit(solution)/shard_map/all_to_all | solution.py:187
  7.4 0.0 copy-start.5
  7.4 0.0 copy-start.2
  7.5 9.6 %collective-permute-start.3 = (bf16[128,512]{1,0:T(8,128)(2,1)S(1)}, bf16[128,512]{1,0:T(8,128)(2,1)S(1)}, u32[]{:S(2)}, u32[]{:S(2)}) collective-permute-start(bf16[128,512]{1,0:T(8,128)(2,1)S(1)} %shard_map.77.refs_3_), channel_id=1, source_target_pairs={{0,3},{1,2},{2,1},{3,0},{4,7},{5,6},{6,5},{7,4},{8,11},{9,10},{10,... | collective-permute-start | bytes 393224 | tf_op jit(solution)/shard_map/ppermute | solution.py:128
  17.1 0.0 collective-permute-start.2
  17.1 0.6 collective-permute-start.1
  17.8 0.1 collective-permute-start.4
  17.8 3.7 %collective-permute-done.3.refs_6_ = bf16[128,512]{1,0:T(8,128)(2,1)S(1)} collective-permute-done((bf16[128,512]{1,0:T(8,128)(2,1)S(1)}, bf16[128,512]{1,0:T(8,128)(2,1)S(1)}, u32[]{:S(2)}, u32[]{:S(2)}) %collective-permute-start.3) | collective-permute-done | bytes 131104 | tf_op jit(solution)/shard_map/ppermute | solution.py:128
  21.5 4.9 %collective-permute-done.2.refs_5_ = bf16[128,512]{1,0:T(8,128)(2,1)S(1)} collective-permute-done((bf16[128,512]{1,0:T(8,128)(2,1)S(1)}, bf16[128,512]{1,0:T(8,128)(2,1)S(1)}, u32[]{:S(2)}, u32[]{:S(2)}) %collective-permute-start.2) | collective-permute-done | bytes 131104 | tf_op jit(solution)/shard_map/ppermute | solution.py:128
  26.5 0.0 collective-permute-start.6
  26.5 0.0 collective-permute-done.1.refs_4_
  26.5 0.5 collective-permute-start.5
  27.0 0.0 collective-permute-done.4.refs_7_
  27.0 0.0 collective-permute-done.7.refs_10_
  27.0 0.8 collective-permute-done.6.refs_9_
  27.8 0.2 collective-permute-done.5.refs_8_
  28.0 0.7 copy-done
  28.7 5.4 %all-to-all-done.refs_1_.ens_ref = bf16[8,2,128,512]{3,2,1,0:T(8,128)(2,1)S(1)} async-done(((bf16[8,2,128,512]{3,2,1,0:T(8,128)(2,1)}), bf16[8,2,128,512]{3,2,1,0:T(8,128)(2,1)S(1)}, u32[]{:S(2)}, u32[]{:S(2)}) %all-to-all-start) | async-done | bytes 2097184 | tf_op jit(solution)/shard_map/all_to_all | solution.py:187
  34.1 0.9 copy-done.1
  35.0 2.8 %shard_map.78 = (bf16[3,128,512]{2,1,0:T(8,128)(2,1)S(1)}, bf16[32,128,256]{2,1,0:T(8,128)(2,1)S(1)}) custom-call(s32[12,32]{1,0:T(8,128)S(1)} %bitcast.23, bf16[8,2,128,512]{3,2,1,0:T(8,128)(2,1)S(1)} %all-to-all-done.refs_1_.ens_ref, bf16[1664,128]{1,0:T(8,128)(2,1)S(1)} %pad_maximum_fusion.refs_2_, bf16[128,512]{1,0:T(8,128)(2,1)S(1)} %shard_map.77.refs_3_, ...), custom_call_target="tpu_custom_call" | custom-call | flops 4831838208 | tf_op jit(solution)/shard_map/pallas_call | solution.py:141
  37.7 0.1 collective-permute-start.8
  37.8 2.3 %shard_map.79 = bf16[3,128,512]{2,1,0:T(8,128)(2,1)S(1)} custom-call(s32[12,32]{1,0:T(8,128)S(1)} %bitcast.24, bf16[8,2,128,512]{3,2,1,0:T(8,128)(2,1)S(1)} %all-to-all-done.refs_1_.ens_ref, bf16[1664,128]{1,0:T(8,128)(2,1)S(1)} %pad_maximum_fusion.refs_2_, bf16[32,128,256]{2,1,0:T(8,128)(2,1)S(1)} %get-tuple-element.20.refs_3_), custom_call_target="tpu_custom_call" | custom-call | flops 4831838208 | tf_op jit(solution)/shard_map/pallas_call | solution.py:141
  40.1 0.0 collective-permute-done.8
  40.1 0.1 add_convert_fusion.1
  40.2 0.6 collective-permute-start.11
  40.9 0.6 collective-permute-start.10
  41.4 2.3 %collective-permute-start.9 = (bf16[128,512]{1,0:T(8,128)(2,1)S(1)}, bf16[128,512]{1,0:T(8,128)(2,1)S(1)}, u32[]{:S(2)}, u32[]{:S(2)}) collective-permute-start(bf16[128,512]{1,0:T(8,128)(2,1)S(1)} %get-tuple-element.35), channel_id=1, source_target_pairs={{0,24},{4,28},{8,16},{12,20},{16,8},{20,12},{24,0},{28,4},{1,25},{... | collective-permute-start | bytes 393224 | tf_op jit(solution)/shard_map/ppermute | solution.py:128
  43.8 1.8 %shard_map.81 = (bf16[1,128,512]{2,1,0:T(8,128)(2,1)S(1)}, bf16[1,128,512]{2,1,0:T(8,128)(2,1)S(1)}) custom-call(s32[12,32]{1,0:T(8,128)S(1)} %bitcast.25, bf16[8,2,128,512]{3,2,1,0:T(8,128)(2,1)S(1)} %all-to-all-done.refs_1_.ens_ref, bf16[1664,128]{1,0:T(8,128)(2,1)S(1)} %pad_maximum_fusion.refs_2_, bf16[32,128,256]{2,1,0:T(8,128)(2,1)S(1)} %get-tuple-element.20.refs_3_), custom_call_target="tpu_custom_call" | custom-call | flops 3221225472 | tf_op jit(solution)/shard_map/pallas_call | solution.py:141
  45.6 0.0 copy-start.3
  45.6 0.1 collective-permute-start.12
  45.7 0.9 collective-permute-done.11.refs_2_
  46.6 2.7 %collective-permute-done.10.refs_1_ = bf16[128,512]{1,0:T(8,128)(2,1)S(1)} collective-permute-done((bf16[128,512]{1,0:T(8,128)(2,1)S(1)}, bf16[128,512]{1,0:T(8,128)(2,1)S(1)}, u32[]{:S(2)}, u32[]{:S(2)}) %collective-permute-start.10) | collective-permute-done | bytes 131104 | tf_op jit(solution)/shard_map/ppermute | solution.py:128
  49.2 0.0 collective-permute-done.9.refs_0_
  49.4 3.3 %collective-permute-start.13 = (bf16[128,512]{1,0:T(8,128)(2,1)S(1)}, bf16[128,512]{1,0:T(8,128)(2,1)S(1)}, u32[]{:S(2)}, u32[]{:S(2)}) collective-permute-start(bf16[128,512]{1,0:T(8,128)(2,1)S(1)} %fusion.1), channel_id=1, source_target_pairs={{0,1},{1,0},{2,3},{3,2},{4,5},{5,4},{6,7},{7,6},{8,9},{9,8},{10,11... | collective-permute-start | bytes 393224 | tf_op jit(solution)/shard_map/ppermute | solution.py:128
  52.7 2.9 %collective-permute-done.13 = bf16[128,512]{1,0:T(8,128)(2,1)S(1)} collective-permute-done((bf16[128,512]{1,0:T(8,128)(2,1)S(1)}, bf16[128,512]{1,0:T(8,128)(2,1)S(1)}, u32[]{:S(2)}, u32[]{:S(2)}) %collective-permute-start.13) | collective-permute-done | bytes 131104 | tf_op jit(solution)/shard_map/ppermute | solution.py:128
  55.7 5.1 %collective-permute-start.14 = (bf16[128,512]{1,0:T(8,128)(2,1)S(1)}, bf16[128,512]{1,0:T(8,128)(2,1)S(1)}, u32[]{:S(2)}, u32[]{:S(2)}) collective-permute-start(bf16[128,512]{1,0:T(8,128)(2,1)S(1)} %add_convert_fusion.3), channel_id=1, source_target_pairs={{0,3},{1,2},{2,1},{3,0},{4,7},{5,6},{6,5},{7,4},{8,11},{9,10},{10,... | collective-permute-start | bytes 393224 | tf_op jit(solution)/shard_map/ppermute | solution.py:128
  60.7 3.1 %collective-permute-done.14 = bf16[128,512]{1,0:T(8,128)(2,1)S(1)} collective-permute-done((bf16[128,512]{1,0:T(8,128)(2,1)S(1)}, bf16[128,512]{1,0:T(8,128)(2,1)S(1)}, u32[]{:S(2)}, u32[]{:S(2)}) %collective-permute-start.14) | collective-permute-done | bytes 131104 | tf_op jit(solution)/shard_map/ppermute | solution.py:128
  63.9 1.4 %collective-permute-start.17 = (bf16[128,512]{1,0:T(8,128)(2,1)S(1)}, bf16[128,512]{1,0:T(8,128)(2,1)S(1)}, u32[]{:S(2)}, u32[]{:S(2)}) collective-permute-start(bf16[128,512]{1,0:T(8,128)(2,1)S(1)} %get-tuple-element.36.refs_0_), channel_id=1, source_target_pairs={{0,24},{4,28},{8,16},{12,20},{16,8},{20,12},{24,0},{28,4},{1,25},{... | collective-permute-start | bytes 393224 | tf_op jit(solution)/shard_map/ppermute | solution.py:128
  65.3 1.5 %collective-permute-start.16 = (bf16[128,512]{1,0:T(8,128)(2,1)S(1)}, bf16[128,512]{1,0:T(8,128)(2,1)S(1)}, u32[]{:S(2)}, u32[]{:S(2)}) collective-permute-start(bf16[128,512]{1,0:T(8,128)(2,1)S(1)} %get-tuple-element.36.refs_0_), channel_id=1, source_target_pairs={{0,16},{4,20},{8,24},{12,28},{16,0},{20,4},{24,8},{28,12},{1,17},{... | collective-permute-start | bytes 393224 | tf_op jit(solution)/shard_map/ppermute | solution.py:128
  66.8 0.6 collective-permute-start.15
  67.4 2.5 %collective-permute-done.17.refs_3_ = bf16[128,512]{1,0:T(8,128)(2,1)S(1)} collective-permute-done((bf16[128,512]{1,0:T(8,128)(2,1)S(1)}, bf16[128,512]{1,0:T(8,128)(2,1)S(1)}, u32[]{:S(2)}, u32[]{:S(2)}) %collective-permute-start.17) | collective-permute-done | bytes 131104 | tf_op jit(solution)/shard_map/ppermute | solution.py:128
  69.9 1.3 %collective-permute-done.16.refs_2_ = bf16[128,512]{1,0:T(8,128)(2,1)S(1)} collective-permute-done((bf16[128,512]{1,0:T(8,128)(2,1)S(1)}, bf16[128,512]{1,0:T(8,128)(2,1)S(1)}, u32[]{:S(2)}, u32[]{:S(2)}) %collective-permute-start.16) | collective-permute-done | bytes 131104 | tf_op jit(solution)/shard_map/ppermute | solution.py:128
  71.2 0.6 collective-permute-done.15.refs_1_
  71.8 0.3 shard_map.82.refs_7_
  72.1 0.4 collective-permute-done.20.refs_5_
  72.5 0.6 collective-permute-done.19.refs_4_
  73.1 2.3 %shard_map.83 = (bf16[3,128,512]{2,1,0:T(8,128)(2,1)S(1)}, bf16[32,128,256]{2,1,0:T(8,128)(2,1)S(1)}) custom-call(s32[12,32]{1,0:T(8,128)S(1)} %bitcast.26, bf16[8,2,128,512]{3,2,1,0:T(8,128)(2,1)S(1)} %all-to-all-done.refs_1_.ens_ref, bf16[1664,128]{1,0:T(8,128)(2,1)S(1)} %pad_maximum_fusion.refs_2_, ...), custom_call_target="tpu_custom_call", output_to_operand_aliasing={{1}: (7, {})} | custom-call | flops 4831838208 | tf_op jit(solution)/shard_map/pallas_call | solution.py:141
  75.4 0.2 collective-permute-start.22
  75.6 2.3 %shard_map.84 = bf16[3,128,512]{2,1,0:T(8,128)(2,1)S(1)} custom-call(s32[12,32]{1,0:T(8,128)S(1)} %bitcast.27, bf16[8,2,128,512]{3,2,1,0:T(8,128)(2,1)S(1)} %all-to-all-done.refs_1_.ens_ref, bf16[1664,128]{1,0:T(8,128)(2,1)S(1)} %pad_maximum_fusion.refs_2_, bf16[32,128,256]{2,1,0:T(8,128)(2,1)S(1)} %get-tuple-element.27.refs_3_), custom_call_target="tpu_custom_call" | custom-call | flops 4831838208 | tf_op jit(solution)/shard_map/pallas_call | solution.py:141
  77.9 0.1 add_convert_fusion
  78.0 1.3 %collective-permute-start.25 = (bf16[128,512]{1,0:T(8,128)(2,1)S(1)}, bf16[128,512]{1,0:T(8,128)(2,1)S(1)}, u32[]{:S(2)}, u32[]{:S(2)}) collective-permute-start(bf16[128,512]{1,0:T(8,128)(2,1)S(1)} %get-tuple-element.30), channel_id=1, source_target_pairs={{0,8},{4,12},{8,0},{12,4},{16,24},{20,28},{24,16},{28,20},{1,9},{5... | collective-permute-start | bytes 393224 | tf_op jit(solution)/shard_map/ppermute | solution.py:128
  79.3 0.8 collective-permute-start.24
  80.1 1.5 %collective-permute-start.23 = (bf16[128,512]{1,0:T(8,128)(2,1)S(1)}, bf16[128,512]{1,0:T(8,128)(2,1)S(1)}, u32[]{:S(2)}, u32[]{:S(2)}) collective-permute-start(bf16[128,512]{1,0:T(8,128)(2,1)S(1)} %get-tuple-element.32), channel_id=1, source_target_pairs={{0,24},{4,28},{8,16},{12,20},{16,8},{20,12},{24,0},{28,4},{1,25},{... | collective-permute-start | bytes 393224 | tf_op jit(solution)/shard_map/ppermute | solution.py:128
  81.6 1.8 %shard_map.86 = (bf16[1,128,512]{2,1,0:T(8,128)(2,1)S(1)}, bf16[1,128,512]{2,1,0:T(8,128)(2,1)S(1)}) custom-call(s32[12,32]{1,0:T(8,128)S(1)} %bitcast.28, bf16[8,2,128,512]{3,2,1,0:T(8,128)(2,1)S(1)} %all-to-all-done.refs_1_.ens_ref, bf16[1664,128]{1,0:T(8,128)(2,1)S(1)} %pad_maximum_fusion.refs_2_, bf16[32,128,256]{2,1,0:T(8,128)(2,1)S(1)} %get-tuple-element.27.refs_3_), custom_call_target="tpu_custom_call" | custom-call | flops 3221225472 | tf_op jit(solution)/shard_map/pallas_call | solution.py:141
  83.4 0.1 collective-permute-start.26
  83.5 0.9 collective-permute-done.25.refs_2_
  84.4 3.0 %collective-permute-done.24.refs_1_ = bf16[128,512]{1,0:T(8,128)(2,1)S(1)} collective-permute-done((bf16[128,512]{1,0:T(8,128)(2,1)S(1)}, bf16[128,512]{1,0:T(8,128)(2,1)S(1)}, u32[]{:S(2)}, u32[]{:S(2)}) %collective-permute-start.24) | collective-permute-done | bytes 131104 | tf_op jit(solution)/shard_map/ppermute | solution.py:128
  87.5 1.8 %collective-permute-start.27 = (bf16[128,512]{1,0:T(8,128)(2,1)S(1)}, bf16[128,512]{1,0:T(8,128)(2,1)S(1)}, u32[]{:S(2)}, u32[]{:S(2)}) collective-permute-start(bf16[128,512]{1,0:T(8,128)(2,1)S(1)} %fusion), channel_id=1, source_target_pairs={{0,1},{1,0},{2,3},{3,2},{4,5},{5,4},{6,7},{7,6},{8,9},{9,8},{10,11... | collective-permute-start | bytes 393224 | tf_op jit(solution)/shard_map/ppermute | solution.py:128
  89.3 3.3 %collective-permute-done.27 = bf16[128,512]{1,0:T(8,128)(2,1)S(1)} collective-permute-done((bf16[128,512]{1,0:T(8,128)(2,1)S(1)}, bf16[128,512]{1,0:T(8,128)(2,1)S(1)}, u32[]{:S(2)}, u32[]{:S(2)}) %collective-permute-start.27) | collective-permute-done | bytes 131104 | tf_op jit(solution)/shard_map/ppermute | solution.py:128
  92.6 3.8 %collective-permute-start.28 = (bf16[128,512]{1,0:T(8,128)(2,1)S(1)}, bf16[128,512]{1,0:T(8,128)(2,1)S(1)}, u32[]{:S(2)}, u32[]{:S(2)}) collective-permute-start(bf16[128,512]{1,0:T(8,128)(2,1)S(1)} %add_convert_fusion.2), channel_id=1, source_target_pairs={{0,3},{1,2},{2,1},{3,0},{4,7},{5,6},{6,5},{7,4},{8,11},{9,10},{10,... | collective-permute-start | bytes 393224 | tf_op jit(solution)/shard_map/ppermute | solution.py:128
  96.4 0.7 mul.7
  97.2 2.4 %collective-permute-done.28 = bf16[128,512]{1,0:T(8,128)(2,1)S(1)} collective-permute-done((bf16[128,512]{1,0:T(8,128)(2,1)S(1)}, bf16[128,512]{1,0:T(8,128)(2,1)S(1)}, u32[]{:S(2)}, u32[]{:S(2)}) %collective-permute-start.28) | collective-permute-done | bytes 131104 | tf_op jit(solution)/shard_map/ppermute | solution.py:128
  99.6 0.7 convert_add_fusion
  (30 shorter events, 0.4 us)
Async XLA Ops:
  0.6 6.8 %collective-permute-start = (f32[128,512]{1,0:T(8,128)}, f32[128,512]{1,0:T(8,128)S(1)}, u32[]{:S(2)}, u32[]{:S(2)}) collective-permute-start(f32[128,512]{1,0:T(8,128)} %param.7), channel_id=1, source_target_pairs={{0,0},{1,9},{2,18},{3,27},{4,4},{5,13},{6,22},{7,31},{8,8},{9,1},{... | collective-permute-start | bytes 786440 | tf_op jit(solution)/shard_map/ppermute | solution.py:181
  2.2 31.8 %all-to-all-start = ((bf16[8,2,128,512]{3,2,1,0:T(8,128)(2,1)}), bf16[8,2,128,512]{3,2,1,0:T(8,128)(2,1)S(1)}, u32[]{:S(2)}, u32[]{:S(2)}) async-start(bf16[8,2,128,512]{3,2,1,0:T(8,128)(2,1)} %bitcast.29), calls=%async_computation | async-start | bytes 4194304 | tf_op jit(solution)/shard_map/all_to_all | solution.py:187
  7.4 10.3 %copy-start.4 = (bf16[12,128,128]{2,1,0:T(8,128)(2,1)S(1)}, bf16[12,128,128]{2,1,0:T(8,128)(2,1)}, u32[]{:S(2)}) copy-start(bf16[12,128,128]{2,1,0:T(8,128)(2,1)} %param.10) | copy-start | bytes 1179652
  7.4 10.3 %copy-start.5 = (bf16[128,128]{1,0:T(8,128)(2,1)S(1)}, bf16[128,128]{1,0:T(8,128)(2,1)}, u32[]{:S(2)}) copy-start(bf16[128,128]{1,0:T(8,128)(2,1)} %param.9) | copy-start | bytes 98308
  7.4 26.6 %copy-start.2 = (s32[32,12]{0,1:T(8,128)S(1)}, s32[32,12]{0,1:T(8,128)}, u32[]{:S(2)}) copy-start(s32[32,12]{0,1:T(8,128)} %param.11) | copy-start | bytes 4612
  7.5 14.1 %collective-permute-start.3 = (bf16[128,512]{1,0:T(8,128)(2,1)S(1)}, bf16[128,512]{1,0:T(8,128)(2,1)S(1)}, u32[]{:S(2)}, u32[]{:S(2)}) collective-permute-start(bf16[128,512]{1,0:T(8,128)(2,1)S(1)} %shard_map.77.refs_3_), channel_id=1, source_target_pairs={{0,3},{1,2},{2,1},{3,0},{4,7},{5,6},{6,5},{7,4},{8,11},{9,10},{10,... | collective-permute-start | bytes 393224 | tf_op jit(solution)/shard_map/ppermute | solution.py:128
  17.1 9.4 %collective-permute-start.2 = (bf16[128,512]{1,0:T(8,128)(2,1)S(1)}, bf16[128,512]{1,0:T(8,128)(2,1)S(1)}, u32[]{:S(2)}, u32[]{:S(2)}) collective-permute-start(bf16[128,512]{1,0:T(8,128)(2,1)S(1)} %shard_map.77.refs_3_), channel_id=1, source_target_pairs={{0,2},{1,3},{2,0},{3,1},{4,6},{5,7},{6,4},{7,5},{8,10},{9,11},{10,... | collective-permute-start | bytes 393224 | tf_op jit(solution)/shard_map/ppermute | solution.py:128
  17.1 9.4 %collective-permute-start.1 = (bf16[128,512]{1,0:T(8,128)(2,1)S(1)}, bf16[128,512]{1,0:T(8,128)(2,1)S(1)}, u32[]{:S(2)}, u32[]{:S(2)}) collective-permute-start(bf16[128,512]{1,0:T(8,128)(2,1)S(1)} %shard_map.77.refs_3_), channel_id=1, source_target_pairs={{0,1},{1,0},{2,3},{3,2},{4,5},{5,4},{6,7},{7,6},{8,9},{9,8},{10,11... | collective-permute-start | bytes 393224 | tf_op jit(solution)/shard_map/ppermute | solution.py:128
  17.8 9.2 %collective-permute-start.4 = (bf16[128,512]{1,0:T(8,128)(2,1)S(1)}, bf16[128,512]{1,0:T(8,128)(2,1)S(1)}, u32[]{:S(2)}, u32[]{:S(2)}) collective-permute-start(bf16[128,512]{1,0:T(8,128)(2,1)S(1)} %shard_map.77.refs_3_), channel_id=1, source_target_pairs={{0,4},{4,0},{8,12},{12,8},{16,20},{20,16},{24,28},{28,24},{1,5},{5... | collective-permute-start | bytes 393224 | tf_op jit(solution)/shard_map/ppermute | solution.py:128
  21.5 5.4 %collective-permute-start.7 = (bf16[128,512]{1,0:T(8,128)(2,1)S(1)}, bf16[128,512]{1,0:T(8,128)(2,1)S(1)}, u32[]{:S(2)}, u32[]{:S(2)}) collective-permute-start(bf16[128,512]{1,0:T(8,128)(2,1)S(1)} %collective-permute-done.3.refs_6_), channel_id=1, source_target_pairs={{0,4},{4,0},{8,12},{12,8},{16,20},{20,16},{24,28},{28,24},{1,5},{5... | collective-permute-start | bytes 393224 | tf_op jit(solution)/shard_map/ppermute | solution.py:128
  26.5 1.3 %collective-permute-start.6 = (bf16[128,512]{1,0:T(8,128)(2,1)S(1)}, bf16[128,512]{1,0:T(8,128)(2,1)S(1)}, u32[]{:S(2)}, u32[]{:S(2)}) collective-permute-start(bf16[128,512]{1,0:T(8,128)(2,1)S(1)} %collective-permute-done.2.refs_5_), channel_id=1, source_target_pairs={{0,4},{4,0},{8,12},{12,8},{16,20},{20,16},{24,28},{28,24},{1,5},{5... | collective-permute-start | bytes 393224 | tf_op jit(solution)/shard_map/ppermute | solution.py:128
  26.5 1.5 %collective-permute-start.5 = (bf16[128,512]{1,0:T(8,128)(2,1)S(1)}, bf16[128,512]{1,0:T(8,128)(2,1)S(1)}, u32[]{:S(2)}, u32[]{:S(2)}) collective-permute-start(bf16[128,512]{1,0:T(8,128)(2,1)S(1)} %collective-permute-done.1.refs_4_), channel_id=1, source_target_pairs={{0,4},{4,0},{8,12},{12,8},{16,20},{20,16},{24,28},{28,24},{1,5},{5... | collective-permute-start | bytes 393224 | tf_op jit(solution)/shard_map/ppermute | solution.py:128
  28.0 0.7 copy-start
  34.1 0.9 copy-start.1
  37.7 2.4 %collective-permute-start.8 = (bf16[3,128,512]{2,1,0:T(8,128)(2,1)S(1)}, bf16[3,128,512]{2,1,0:T(8,128)(2,1)S(1)}, u32[]{:S(2)}, u32[]{:S(2)}) collective-permute-start(bf16[3,128,512]{2,1,0:T(8,128)(2,1)S(1)} %get-tuple-element.19), channel_id=1, source_target_pairs={{0,4},{4,0},{8,12},{12,8},{16,20},{20,16},{24,28},{28,24},{1,5},{5... | collective-permute-start | bytes 1179656 | tf_op jit(solution)/shard_map/ppermute | solution.py:128
  40.2 6.4 %collective-permute-start.11 = (bf16[128,512]{1,0:T(8,128)(2,1)S(1)}, bf16[128,512]{1,0:T(8,128)(2,1)S(1)}, u32[]{:S(2)}, u32[]{:S(2)}) collective-permute-start(bf16[128,512]{1,0:T(8,128)(2,1)S(1)} %get-tuple-element.33), channel_id=1, source_target_pairs={{0,8},{4,12},{8,0},{12,4},{16,24},{20,28},{24,16},{28,20},{1,9},{5... | collective-permute-start | bytes 393224 | tf_op jit(solution)/shard_map/ppermute | solution.py:128
  40.9 8.4 %collective-permute-start.10 = (bf16[128,512]{1,0:T(8,128)(2,1)S(1)}, bf16[128,512]{1,0:T(8,128)(2,1)S(1)}, u32[]{:S(2)}, u32[]{:S(2)}) collective-permute-start(bf16[128,512]{1,0:T(8,128)(2,1)S(1)} %get-tuple-element.34), channel_id=1, source_target_pairs={{0,16},{4,20},{8,24},{12,28},{16,0},{20,4},{24,8},{28,12},{1,17},{... | collective-permute-start | bytes 393224 | tf_op jit(solution)/shard_map/ppermute | solution.py:128
  41.4 7.8 %collective-permute-start.9 = (bf16[128,512]{1,0:T(8,128)(2,1)S(1)}, bf16[128,512]{1,0:T(8,128)(2,1)S(1)}, u32[]{:S(2)}, u32[]{:S(2)}) collective-permute-start(bf16[128,512]{1,0:T(8,128)(2,1)S(1)} %get-tuple-element.35), channel_id=1, source_target_pairs={{0,24},{4,28},{8,16},{12,20},{16,8},{20,12},{24,0},{28,4},{1,25},{... | collective-permute-start | bytes 393224 | tf_op jit(solution)/shard_map/ppermute | solution.py:128
  45.6 18.2 %copy-start.3 = (f32[128,512]{1,0:T(8,128)S(1)}, f32[128,512]{1,0:T(8,128)}, u32[]{:S(2)}) copy-start(f32[128,512]{1,0:T(8,128)} %param.8) | copy-start | bytes 786436
  45.6 3.7 %collective-permute-start.12 = (bf16[1,128,512]{2,1,0:T(8,128)(2,1)S(1)}, bf16[1,128,512]{2,1,0:T(8,128)(2,1)S(1)}, u32[]{:S(2)}, u32[]{:S(2)}) collective-permute-start(bf16[1,128,512]{2,1,0:T(8,128)(2,1)S(1)} %get-tuple-element.22), channel_id=1, source_target_pairs={{0,4},{4,0},{8,12},{12,8},{16,20},{20,16},{24,28},{28,24},{1,5},{5... | collective-permute-start | bytes 393224 | tf_op jit(solution)/shard_map/ppermute | solution.py:128
  49.4 6.3 %collective-permute-start.13 = (bf16[128,512]{1,0:T(8,128)(2,1)S(1)}, bf16[128,512]{1,0:T(8,128)(2,1)S(1)}, u32[]{:S(2)}, u32[]{:S(2)}) collective-permute-start(bf16[128,512]{1,0:T(8,128)(2,1)S(1)} %fusion.1), channel_id=1, source_target_pairs={{0,1},{1,0},{2,3},{3,2},{4,5},{5,4},{6,7},{7,6},{8,9},{9,8},{10,11... | collective-permute-start | bytes 393224 | tf_op jit(solution)/shard_map/ppermute | solution.py:128
  55.7 8.1 %collective-permute-start.14 = (bf16[128,512]{1,0:T(8,128)(2,1)S(1)}, bf16[128,512]{1,0:T(8,128)(2,1)S(1)}, u32[]{:S(2)}, u32[]{:S(2)}) collective-permute-start(bf16[128,512]{1,0:T(8,128)(2,1)S(1)} %add_convert_fusion.3), channel_id=1, source_target_pairs={{0,3},{1,2},{2,1},{3,0},{4,7},{5,6},{6,5},{7,4},{8,11},{9,10},{10,... | collective-permute-start | bytes 393224 | tf_op jit(solution)/shard_map/ppermute | solution.py:128
  63.9 6.0 %collective-permute-start.17 = (bf16[128,512]{1,0:T(8,128)(2,1)S(1)}, bf16[128,512]{1,0:T(8,128)(2,1)S(1)}, u32[]{:S(2)}, u32[]{:S(2)}) collective-permute-start(bf16[128,512]{1,0:T(8,128)(2,1)S(1)} %get-tuple-element.36.refs_0_), channel_id=1, source_target_pairs={{0,24},{4,28},{8,16},{12,20},{16,8},{20,12},{24,0},{28,4},{1,25},{... | collective-permute-start | bytes 393224 | tf_op jit(solution)/shard_map/ppermute | solution.py:128
  65.3 5.9 %collective-permute-start.16 = (bf16[128,512]{1,0:T(8,128)(2,1)S(1)}, bf16[128,512]{1,0:T(8,128)(2,1)S(1)}, u32[]{:S(2)}, u32[]{:S(2)}) collective-permute-start(bf16[128,512]{1,0:T(8,128)(2,1)S(1)} %get-tuple-element.36.refs_0_), channel_id=1, source_target_pairs={{0,16},{4,20},{8,24},{12,28},{16,0},{20,4},{24,8},{28,12},{1,17},{... | collective-permute-start | bytes 393224 | tf_op jit(solution)/shard_map/ppermute | solution.py:128
  66.8 5.0 %collective-permute-start.15 = (bf16[128,512]{1,0:T(8,128)(2,1)S(1)}, bf16[128,512]{1,0:T(8,128)(2,1)S(1)}, u32[]{:S(2)}, u32[]{:S(2)}) collective-permute-start(bf16[128,512]{1,0:T(8,128)(2,1)S(1)} %get-tuple-element.36.refs_0_), channel_id=1, source_target_pairs={{0,8},{4,12},{8,0},{12,4},{16,24},{20,28},{24,16},{28,20},{1,9},{5... | collective-permute-start | bytes 393224 | tf_op jit(solution)/shard_map/ppermute | solution.py:128
  67.4 4.7 %collective-permute-start.18 = (bf16[128,512]{1,0:T(8,128)(2,1)S(1)}, bf16[128,512]{1,0:T(8,128)(2,1)S(1)}, u32[]{:S(2)}, u32[]{:S(2)}) collective-permute-start(bf16[128,512]{1,0:T(8,128)(2,1)S(1)} %get-tuple-element.36.refs_0_), channel_id=1, source_target_pairs={{0,4},{4,0},{8,12},{12,8},{16,20},{20,16},{24,28},{28,24},{1,5},{5... | collective-permute-start | bytes 393224 | tf_op jit(solution)/shard_map/ppermute | solution.py:128
  69.9 2.2 %collective-permute-start.21 = (bf16[128,512]{1,0:T(8,128)(2,1)S(1)}, bf16[128,512]{1,0:T(8,128)(2,1)S(1)}, u32[]{:S(2)}, u32[]{:S(2)}) collective-permute-start(bf16[128,512]{1,0:T(8,128)(2,1)S(1)} %collective-permute-done.17.refs_3_), channel_id=1, source_target_pairs={{0,4},{4,0},{8,12},{12,8},{16,20},{20,16},{24,28},{28,24},{1,5},{5... | collective-permute-start | bytes 393224 | tf_op jit(solution)/shard_map/ppermute | solution.py:128
  71.2 1.3 %collective-permute-start.20 = (bf16[128,512]{1,0:T(8,128)(2,1)S(1)}, bf16[128,512]{1,0:T(8,128)(2,1)S(1)}, u32[]{:S(2)}, u32[]{:S(2)}) collective-permute-start(bf16[128,512]{1,0:T(8,128)(2,1)S(1)} %collective-permute-done.16.refs_2_), channel_id=1, source_target_pairs={{0,4},{4,0},{8,12},{12,8},{16,20},{20,16},{24,28},{28,24},{1,5},{5... | collective-permute-start | bytes 393224 | tf_op jit(solution)/shard_map/ppermute | solution.py:128
  71.8 1.3 %collective-permute-start.19 = (bf16[128,512]{1,0:T(8,128)(2,1)S(1)}, bf16[128,512]{1,0:T(8,128)(2,1)S(1)}, u32[]{:S(2)}, u32[]{:S(2)}) collective-permute-start(bf16[128,512]{1,0:T(8,128)(2,1)S(1)} %collective-permute-done.15.refs_1_), channel_id=1, source_target_pairs={{0,4},{4,0},{8,12},{12,8},{16,20},{20,16},{24,28},{28,24},{1,5},{5... | collective-permute-start | bytes 393224 | tf_op jit(solution)/shard_map/ppermute | solution.py:128
  75.4 2.5 %collective-permute-start.22 = (bf16[3,128,512]{2,1,0:T(8,128)(2,1)S(1)}, bf16[3,128,512]{2,1,0:T(8,128)(2,1)S(1)}, u32[]{:S(2)}, u32[]{:S(2)}) collective-permute-start(bf16[3,128,512]{2,1,0:T(8,128)(2,1)S(1)} %get-tuple-element.26), channel_id=1, source_target_pairs={{0,4},{4,0},{8,12},{12,8},{16,20},{20,16},{24,28},{28,24},{1,5},{5... | collective-permute-start | bytes 1179656 | tf_op jit(solution)/shard_map/ppermute | solution.py:128
  78.0 6.4 %collective-permute-start.25 = (bf16[128,512]{1,0:T(8,128)(2,1)S(1)}, bf16[128,512]{1,0:T(8,128)(2,1)S(1)}, u32[]{:S(2)}, u32[]{:S(2)}) collective-permute-start(bf16[128,512]{1,0:T(8,128)(2,1)S(1)} %get-tuple-element.30), channel_id=1, source_target_pairs={{0,8},{4,12},{8,0},{12,4},{16,24},{20,28},{24,16},{28,20},{1,9},{5... | collective-permute-start | bytes 393224 | tf_op jit(solution)/shard_map/ppermute | solution.py:128
  79.3 8.1 %collective-permute-start.24 = (bf16[128,512]{1,0:T(8,128)(2,1)S(1)}, bf16[128,512]{1,0:T(8,128)(2,1)S(1)}, u32[]{:S(2)}, u32[]{:S(2)}) collective-permute-start(bf16[128,512]{1,0:T(8,128)(2,1)S(1)} %get-tuple-element.31), channel_id=1, source_target_pairs={{0,16},{4,20},{8,24},{12,28},{16,0},{20,4},{24,8},{28,12},{1,17},{... | collective-permute-start | bytes 393224 | tf_op jit(solution)/shard_map/ppermute | solution.py:128
  80.1 7.3 %collective-permute-start.23 = (bf16[128,512]{1,0:T(8,128)(2,1)S(1)}, bf16[128,512]{1,0:T(8,128)(2,1)S(1)}, u32[]{:S(2)}, u32[]{:S(2)}) collective-permute-start(bf16[128,512]{1,0:T(8,128)(2,1)S(1)} %get-tuple-element.32), channel_id=1, source_target_pairs={{0,24},{4,28},{8,16},{12,20},{16,8},{20,12},{24,0},{28,4},{1,25},{... | collective-permute-start | bytes 393224 | tf_op jit(solution)/shard_map/ppermute | solution.py:128
  83.4 4.0 %collective-permute-start.26 = (bf16[1,128,512]{2,1,0:T(8,128)(2,1)S(1)}, bf16[1,128,512]{2,1,0:T(8,128)(2,1)S(1)}, u32[]{:S(2)}, u32[]{:S(2)}) collective-permute-start(bf16[1,128,512]{2,1,0:T(8,128)(2,1)S(1)} %get-tuple-element.29), channel_id=1, source_target_pairs={{0,4},{4,0},{8,12},{12,8},{16,20},{20,16},{24,28},{28,24},{1,5},{5... | collective-permute-start | bytes 393224 | tf_op jit(solution)/shard_map/ppermute | solution.py:128
  87.5 5.0 %collective-permute-start.27 = (bf16[128,512]{1,0:T(8,128)(2,1)S(1)}, bf16[128,512]{1,0:T(8,128)(2,1)S(1)}, u32[]{:S(2)}, u32[]{:S(2)}) collective-permute-start(bf16[128,512]{1,0:T(8,128)(2,1)S(1)} %fusion), channel_id=1, source_target_pairs={{0,1},{1,0},{2,3},{3,2},{4,5},{5,4},{6,7},{7,6},{8,9},{9,8},{10,11... | collective-permute-start | bytes 393224 | tf_op jit(solution)/shard_map/ppermute | solution.py:128
  92.6 6.9 %collective-permute-start.28 = (bf16[128,512]{1,0:T(8,128)(2,1)S(1)}, bf16[128,512]{1,0:T(8,128)(2,1)S(1)}, u32[]{:S(2)}, u32[]{:S(2)}) collective-permute-start(bf16[128,512]{1,0:T(8,128)(2,1)S(1)} %add_convert_fusion.2), channel_id=1, source_target_pairs={{0,3},{1,2},{2,1},{3,0},{4,7},{5,6},{6,5},{7,4},{8,11},{9,10},{10,... | collective-permute-start | bytes 393224 | tf_op jit(solution)/shard_map/ppermute | solution.py:128
